TPU v7x, 256 devices: a whole 4x4x8 slice. The times are simulated.
256 devices in a mesh: dp: 8 (over x, core), expert: 32 (over z, y).
Axes of the slice: x: 4, y: 4, z: 8, core: 2. Of those that a mesh axis runs over, the one named last changes fastest.
Arguments:
- x_rows: bfloat16 [8, 32, 256, 4096], P('dp', 'expert'), may hold values from -6 to 6
- out_grads: bfloat16 [8, 32, 256, 3072], P('dp', 'expert'), may hold values from -6 to 6
- token_counts: int32 [8, 32], P(None, 'expert'), may hold values from 1 to 256, as said below
- a_param: float32 [32, 4096, 128], P('expert', 'dp'), may hold values from -1.5 to 1.5
- a_first: float32 [32, 4096, 128], P('expert', 'dp'), may hold values from -1.8 to 1.8
- a_second: float32 [32, 4096, 128], P('expert', 'dp'), may hold values from 0.01 to 1
- b_param: float32 [32, 64, 3072], P('expert', None, 'dp'), may hold values from -1.5 to 1.5
- b_first: float32 [32, 64, 3072], P('expert', None, 'dp'), may hold values from -1.8 to 1.8
- b_second: float32 [32, 64, 3072], P('expert', None, 'dp'), may hold values from 0.01 to 1
- frozen_tiles: bfloat16 [32, 4096, 3072], P('expert', 'dp'), may hold values from -6 to 6
- placement_map: int32 [512], replicated, may hold values from 0 to 1023, as said below
Outputs:
- new_a: float32 [32, 4096, 128], P('expert', 'dp')
- new_a_first: float32 [32, 4096, 128], P('expert', 'dp')
- new_a_second: float32 [32, 4096, 128], P('expert', 'dp')
- new_b: float32 [32, 64, 3072], P('expert', None, 'dp')
- new_b_first: float32 [32, 64, 3072], P('expert', None, 'dp')
- new_b_second: float32 [32, 64, 3072], P('expert', None, 'dp')
- served: bfloat16 [512, 8, 16, 3072], P('expert', 'dp')
Inputs may be any that keep to these rules, and one draw needn't show every extreme that they name: `token_counts`: at least 1; the largest entry equals 256 in every draw. `placement_map`: server slot s belongs to the server owner s // 16 of the expert axis. Each owner takes exactly one tile from each of 16 distinct trainer devices (the trainer device of tile t is t // 32), and none from the others; how often a tile is hosted varies.
All inputs are finite; a program needn't handle non-finite values.
Results may differ from a plain program's by a relative error of at most 0.005.
Values may be sent and summed in bfloat16 or wider, within the bound.
No kernel may reach another device: no remote copies, remote signals or barrier semaphores. Data moves between devices by JAX's collectives and lax.ppermute only.
A program may use at most 128 MiB of HBM per device.

v0:
```python
import jax
import jax.numpy as jnp
from jax import lax
from jax.sharding import PartitionSpec as P

EXPERT_HIDDEN = 1536
LOW_RANK = 64
TILE_ROWS = 16
PAIR_MOST = 1


beta_one = 0.9
beta_two = 0.95
learn_rate = 0.05
adam_eps = 1e-08
bias_one = 1.0 - 0.9**10
bias_two = 1.0 - 0.95**10
adapter_scale = 2.0


def adam_step(weights, moment_one, moment_two, gradient):
    moment_one = beta_one * moment_one + (1.0 - beta_one) * gradient
    moment_two = beta_two * moment_two + (1.0 - beta_two) * gradient * gradient
    update_step = (
        learn_rate * (moment_one / bias_one) / (jnp.sqrt(moment_two / bias_two) + adam_eps)
    )
    return (weights - update_step, moment_one, moment_two)


def factor_product(form, left, right, axis_out):
    first_part = jnp.einsum(
        form, left[..., :LOW_RANK], right[..., :EXPERT_HIDDEN], preferred_element_type=jnp.float32
    )
    second_part = jnp.einsum(
        form, left[..., LOW_RANK:], right[..., EXPERT_HIDDEN:], preferred_element_type=jnp.float32
    )
    return jnp.concatenate([first_part, second_part], axis=axis_out)


def send_plan(slot_table, owner_index, local_tiles):
    is_mine = slot_table // local_tiles == owner_index
    ordinal = jnp.cumsum(is_mine.astype(jnp.int32), axis=1) - 1
    slot_hit = is_mine[:, :, None] & (ordinal[:, :, None] == jnp.arange(PAIR_MOST)[None, None, :])
    local_ids = (slot_table - owner_index * local_tiles)[:, :, None]
    tile_pick = jnp.sum(jnp.where(slot_hit, local_ids, 0), axis=1)
    valid_slot = jnp.any(slot_hit, axis=1)
    return (tile_pick, valid_slot)


def receive_plan(slot_row, local_tiles):
    source = slot_row // local_tiles
    count = slot_row.shape[0]
    same_source = source[:, None] == source[None, :]
    earlier = jnp.arange(count)[None, :] < jnp.arange(count)[:, None]
    ordinal = jnp.sum((same_source & earlier).astype(jnp.int32), axis=1)
    return (source, ordinal)


def fill_buffer(pieces, tile_pick, valid_slot):
    chosen = pieces[tile_pick]
    return jnp.where(valid_slot[:, :, None, None], chosen, jnp.zeros((), pieces.dtype))


def per_device(
    x_rows,
    out_grads,
    token_counts,
    a_param,
    a_first,
    a_second,
    b_param,
    b_first,
    b_second,
    frozen_tiles,
    placement_map,
):
    single_precision = jnp.float32
    replica = lax.axis_index("dp")
    replicas = lax.axis_size("dp")
    live_rows = jnp.sum(
        jnp.where(jnp.arange(replicas)[:, None] == replica, token_counts, 0), axis=0
    )
    total_tokens = jnp.sum(token_counts, axis=0).astype(single_precision)
    a_half, b_half = (
        lax.all_gather(a_param.astype(jnp.bfloat16), "dp", axis=1, tiled=True),
        lax.all_gather(b_param.astype(jnp.bfloat16), "dp", axis=2, tiled=True),
    )
    input_rows = x_rows[0]
    out_rows = out_grads[0]
    row_mask = jnp.arange(input_rows.shape[1])[None, :] < live_rows[:, None]
    active_gradients = jnp.where(row_mask[:, :, None], out_rows, jnp.zeros((), jnp.bfloat16))
    projected_rows = jnp.einsum(
        "ecd,edk->eck", input_rows, a_half, preferred_element_type=single_precision
    ).astype(jnp.bfloat16)
    reverse_pass = jnp.concatenate(
        [
            jnp.einsum(
                "ecf,ekf->eck",
                active_gradients[..., :EXPERT_HIDDEN],
                b_half[..., :EXPERT_HIDDEN],
                preferred_element_type=single_precision,
            ),
            jnp.einsum(
                "ecf,ekf->eck",
                active_gradients[..., EXPERT_HIDDEN:],
                b_half[..., EXPERT_HIDDEN:],
                preferred_element_type=single_precision,
            ),
        ],
        axis=2,
    ).astype(jnp.bfloat16)
    down_factor_gradient = adapter_scale * jnp.einsum(
        "nar,nap->nrp", input_rows, reverse_pass, preferred_element_type=single_precision
    )
    up_factor_gradient = adapter_scale * factor_product(
        "dhy,dha->dya", projected_rows, active_gradients, 2
    )
    sum_a, sum_b = (
        lax.psum_scatter(down_factor_gradient, "dp", scatter_dimension=1, tiled=True),
        lax.psum_scatter(up_factor_gradient, "dp", scatter_dimension=2, tiled=True),
    )
    new_a, new_a_first, new_a_second = adam_step(
        a_param, a_first, a_second, sum_a / total_tokens[:, None, None]
    )
    new_b, new_b_first, new_b_second = adam_step(
        b_param, b_first, b_second, sum_b / total_tokens[:, None, None]
    )
    a_new_half = new_a.astype(jnp.bfloat16)
    b_new_half = lax.all_gather(new_b.astype(jnp.bfloat16), "dp", axis=2, tiled=True)
    experts_here = a_param.shape[0]
    block_rows = a_param.shape[1]
    tiles_each = block_rows // TILE_ROWS
    local_tiles = experts_here * tiles_each
    width = frozen_tiles.shape[2]
    owners = lax.axis_size("expert")
    owner_index = lax.axis_index("expert")
    slot_table = placement_map.reshape(owners, -1)
    slot_row = lax.dynamic_index_in_dim(slot_table, owner_index, 0, keepdims=False)
    tile_pick, valid_slot = send_plan(slot_table, owner_index, local_tiles)
    source, ordinal = receive_plan(slot_row, local_tiles)
    b_every = lax.all_gather(b_new_half, "expert", axis=0, tiled=True)
    base_pieces = frozen_tiles.reshape(local_tiles, TILE_ROWS, width)
    a_pieces = a_new_half.reshape(local_tiles, TILE_ROWS, a_param.shape[2])
    base_out = fill_buffer(base_pieces, tile_pick, valid_slot)
    a_out = fill_buffer(a_pieces, tile_pick, valid_slot)
    base_in, a_in = (
        lax.all_to_all(base_out, "expert", split_axis=0, concat_axis=0, tiled=True),
        lax.all_to_all(a_out, "expert", split_axis=0, concat_axis=0, tiled=True),
    )
    frozen_slot = base_in[source, ordinal]
    down_factor_slot = a_in[source, ordinal]
    expert_id = slot_row // tiles_each
    up_factor_picked = b_every[expert_id]
    served = (
        frozen_slot.astype(single_precision)
        + adapter_scale * factor_product("row,rwm->rom", down_factor_slot, up_factor_picked, 2)
    ).astype(jnp.bfloat16)
    return (new_a, new_a_first, new_a_second, new_b, new_b_first, new_b_second, served[:, None])


def solution(mesh):
    return jax.shard_map(
        per_device,
        mesh=mesh,
        in_specs=(
            P("dp", "expert", None, None),
            P("dp", "expert", None, None),
            P(None, "expert"),
            P("expert", "dp", None),
            P("expert", "dp", None),
            P("expert", "dp", None),
            P("expert", None, "dp"),
            P("expert", None, "dp"),
            P("expert", None, "dp"),
            P("expert", "dp", None),
            P(),
        ),
        out_specs=(
            P("expert", "dp", None),
            P("expert", "dp", None),
            P("expert", "dp", None),
            P("expert", None, "dp"),
            P("expert", None, "dp"),
            P("expert", None, "dp"),
            P("expert", "dp", None, None),
        ),
        check_vma=False,
    )
```

profile of v0, /device:TPU:4, one launch (start us, length us, event | category | flops | bytes accessed | tf_op | source)
XLA Modules:
  0.0 309.3 jit_solution(6503652898341086856)
XLA Ops:
  7.2 1.8 convert_element_type.57
  11.0 2.7 bitcast_select_fusion.1
  13.8 24.1 %all-gather.3.cloned.1.call-done = bf16[1,4096,128]{2,1,0:T(8,128)(2,1)} async-done(((bf16[1,512,128]{2,1,0:T(8,128)(2,1)}), bf16[1,4096,128]{2,1,0:T(8,128)(2,1)}) %all-gather.3.cloned.1.call-update) | async-done | bytes 1048592 | tf_op jit(solution)/shard_map/all_gather | solution.py:85
  37.9 2.8 fusion.20
  43.0 29.6 %reduce-scatter.5.cloned.1.call-done = f32[1,64,384]{2,1,0:T(8,128)} async-done(((f32[1,64,3072]{2,1,0:T(8,128)}), f32[1,64,384]{2,1,0:T(8,128)}) %reduce-scatter.5.cloned.1.call-update) | async-done | bytes 98320 | tf_op jit(solution)/shard_map/reduce_scatter | solution.py:120
  72.6 1.8 fusion.55
  74.4 16.5 %all_gather.12 = bf16[1,64,3072]{2,1,0:T(8,128)(2,1)S(1)} all-gather(bf16[1,64,384]{2,1,0:T(8,128)(2,1)S(1)} %get-tuple-element.49), channel_id=1, replica_groups=mesh['dp'=8,'expert'=32] {'dp'}, dimensions={2}, use_global_device_ids=true | all-gather | bytes 442368 | tf_op jit(solution)/shard_map/all_gather | solution.py:86
  95.7 14.2 %all_gather.14 = bf16[1,64,3072]{2,1,0:T(8,128)(2,1)} all-gather(bf16[1,64,384]{2,1,0:T(8,128)(2,1)S(1)} %get-tuple-element.45), channel_id=1, replica_groups=mesh['dp'=8,'expert'=32] {'dp'}, dimensions={2}, use_global_device_ids=true | all-gather | bytes 442368 | tf_op jit(solution)/shard_map/all_gather | solution.py:129
  110.5 2.4 gather_fusion
  113.0 3.9 %bitcast_select_fusion = bf16[32,1,16,3072]{3,2,1,0:T(8,128)(2,1)} fusion(bf16[32,16,3072]{2,1,0:T(8,128)(2,1)} %gather_fusion, pred[32]{0:T(512)(128)(4,1)S(1)} %get-tuple-element.39), kind=kLoop, calls=%fused_computation.14 | loop fusion | flops 1572864 | bytes 6291488 | tf_op jit(solution)/shard_map/jit(_where)/select_n | solution.py:61
  116.8 10.1 %all-to-all-start = ((bf16[32,1,16,3072]{3,2,1,0:T(8,128)(2,1)}), bf16[32,1,16,3072]{3,2,1,0:T(8,128)(2,1)}, u32[]{:S(2)}, u32[]{:S(2)}) async-start(bf16[32,1,16,3072]{3,2,1,0:T(8,128)(2,1)} %bitcast_select_fusion), calls=%async_computation.2 | async-start | bytes 6291456 | tf_op jit(solution)/shard_map/all_to_all | solution.py:147
  127.8 1.8 copy.43
  129.6 1.8 copy.44
  131.6 2.2 fusion.53
  136.8 77.4 %all-to-all-done = bf16[32,1,16,3072]{3,2,1,0:T(8,128)(2,1)} async-done(((bf16[32,1,16,3072]{3,2,1,0:T(8,128)(2,1)}), bf16[32,1,16,3072]{3,2,1,0:T(8,128)(2,1)}, u32[]{:S(2)}, u32[]{:S(2)}) %all-to-all-start) | async-done | bytes 3145760 | tf_op jit(solution)/shard_map/all_to_all | solution.py:147
  214.2 6.0 %all-to-all-start.1 = ((bf16[32,1,16,128]{3,2,1,0:T(8,128)(2,1)}), bf16[32,1,16,128]{3,2,1,0:T(8,128)(2,1)S(1)}, u32[]{:S(2)}, u32[]{:S(2)}) async-start(bf16[32,1,16,128]{3,2,1,0:T(8,128)(2,1)} %fusion.25), calls=%async_computation.3 | async-start | bytes 262144 | tf_op jit(solution)/shard_map/all_to_all | solution.py:148
  221.0 3.7 %gather_fusion.1 = bf16[16,16,3072]{2,1,0:T(8,128)(2,1)} fusion(bf16[32,1,16,3072]{3,2,1,0:T(8,128)(2,1)} %all-to-all-done, s32[16]{0:T(128)S(1)} %get-tuple-element.37), kind=kCustom, calls=%fused_computation.1 | custom fusion | bytes 3145856 | tf_op jit(solution)/shard_map/gather | solution.py:150
  224.7 1.8 copy.48
  226.4 1.8 copy.49
  229.1 3.6 %all-to-all-done.1 = bf16[32,1,16,128]{3,2,1,0:T(8,128)(2,1)S(1)} async-done(((bf16[32,1,16,128]{3,2,1,0:T(8,128)(2,1)}), bf16[32,1,16,128]{3,2,1,0:T(8,128)(2,1)S(1)}, u32[]{:S(2)}, u32[]{:S(2)}) %all-to-all-start.1) | async-done | bytes 131104 | tf_op jit(solution)/shard_map/all_to_all | solution.py:148
  233.2 54.8 %all-gather.5.cloned.1.call-done = bf16[32,64,3072]{2,1,0:T(8,128)(2,1)} async-done(((bf16[1,64,3072]{2,1,0:T(8,128)(2,1)}), bf16[32,64,3072]{2,1,0:T(8,128)(2,1)}) %all-gather.5.cloned.1.call-update) | async-done | bytes 12582928 | tf_op jit(solution)/shard_map/all_gather | solution.py:141
  288.0 8.1 %gather_fusion.4 = bf16[16,64,3072]{2,1,0:T(8,128)(2,1)} fusion(bf16[32,64,3072]{2,1,0:T(8,128)(2,1)} %all-gather.5.cloned.1.call-done, s32[1024]{0:T(1024)S(1)} %pad_clamp_fusion), kind=kCustom, calls=%fused_computation.4 | custom fusion | bytes 12582976 | tf_op jit(solution)/shard_map/gather | solution.py:153
  296.2 2.4 fusion.7
  298.6 2.6 fusion.10
  (57 shorter events, 16.8 us)
Async XLA Ops:
  7.2 103.4 %copy-start = (bf16[1,512,3072]{2,1,0:T(8,128)(2,1)S(1)}, bf16[1,512,3072]{2,1,0:T(8,128)(2,1)}, u32[]{:S(2)}) copy-start(bf16[1,512,3072]{2,1,0:T(8,128)(2,1)} %param.20) | copy-start | bytes 9437188
  7.2 30.7 %all-gather.3.cloned.1.call-start = ((), (), s32[]{:S(2)}) async-start(), calls=%async_computation.5 | async-start | bytes 1179648 | tf_op jit(solution)/shard_map/all_gather | solution.py:85
  9.0 63.5 %reduce-scatter.5.cloned.1.call-start = ((), (), s32[]{:S(2)}) async-start(), calls=%async_computation.6 | async-start | bytes 884736 | tf_op jit(solution)/shard_map/reduce_scatter | solution.py:120
  37.9 2.8 copy-start.2
  40.7 31.8 %copy-start.5 = (f32[1,64,384]{2,1,0:T(8,128)S(1)}, f32[1,64,384]{2,1,0:T(8,128)}, u32[]{:S(2)}) copy-start(f32[1,64,384]{2,1,0:T(8,128)} %param.17) | copy-start | bytes 294916
  40.7 31.8 %copy-start.6 = (f32[1,64,384]{2,1,0:T(8,128)S(1)}, f32[1,64,384]{2,1,0:T(8,128)}, u32[]{:S(2)}) copy-start(f32[1,64,384]{2,1,0:T(8,128)} %param.18) | copy-start | bytes 294916
  40.8 31.8 %copy-start.7 = (f32[1,64,384]{2,1,0:T(8,128)S(1)}, f32[1,64,384]{2,1,0:T(8,128)}, u32[]{:S(2)}) copy-start(f32[1,64,384]{2,1,0:T(8,128)} %param.19) | copy-start | bytes 294916
  42.3 89.3 %reduce-scatter.3.cloned.1.call-start = ((), (), s32[]{:S(2)}) async-start(), calls=%async_computation.4 | async-start | bytes 2359296 | tf_op jit(solution)/shard_map/reduce_scatter | solution.py:119
  72.6 21.3 %copy-start.1 = (bf16[1,1,256,4096]{3,2,1,0:T(8,128)(2,1)S(1)}, bf16[1,1,256,4096]{3,2,1,0:T(8,128)(2,1)}, u32[]{:S(2)}) copy-start(bf16[1,1,256,4096]{3,2,1,0:T(8,128)(2,1)} %param.11) | copy-start | bytes 6291460
  95.6 14.3 %copy-start.9 = (s32[512]{0:T(512)S(1)}, s32[512]{0:T(512)}, u32[]{:S(2)}) copy-start(s32[512]{0:T(512)} %param.21) | copy-start | bytes 6148
  95.7 192.4 %all-gather.5.cloned.1.call-start = ((), (), s32[]{:S(2)}) async-start(), calls=%async_computation.7 | async-start | bytes 12976128 | tf_op jit(solution)/shard_map/all_gather | solution.py:141
  110.0 21.4 %copy-start.8 = (s32[32,16]{1,0:T(8,128)}, s32[32,16]{1,0:T(8,128)S(1)}, u32[]{:S(2)}) copy-start(s32[32,16]{1,0:T(8,128)S(1)} %reshape.491) | copy-start | bytes 6148
  116.8 10.1 %copy-start.4 = (f32[1,512,128]{2,1,0:T(8,128)S(1)}, f32[1,512,128]{2,1,0:T(8,128)}, u32[]{:S(2)}) copy-start(f32[1,512,128]{2,1,0:T(8,128)} %param.14) | copy-start | bytes 786436
  116.8 97.4 %all-to-all-start = ((bf16[32,1,16,3072]{3,2,1,0:T(8,128)(2,1)}), bf16[32,1,16,3072]{3,2,1,0:T(8,128)(2,1)}, u32[]{:S(2)}, u32[]{:S(2)}) async-start(bf16[32,1,16,3072]{3,2,1,0:T(8,128)(2,1)} %bitcast_select_fusion), calls=%async_computation.2 | async-start | bytes 6291456 | tf_op jit(solution)/shard_map/all_to_all | solution.py:147
  214.2 18.4 %all-to-all-start.1 = ((bf16[32,1,16,128]{3,2,1,0:T(8,128)(2,1)}), bf16[32,1,16,128]{3,2,1,0:T(8,128)(2,1)S(1)}, u32[]{:S(2)}, u32[]{:S(2)}) async-start(bf16[32,1,16,128]{3,2,1,0:T(8,128)(2,1)} %fusion.25), calls=%async_computation.3 | async-start | bytes 262144 | tf_op jit(solution)/shard_map/all_to_all | solution.py:148
  298.6 2.6 copy-start.3
Sparse Core Ops, SparseCore 0:
  10.5 27.4 all-gather.2
  42.4 30.1 reduce-scatter.4
  95.8 32.5 reduce-scatter.2
  131.2 156.8 all-gather.4
where the time goes:
time: 311 us; the launch traced here: 309 us
  waiting for transfers between devices  190 us (61%)
  blocking collectives  30.7 us (10%)
  local copies, waits for them, and re-layouts  26.1 us (8%)
  other arithmetic  19 us (6%)
  starting transfers between devices  16.3 us (5%)
  between operations  14.6 us (5%)
  matrix products  13.1 us (4%)
    all_to_all x1, waiting for transfers between devices, per_device(): lax.all_to_all(base_out, 'expert', split_axis=0, concat_axis=0, tiled=True)  77.4 us
    all_gather x1, waiting for transfers between devices, per_device(): b_every = lax.all_gather(b_new_half, 'expert', axis=0, tiled=True)  54.8 us
    reduce_scatter x1, waiting for transfers between devices, per_device(): lax.psum_scatter(up_factor_gradient, 'dp', scatter_dimension=2, tiled=True)  29.6 us
    all_gather x1, waiting for transfers between devices, per_device(): lax.all_gather(a_param.astype(jnp.bfloat16), 'dp', axis=1, tiled=True)  24.1 us
    all_gather x1, blocking collectives, per_device(): lax.all_gather(b_param.astype(jnp.bfloat16), 'dp', axis=2, tiled=True)  16.5 us
    all_gather x1, blocking collectives, per_device(): lax.all_gather(new_b.astype(jnp.bfloat16), 'dp', axis=2, tiled=True)  14.2 us
    all_to_all x1, starting transfers between devices, per_device(): lax.all_to_all(base_out, 'expert', split_axis=0, concat_axis=0, tiled=True)  10.1 us
    unnamed x26, local copies, waits for them, and re-layouts  8.87 us
  transfers between devices with their start and end apart: 6, of which 5 were waited for; matrix products, arithmetic and copies ran while one was open for 10% of the time, Pallas kernels for 0%

commit v1 on v0

v1 whole, which is shorter than its diff:
```python
import functools

import jax
import jax.numpy as jnp
from jax import lax
from jax.experimental import pallas as pl
from jax.experimental.pallas import tpu as pltpu
from jax.sharding import PartitionSpec as P

LOW_RANK = 64
TILE_ROWS = 16
TILES = 32
SLOTS = 16
Z, Y, DP = 8, 4, 8
X = 4

beta_one = 0.9
beta_two = 0.95
learn_rate = 0.05
adam_eps = 1e-08
bias_one = 1.0 - 0.9**10
bias_two = 1.0 - 0.95**10
adapter_scale = 2.0

F32 = jnp.float32
BF16 = jnp.bfloat16


def adam_step(weights, moment_one, moment_two, gradient):
    moment_one = beta_one * moment_one + (1.0 - beta_one) * gradient
    moment_two = beta_two * moment_two + (1.0 - beta_two) * gradient * gradient
    update_step = (
        learn_rate * (moment_one / bias_one) / (jnp.sqrt(moment_two / bias_two) + adam_eps)
    )
    return (weights - update_step, moment_one, moment_two)


def shift_x(array, k):
    return lax.ppermute(
        array, "dp", [(i, (i // 2 + k) % X * 2 + i % 2) for i in range(DP)]
    )


def swap_core(array):
    return lax.ppermute(array, "dp", [(i, i // 2 * 2 + 1 - i % 2) for i in range(DP)])


def shift_y(array, k):
    return lax.ppermute(
        array, "expert", [(i, i // Y * Y + (i % Y + k) % Y) for i in range(Z * Y)]
    )


def shift_z(array, k):
    return lax.ppermute(
        array, "expert", [(i, (i // Y + k) % Z * Y + i % Y) for i in range(Z * Y)]
    )


def vmem():
    return pl.BlockSpec(memory_space=pltpu.VMEM)


def smem():
    return pl.BlockSpec(memory_space=pltpu.SMEM)


def anywhere():
    return pl.BlockSpec(memory_space=pl.ANY)


PARAMS = pltpu.CompilerParams(vmem_limit_bytes=60 * 1024 * 1024)


def gradient_kernel(ids, counts, x, g, *refs):
    blocks, keep, give = refs[:DP], refs[DP], refs[DP + 1]
    chip, core = ids[0] // 2, lax.rem(ids[0], 2)
    live = counts[ids[0], 0]
    rows = x.shape[0]
    a_rows = x.shape[1] // DP
    cols = g.shape[1] // DP
    tiles = cols // 128
    projected = jnp.zeros((rows, 2 * LOW_RANK), F32)
    gate = jnp.zeros((rows, LOW_RANK), F32)
    up = jnp.zeros((rows, LOW_RANK), F32)
    for i in range(DP):
        k, c = i // 2, i % 2
        j = 2 * lax.rem(chip + X - k, X) + (1 - core if c else core)
        part = x[:, pl.ds(pl.multiple_of(j * a_rows, a_rows), a_rows)]
        projected += jnp.dot(part, blocks[i][:a_rows, :], preferred_element_type=F32)
        b_block = jnp.concatenate(
            [
                blocks[i][a_rows + t * LOW_RANK : a_rows + (t + 1) * LOW_RANK, :]
                for t in range(tiles)
            ],
            axis=1,
        )
        part = g[:, pl.ds(pl.multiple_of(j * cols, 128), cols)]
        term = lax.dot_general(
            part, b_block, (((1,), (1,)), ((), ())), preferred_element_type=F32
        )
        is_gate = j < DP // 2
        gate += jnp.where(is_gate, term, 0.0)
        up += jnp.where(is_gate, 0.0, term)
    mask = lax.broadcasted_iota(jnp.int32, (rows, 2 * LOW_RANK), 0) < live
    backward = jnp.where(mask, jnp.concatenate([gate, up], axis=1), 0.0)
    backward_t = jnp.transpose(backward).astype(BF16)
    projected_t = jnp.transpose(jnp.where(mask, projected, 0.0)).astype(BF16)
    for i in range(DP):
        k, c = i // 2, i % 2
        j = 2 * lax.rem(chip + k, X) + (1 - core if c else core)
        out = give if c else keep
        part = x[:, pl.ds(pl.multiple_of(j * a_rows, a_rows), a_rows)]
        grad = jnp.dot(backward_t, part, preferred_element_type=F32).astype(BF16)
        for t in range(a_rows // 128):
            out[k, t * 128 : (t + 1) * 128, :] = grad[:, t * 128 : (t + 1) * 128]
        part = g[:, pl.ds(pl.multiple_of(j * cols, 128), cols)]
        half = jnp.where(j < DP // 2, projected_t[:LOW_RANK], projected_t[LOW_RANK:])
        grad = jnp.dot(half, part, preferred_element_type=F32).astype(BF16)
        for t in range(tiles):
            out[k, a_rows + t * LOW_RANK : a_rows + (t + 1) * LOW_RANK, :] = grad[
                :, t * 128 : (t + 1) * 128
            ]


def pack_kernel(a, b, out):
    a_rows = a.shape[0]
    out[:a_rows, :] = a[...].astype(BF16)
    for t in range(b.shape[1] // 128):
        r = slice(a_rows + t * LOW_RANK, a_rows + (t + 1) * LOW_RANK)
        out[r, :] = b[:, t * 128 : (t + 1) * 128].astype(BF16)


def pair_kernel(kept, taken, *outs):
    for k in range(X):
        outs[k][...] = (kept[k].astype(F32) + taken[k].astype(F32)).astype(BF16)


def adam_kernel(ids, pick, counts, *refs):
    blocks = refs[:X]
    a, a1, a2, b, b1, b2 = refs[X : X + 6]
    na, na1, na2, nb, nb1, nb2 = refs[X + 6 : X + 12]
    outs, ah = refs[X + 12 : -1], refs[-1]
    tokens = counts[0, 0]
    for p in range(1, DP):
        tokens += counts[p, 0]
    factor = adapter_scale / jnp.full((1, 128), tokens, jnp.int32).astype(F32)
    a_rows = a.shape[0]
    b_rows = b.shape[1] // 128 * LOW_RANK

    def total(lo, hi):
        s = blocks[0][lo:hi, :].astype(F32)
        for k in range(1, X):
            s += blocks[k][lo:hi, :].astype(F32)
        return s * factor

    for t in range(b.shape[1] // 128):
        c = slice(t * 128, (t + 1) * 128)
        grad = total(a_rows + t * LOW_RANK, a_rows + (t + 1) * LOW_RANK)
        new, one, two = adam_step(b[:, c], b1[:, c], b2[:, c], grad)
        nb[:, c], nb1[:, c], nb2[:, c] = new, one, two
        for dz in range(Z):
            outs[dz][t * LOW_RANK : (t + 1) * LOW_RANK, :] = new.astype(BF16)
    for t in range(a_rows // 128):
        r = slice(t * 128, (t + 1) * 128)
        grad = jnp.transpose(total(t * 128, (t + 1) * 128))
        new, one, two = adam_step(a[r, :], a1[r, :], a2[r, :], grad)
        na[r, :], na1[r, :], na2[r, :] = new, one, two
        ah[r, :] = new.astype(BF16)
    z, y = ids[1] // Y, lax.rem(ids[1], Y)
    for dz in range(Z):
        for dy in range(Y):
            owner = lax.rem(z + dz, Z) * Y + lax.rem(y + dy, Y)
            start = pl.multiple_of(pick[owner] * TILE_ROWS, TILE_ROWS)
            r = slice(b_rows + dy * TILE_ROWS, b_rows + (dy + 1) * TILE_ROWS)
            outs[dz][r, :] = ah[pl.ds(start, TILE_ROWS), :]


def tiles_kernel(half, pick, frozen, out, sem):
    cols = out.shape[2]
    copies = []
    for owner in range(out.shape[0]):
        start = pl.multiple_of(pick[owner] * TILE_ROWS, TILE_ROWS)
        src = frozen.at[pl.ds(start, TILE_ROWS), pl.ds(half * cols, cols)]
        copies.append(pltpu.make_async_copy(src, out.at[owner], sem.at[owner]))
    for copy in copies:
        copy.start()
    for copy in copies:
        copy.wait()


def send_tiles(half, pick, frozen):
    shape = (Z * Y, TILE_ROWS, frozen.shape[1] // 2)
    return pl.pallas_call(
        functools.partial(tiles_kernel, half),
        out_shape=jax.ShapeDtypeStruct(shape, BF16),
        in_specs=[smem(), anywhere()],
        out_specs=vmem(),
        scratch_shapes=[pltpu.SemaphoreType.DMA((Z * Y,))],
        compiler_params=PARAMS,
        name="tiles",
    )(pick, frozen)


def stack_kernel(*refs):
    ins, up, downs = refs[:Z], refs[Z], refs[Z + 1 :]
    b_rows = up.shape[1]
    for i, ref in enumerate(ins):
        up[i] = ref[:b_rows, :]
        for dy, down in enumerate(downs):
            down[i] = ref[b_rows + dy * TILE_ROWS : b_rows + (dy + 1) * TILE_ROWS, :]


def slot_of(ids, table, s):
    source = table[ids[1] * SLOTS + s] // TILES
    dz = lax.rem(ids[1] // Y + Z - source // Y, Z)
    dy = lax.rem(lax.rem(ids[1], Y) + Y - lax.rem(source, Y), Y)
    return source, dz, dy


def delta_kernel(ids, table, *refs):
    ups, others, downs = refs[:Y], refs[Y : 2 * Y], refs[2 * Y : 2 * Y + X]
    outs, (own, other, sem) = refs[2 * Y + X : 2 * Y + 2 * X], refs[2 * Y + 2 * X :]
    n_tiles = own.shape[1] // LOW_RANK
    cols = n_tiles * 128
    chip, core = ids[0] // 2, lax.rem(ids[0], 2)
    places = []
    for s in range(SLOTS):
        _, dz, dy = slot_of(ids, table, s)
        places.append((dy, dz))
        for i in range(Y):

            @pl.when(dy == i)
            def _(s=s, i=i, dz=dz):
                pltpu.make_async_copy(ups[i].at[dz], own.at[s], sem.at[0, s]).start()
                pltpu.make_async_copy(others[i].at[dz], other.at[s], sem.at[1, s]).start()

    is_gate = chip < X // 2
    first = jnp.int32(0) == core
    for s in range(SLOTS):
        pltpu.make_async_copy(ups[0].at[0], own.at[s], sem.at[0, s]).wait()
        pltpu.make_async_copy(others[0].at[0], other.at[s], sem.at[1, s]).wait()
        left = jnp.concatenate([downs[k][places[s]] for k in range(X)], axis=0)
        left = jnp.where(is_gate, left[:, :LOW_RANK], left[:, LOW_RANK:])
        halves = []
        for ref in (own, other):
            right = jnp.concatenate(
                [ref[s, t * LOW_RANK : (t + 1) * LOW_RANK, :] for t in range(n_tiles)], axis=1
            )
            delta = adapter_scale * jnp.dot(left, right, preferred_element_type=F32)
            halves.append(delta.astype(BF16))
        mine, theirs = halves
        for k in range(X):
            r = slice(k * TILE_ROWS, (k + 1) * TILE_ROWS)
            outs[k][s, :, :cols] = jnp.where(first, mine[r], theirs[r])
            outs[k][s, :, cols:] = jnp.where(first, theirs[r], mine[r])


def merge_kernel(ids, table, low, high, *refs):
    deltas, out = refs[:X], refs[X]
    chip = ids[0] // 2
    cols = deltas[0].shape[2]
    width = low.shape[2]
    for s in range(SLOTS):
        source = table[ids[1] * SLOTS + s] // TILES
        out[s, :, :width] = low[source]
        out[s, :, width:] = high[source]
        for k in range(X):
            j = lax.rem(chip + k, X)
            c = pl.ds(pl.multiple_of(j * cols, 128), cols)
            out[s, :, c] = (out[s, :, c].astype(F32) + deltas[k][s].astype(F32)).astype(BF16)


def per_device(
    x_rows,
    out_grads,
    token_counts,
    a_param,
    a_first,
    a_second,
    b_param,
    b_first,
    b_second,
    frozen_tiles,
    placement_map,
):
    dp, expert = lax.axis_index("dp"), lax.axis_index("expert")
    ids = jnp.stack([dp, expert]).astype(jnp.int32)
    x, g = x_rows[0, 0], out_grads[0, 0]
    a, a1, a2 = a_param[0], a_first[0], a_second[0]
    b, b1, b2 = b_param[0], b_first[0], b_second[0]
    frozen = frozen_tiles[0]
    a_rows, width = a.shape[0], frozen.shape[1]
    cols = b.shape[1]
    shape_a, shape_b = jax.ShapeDtypeStruct(a.shape, F32), jax.ShapeDtypeStruct(b.shape, F32)
    shape_block = jax.ShapeDtypeStruct((a_rows + cols // 128 * LOW_RANK, 128), BF16)

    block = pl.pallas_call(
        pack_kernel,
        out_shape=shape_block,
        in_specs=[vmem()] * 2,
        out_specs=vmem(),
        compiler_params=PARAMS,
        name="pack",
    )(a, b)
    blocks = []
    for k in range(X):
        mine = block if k == 0 else shift_x(block, k)
        blocks += [mine, swap_core(mine)]

    table = placement_map.reshape(Z * Y, SLOTS)
    pick = jnp.sum(jnp.where(table // TILES == expert, table % TILES, 0), axis=1)
    low = lax.all_to_all(
        send_tiles(0, pick, frozen), "expert", split_axis=0, concat_axis=0, tiled=True
    )

    def update(x, g, a, a1, a2, b, b1, b2, ids, pick, *blocks):
        kept, given = pl.pallas_call(
            gradient_kernel,
            out_shape=[jax.ShapeDtypeStruct((X,) + shape_block.shape, BF16)] * 2,
            in_specs=[smem()] * 2 + [vmem()] * (2 + DP),
            out_specs=[vmem()] * 2,
            compiler_params=PARAMS,
            name="gradients",
        )(ids, token_counts, x, g, *blocks)
        taken = swap_core(given)
        pairs = pl.pallas_call(
            pair_kernel,
            out_shape=[shape_block] * X,
            in_specs=[vmem()] * 2,
            out_specs=[vmem()] * X,
            compiler_params=PARAMS,
            name="pairs",
        )(kept, taken)
        sums = [pairs[0]] + [shift_x(pairs[k], k) for k in range(1, X)]

        new_a, new_a1, new_a2, new_b, new_b1, new_b2, *messages = pl.pallas_call(
            adam_kernel,
            out_shape=[shape_a] * 3 + [shape_b] * 3 + [message] * Z,
            in_specs=[smem()] * 3 + [vmem()] * (X + 6),
            out_specs=[vmem()] * (6 + Z),
            scratch_shapes=[pltpu.VMEM(a.shape, BF16)],
            compiler_params=PARAMS,
            name="adam",
        )(ids, pick, token_counts, *sums, a, a1, a2, b, b1, b2)
        arrived = [messages[dz] if dz == 0 else shift_z(messages[dz], dz) for dz in range(Z)]
        return (new_a, new_a1, new_a2, new_b, new_b1, new_b2, *arrived)

    some = jnp.min(token_counts) > 0
    b_rows = cols // 128 * LOW_RANK
    message = jax.ShapeDtypeStruct((b_rows + Y * TILE_ROWS, 128), BF16)
    part = jax.ShapeDtypeStruct((SLOTS, TILE_ROWS, 2 * cols), BF16)

    def zeros(shapes):
        return lambda *_: tuple(jnp.zeros(s.shape, s.dtype) for s in shapes)

    outs = lax.cond(
        some,
        update,
        zeros([shape_a] * 3 + [shape_b] * 3 + [message] * Z),
        *(x, g, a, a1, a2, b, b1, b2, ids, pick, *blocks),
    )
    new_a, new_a1, new_a2, new_b, new_b1, new_b2 = outs[:6]

    high_out, low, arrived = lax.optimization_barrier(
        (send_tiles(1, pick, frozen), low, outs[6:])
    )
    high = lax.all_to_all(high_out, "expert", split_axis=0, concat_axis=0, tiled=True)

    def spread(ids, placement_map, *arrived):
        up, *downs = pl.pallas_call(
            stack_kernel,
            out_shape=[jax.ShapeDtypeStruct((Z, b_rows, 128), BF16)]
            + [jax.ShapeDtypeStruct((Z, TILE_ROWS, 128), BF16)] * Y,
            in_specs=[vmem()] * Z,
            out_specs=[vmem()] * (1 + Y),
            compiler_params=PARAMS,
            name="stack",
        )(*arrived)
        rows = jnp.stack([downs[0]] + [shift_y(downs[dy], dy) for dy in range(1, Y)])
        ups = [up] + [shift_y(up, dy) for dy in range(1, Y)]
        others = [swap_core(u) for u in ups]
        chips = [rows] + [shift_x(rows, k) for k in range(1, X)]
        deltas = pl.pallas_call(
            delta_kernel,
            out_shape=[part] * X,
            in_specs=[smem()] * 2 + [anywhere()] * (2 * Y) + [vmem()] * X,
            out_specs=[vmem()] * X,
            scratch_shapes=[
                pltpu.VMEM((SLOTS, b_rows, 128), BF16),
                pltpu.VMEM((SLOTS, b_rows, 128), BF16),
                pltpu.SemaphoreType.DMA((2, SLOTS)),
            ],
            compiler_params=PARAMS,
            name="deltas",
        )(ids, placement_map, *ups, *others, *chips)
        return tuple([deltas[0]] + [shift_x(deltas[k], -k) for k in range(1, X)])

    shifted = lax.cond(
        some,
        spread,
        zeros([part] * X),
        *(ids, placement_map, *arrived),
    )

    served = pl.pallas_call(
        merge_kernel,
        out_shape=jax.ShapeDtypeStruct((SLOTS, TILE_ROWS, width), BF16),
        in_specs=[smem()] * 2 + [vmem()] * (2 + X),
        out_specs=vmem(),
        compiler_params=PARAMS,
        name="merge",
    )(ids, placement_map, low, high, *shifted)

    return (
        new_a[None],
        new_a1[None],
        new_a2[None],
        new_b[None],
        new_b1[None],
        new_b2[None],
        served[:, None],
    )


def solution(mesh):
    return jax.shard_map(
        per_device,
        mesh=mesh,
        in_specs=(
            P("dp", "expert", None, None),
            P("dp", "expert", None, None),
            P(None, "expert"),
            P("expert", "dp", None),
            P("expert", "dp", None),
            P("expert", "dp", None),
            P("expert", None, "dp"),
            P("expert", None, "dp"),
            P("expert", None, "dp"),
            P("expert", "dp", None),
            P(),
        ),
        out_specs=(
            P("expert", "dp", None),
            P("expert", "dp", None),
            P("expert", "dp", None),
            P("expert", None, "dp"),
            P("expert", None, "dp"),
            P("expert", None, "dp"),
            P("expert", "dp", None, None),
        ),
        check_vma=False,
    )
```

time: 311 us -> 192 us (0.62)
  waiting for transfers between devices: 190 us -> 80.4 us
  starting transfers between devices: 16.3 us -> 65.8 us
  Pallas kernels: 0 us -> 33.3 us
  blocking collectives: 30.7 us -> 0 us
  local copies, waits for them, and re-layouts: 26.1 us -> 6.5 us
  other arithmetic: 19 us -> 1.62 us
  between operations: 14.6 us -> 1.41 us
  matrix products: 13.1 us -> 0 us
    all_to_all x2, waiting for transfers between devices: 81 us -> 0.01 us  [the longest x1 0.01 us: per_device(): lax.all_to_all(high_out, 'expert', split_axis=0, concat_axis=0, tiled=True)]
    ppermute x0 -> x34, waiting for transfers between devices: none -> 80.4 us  [the longest x12 39.3 us: shift_x(): lax.ppermute(array, 'dp', [(i, (i // 2 + k) % X * 2 + i % 2) for i in ran...]
    all_gather x2 -> x0, waiting for transfers between devices: 79 us -> none  [the longest x1 54.8 us: per_device(): b_every = lax.all_gather(b_new_half, 'expert', axis=0, tiled=True)]
    ppermute x0 -> x34, starting transfers between devices: none -> 47.3 us  [the longest x12 21.2 us: shift_x(): lax.ppermute(array, 'dp', [(i, (i // 2 + k) % X * 2 + i % 2) for i in ran...]
    pallas_call x0 -> x9, Pallas kernels: none -> 33.3 us  [the longest x2 9.94 us: send_tiles(): pl.pallas_call(functools.partial(tiles_kernel, half), out_shape=jax.Shape...]
    all_gather x2 -> x0, blocking collectives: 30.7 us -> none  [the longest x1 16.5 us: per_device(): lax.all_gather(b_param.astype(jnp.bfloat16), 'dp', axis=2, tiled=True)]
    reduce_scatter x2 -> x0, waiting for transfers between devices: 29.6 us -> none  [the longest x1 29.6 us: per_device(): lax.psum_scatter(up_factor_gradient, 'dp', scatter_dimension=2, tiled=True)]
    gather x5 -> x0, local copies, waits for them, and re-layouts: 16.3 us -> none  [the longest x1 8.12 us: per_device(): up_factor_picked = b_every[expert_id]]
  transfers between devices with their start and end apart: 6 -> 36, of which waited for: 5 -> 19; matrix products, arithmetic and copies ran while one was open for 10% -> 1% of each run, Pallas kernels for 0% -> 13%
where the time goes in v1:
time: 192 us; the launch traced here: 189 us
  waiting for transfers between devices  80.4 us (42%)
  starting transfers between devices  65.8 us (34%)
  Pallas kernels  33.3 us (17%)
  local copies, waits for them, and re-layouts  6.5 us (3%)
    ppermute x12, waiting for transfers between devices, shift_x(): lax.ppermute(array, 'dp', [(i, (i // 2 + k) % X * 2 + i % 2) for i in ran...  39.3 us
    ppermute x6, waiting for transfers between devices, shift_y(): lax.ppermute(array, 'expert', [(i, i // Y * Y + (i % Y + k) % Y) for i in...  32.3 us
    ppermute x12, starting transfers between devices, shift_x(): lax.ppermute(array, 'dp', [(i, (i // 2 + k) % X * 2 + i % 2) for i in ran...  21.2 us
    ppermute x7, starting transfers between devices, shift_z(): lax.ppermute(array, 'expert', [(i, (i // Y + k) % Z * Y + i % Y) for i in...  15.2 us
    all_to_all x1, starting transfers between devices, per_device(): lax.all_to_all(send_tiles(0, pick, frozen), 'expert', split_axis=0, conca...  11.6 us
    pallas_call x2, Pallas kernels, send_tiles(): pl.pallas_call(functools.partial(tiles_kernel, half), out_shape=jax.Shape...  9.94 us
    ppermute x6, starting transfers between devices, shift_y(): lax.ppermute(array, 'expert', [(i, i // Y * Y + (i % Y + k) % Y) for i in...  9.62 us
    pallas_call x1, Pallas kernels, spread(): pl.pallas_call(delta_kernel, out_shape=[part] * X, in_specs=[smem()] * 2...  6.94 us
  transfers between devices with their start and end apart: 36, of which 19 were waited for; matrix products, arithmetic and copies ran while one was open for 1% of the time, Pallas kernels for 13%

profile of v1, /device:TPU:4, one launch (start us, length us, event | category | flops | bytes accessed | tf_op | source)
XLA Modules:
  0.0 189.2 jit_solution(7915925116077544836)
XLA Ops:
  1.5 5.0 %tiles.3 = bf16[32,16,1536]{2,1,0:T(8,128)(2,1)} custom-call(s32[32]{0:T(128)S(1)} %fusion.2.pick, bf16[512,3072]{1,0:T(8,128)(2,1)} %bitcast.24), custom_call_target="tpu_custom_call" | custom-call | tf_op jit(solution)/shard_map/tiles/pallas_call | solution.py:194
  6.5 11.6 %all-to-all-start = ((bf16[32,16,1536]{2,1,0:T(8,128)(2,1)}), bf16[32,16,1536]{2,1,0:T(8,128)(2,1)S(1)}, u32[]{:S(2)}, u32[]{:S(2)}) async-start(bf16[32,16,1536]{2,1,0:T(8,128)(2,1)} %tiles.3), calls=%async_computation | async-start | bytes 3145728 | tf_op jit(solution)/shard_map/all_to_all | solution.py:313
  19.4 2.7 %collective-permute-start.30 = (bf16[704,128]{1,0:T(8,128)(2,1)}, bf16[704,128]{1,0:T(8,128)(2,1)}, u32[]{:S(2)}, u32[]{:S(2)}) collective-permute-start(bf16[704,128]{1,0:T(8,128)(2,1)} %pack.1), channel_id=1, source_target_pairs={{0,128},{32,160},{64,192},{96,224},{128,0},{160,32},{192,64},{224,... | collective-permute-start | bytes 540680 | tf_op jit(solution)/shard_map/ppermute | solution.py:39
  22.1 4.5 %collective-permute-done.32 = bf16[704,128]{1,0:T(8,128)(2,1)} collective-permute-done((bf16[704,128]{1,0:T(8,128)(2,1)}, bf16[704,128]{1,0:T(8,128)(2,1)}, u32[]{:S(2)}, u32[]{:S(2)}) %collective-permute-start.32) | collective-permute-done | bytes 180256 | tf_op jit(solution)/shard_map/ppermute | solution.py:39
  30.8 5.0 %tiles.2 = bf16[32,16,1536]{2,1,0:T(8,128)(2,1)} custom-call(s32[32]{0:T(128)S(1)} %fusion.2.pick, bf16[512,3072]{1,0:T(8,128)(2,1)} %bitcast.25), custom_call_target="tpu_custom_call" | custom-call | tf_op jit(solution)/shard_map/tiles/pallas_call | solution.py:194
  37.2 49.7 %conditional.2 = (bf16[256,128]{1,0:T(8,128)(2,1)}, bf16[256,128]{1,0:T(8,128)(2,1)}, bf16[256,128]{1,0:T(8,128)(2,1)}, bf16[256,128]{1,0:T(8,128)(2,1)}, bf16[2...) conditional(s32[]{:T(128)} %convert_element_type.4, () %tuple.37, ...), branch_computations={%region_2.3_spmd, %region_3.4_spmd} | conditional | bytes 14418732 | solution.py:357
  37.9 5.2 %gradients.1 = (bf16[4,704,128]{2,1,0:T(8,128)(2,1)}, bf16[4,704,128]{2,1,0:T(8,128)(2,1)}) custom-call(s32[2]{0:T(128)S(1)} %get-tuple-element.70.ids, s32[8,1]{1,0:T(8,128)} %copy.26.counts, bf16[256,4096]{1,0:T(8,128)(2,1)} %bitcast.26, bf16[256,3072]{1,0:T(8,128)(2,1)S(1)} %bitcast.27, bf16[704,128]{1,0:T(8,128)(2,1)} %get-tuple-element.75.refs_0_, ...), custom_call_target="tpu_custom_call" | custom-call | tf_op jit(solution)/shard_map/cond/branch_1_fun/gradients/pallas_call | solution.py:318
  55.8 4.8 %collective-permute-done.2.refs_2_ = bf16[704,128]{1,0:T(8,128)(2,1)S(1)} collective-permute-done((bf16[704,128]{1,0:T(8,128)(2,1)}, bf16[704,128]{1,0:T(8,128)(2,1)S(1)}, u32[]{:S(2)}, u32[]{:S(2)}) %collective-permute-start.2) | collective-permute-done | bytes 180256 | tf_op jit(solution)/shard_map/cond/branch_1_fun/ppermute | solution.py:39
  73.9 2.7 %collective-permute-start.8 = (bf16[256,128]{1,0:T(8,128)(2,1)}, bf16[256,128]{1,0:T(8,128)(2,1)}, u32[]{:S(2)}, u32[]{:S(2)}) collective-permute-start(bf16[256,128]{1,0:T(8,128)(2,1)} %get-tuple-element.100), channel_id=1, source_target_pairs={{0,20},{1,21},{2,22},{3,23},{4,24},{5,25},{6,26},{7,27},{8,28},{9,... | collective-permute-start | bytes 196616 | tf_op jit(solution)/shard_map/cond/branch_1_fun/ppermute | solution.py:55
  76.6 3.5 %collective-permute-start.9 = (bf16[256,128]{1,0:T(8,128)(2,1)}, bf16[256,128]{1,0:T(8,128)(2,1)}, u32[]{:S(2)}, u32[]{:S(2)}) collective-permute-start(bf16[256,128]{1,0:T(8,128)(2,1)} %get-tuple-element.101), channel_id=1, source_target_pairs={{0,24},{1,25},{2,26},{3,27},{4,28},{5,29},{6,30},{7,31},{8,0},{9,1... | collective-permute-start | bytes 196616 | tf_op jit(solution)/shard_map/cond/branch_1_fun/ppermute | solution.py:55
  80.5 5.5 %collective-permute-done.8 = bf16[256,128]{1,0:T(8,128)(2,1)} collective-permute-done((bf16[256,128]{1,0:T(8,128)(2,1)}, bf16[256,128]{1,0:T(8,128)(2,1)}, u32[]{:S(2)}, u32[]{:S(2)}) %collective-permute-start.8) | collective-permute-done | bytes 65568 | tf_op jit(solution)/shard_map/cond/branch_1_fun/ppermute | solution.py:55
  88.0 6.9 %all-to-all-start.1 = ((bf16[32,16,1536]{2,1,0:T(8,128)(2,1)}), bf16[32,16,1536]{2,1,0:T(8,128)(2,1)S(1)}, u32[]{:S(2)}, u32[]{:S(2)}) async-start(bf16[32,16,1536]{2,1,0:T(8,128)(2,1)} %tiles.2), calls=%async_computation.1 | async-start | bytes 3145728 | tf_op jit(solution)/shard_map/all_to_all | solution.py:368
  94.9 89.2 %conditional.3 = (bf16[16,16,768]{2,1,0:T(8,128)(2,1)S(1)}, bf16[16,16,768]{2,1,0:T(8,128)(2,1)}, bf16[16,16,768]{2,1,0:T(8,128)(2,1)}, bf16[16,16,768]{2,1,0:T(8,128)(2,1)}) conditional(s32[]{:T(128)} %convert_element_type.4, () %tuple.40, (bf16[256,128]{1,0:T(8,128)(2,1)}, bf16[256,128]{1,0:T(8,128)(2,1)}, bf16[256,128]{1,0:T(8,128)(2,1)}, ...), branch_computations={%region_4.5_spmd, %region_5.6_spmd} | conditional | flops 196608 | bytes 31065044 | solution.py:399
  96.8 3.0 %collective-permute-start.13 = (bf16[8,192,128]{2,1,0:T(8,128)(2,1)}, bf16[8,192,128]{2,1,0:T(8,128)(2,1)S(1)}, u32[]{:S(2)}, u32[]{:S(2)}) collective-permute-start(bf16[8,192,128]{2,1,0:T(8,128)(2,1)} %get-tuple-element.119.refs_0_), channel_id=1, source_target_pairs={{0,3},{1,0},{2,1},{3,2},{4,7},{5,4},{6,5},{7,6},{8,11},{9,8},{10,9... | collective-permute-start | bytes 1179656 | tf_op jit(solution)/shard_map/cond/branch_1_fun/ppermute | solution.py:49
  105.3 29.2 %collective-permute-done.18 = bf16[8,16,128]{2,1,0:T(8,128)(2,1)S(1)} collective-permute-done((bf16[8,16,128]{2,1,0:T(8,128)(2,1)}, bf16[8,16,128]{2,1,0:T(8,128)(2,1)S(1)}, u32[]{:S(2)}, u32[]{:S(2)}) %collective-permute-start.18) | collective-permute-done | bytes 32800 | tf_op jit(solution)/shard_map/cond/branch_1_fun/ppermute | solution.py:49
  135.6 3.1 %collective-permute-done.20 = bf16[8,16,128]{2,1,0:T(8,128)(2,1)S(1)} collective-permute-done((bf16[8,16,128]{2,1,0:T(8,128)(2,1)}, bf16[8,16,128]{2,1,0:T(8,128)(2,1)S(1)}, u32[]{:S(2)}, u32[]{:S(2)}) %collective-permute-start.20) | collective-permute-done | bytes 32800 | tf_op jit(solution)/shard_map/cond/branch_1_fun/ppermute | solution.py:49
  142.7 3.3 %collective-permute-done.23.refs_11_ = bf16[4,8,16,128]{3,2,1,0:T(8,128)(2,1)S(1)} collective-permute-done((bf16[4,8,16,128]{3,2,1,0:T(8,128)(2,1)S(1)}, bf16[4,8,16,128]{3,2,1,0:T(8,128)(2,1)S(1)}, u32[]{:S(2)}, u32[]{:S(2)}) %collective-permute-start.23) | collective-permute-done | bytes 131104 | tf_op jit(solution)/shard_map/cond/branch_1_fun/ppermute | solution.py:39
  147.6 4.9 %collective-permute-done.22.refs_10_ = bf16[4,8,16,128]{3,2,1,0:T(8,128)(2,1)S(1)} collective-permute-done((bf16[4,8,16,128]{3,2,1,0:T(8,128)(2,1)S(1)}, bf16[4,8,16,128]{3,2,1,0:T(8,128)(2,1)S(1)}, u32[]{:S(2)}, u32[]{:S(2)}) %collective-permute-start.22) | collective-permute-done | bytes 131104 | tf_op jit(solution)/shard_map/cond/branch_1_fun/ppermute | solution.py:39
  152.5 3.2 %collective-permute-start.21 = (bf16[4,8,16,128]{3,2,1,0:T(8,128)(2,1)S(1)}, bf16[4,8,16,128]{3,2,1,0:T(8,128)(2,1)S(1)}, u32[]{:S(2)}, u32[]{:S(2)}) collective-permute-start(bf16[4,8,16,128]{3,2,1,0:T(8,128)(2,1)S(1)} %pad_maximum_fusion.refs_8_), channel_id=1, source_target_pairs={{0,64},{32,96},{64,128},{96,160},{128,192},{160,224},{192,0},{224,... | collective-permute-start | bytes 393224 | tf_op jit(solution)/shard_map/cond/branch_1_fun/ppermute | solution.py:39
  159.4 6.9 %deltas.1 = (bf16[16,16,768]{2,1,0:T(8,128)(2,1)S(1)}, bf16[16,16,768]{2,1,0:T(8,128)(2,1)}, bf16[16,16,768]{2,1,0:T(8,128)(2,1)}, bf16[16,16,768]{2,1,0:T(8,128)(2,1)}) custom-call(s32[2]{0:T(128)S(1)} %get-tuple-element.109.ids, s32[512]{0:T(512)S(1)} %get-tuple-element.110.table, bf16[8,192,128]{2,1,0:T(8,128)(2,1)} %get-tuple-element.119.refs_0_, ...), custom_call_target="tpu_custom_call" | custom-call | tf_op jit(solution)/shard_map/cond/branch_1_fun/deltas/pallas_call | solution.py:384
  166.8 4.1 %collective-permute-start.25 = (bf16[16,16,768]{2,1,0:T(8,128)(2,1)}, bf16[16,16,768]{2,1,0:T(8,128)(2,1)}, u32[]{:S(2)}, u32[]{:S(2)}) collective-permute-start(bf16[16,16,768]{2,1,0:T(8,128)(2,1)} %get-tuple-element.126), channel_id=1, source_target_pairs={{0,128},{32,160},{64,192},{96,224},{128,0},{160,32},{192,64},{224,... | collective-permute-start | bytes 1179656 | tf_op jit(solution)/shard_map/cond/branch_1_fun/ppermute | solution.py:39
  171.6 6.6 %collective-permute-done.24 = bf16[16,16,768]{2,1,0:T(8,128)(2,1)} collective-permute-done((bf16[16,16,768]{2,1,0:T(8,128)(2,1)}, bf16[16,16,768]{2,1,0:T(8,128)(2,1)}, u32[]{:S(2)}, u32[]{:S(2)}) %collective-permute-start.24) | collective-permute-done | bytes 393248 | tf_op jit(solution)/shard_map/cond/branch_1_fun/ppermute | solution.py:39
  180.0 4.1 %collective-permute-done.26 = bf16[16,16,768]{2,1,0:T(8,128)(2,1)} collective-permute-done((bf16[16,16,768]{2,1,0:T(8,128)(2,1)}, bf16[16,16,768]{2,1,0:T(8,128)(2,1)}, u32[]{:S(2)}, u32[]{:S(2)}) %collective-permute-start.26) | collective-permute-done | bytes 393248 | tf_op jit(solution)/shard_map/cond/branch_1_fun/ppermute | solution.py:39
  185.3 3.9 %merge.1 = bf16[16,16,3072]{2,1,0:T(8,128)(2,1)} custom-call(s32[2]{0:T(128)S(1)} %pad_add_fusion.ids, s32[512]{0:T(512)S(1)} %copy-done.23, bf16[32,16,1536]{2,1,0:T(8,128)(2,1)} %copy-done, bf16[32,16,1536]{2,1,0:T(8,128)(2,1)} %copy-done.1, bf16[16,16,768]{2,1,0:T(8,128)(2,1)S(1)} %get-tuple-element.187.refs_0_, ...), custom_call_target="tpu_custom_call" | custom-call | tf_op jit(solution)/shard_map/merge/pallas_call | solution.py:406
  (115 shorter events, 58.0 us)
Async XLA Ops:
  6.5 80.4 %all-to-all-start = ((bf16[32,16,1536]{2,1,0:T(8,128)(2,1)}), bf16[32,16,1536]{2,1,0:T(8,128)(2,1)S(1)}, u32[]{:S(2)}, u32[]{:S(2)}) async-start(bf16[32,16,1536]{2,1,0:T(8,128)(2,1)} %tiles.3), calls=%async_computation | async-start | bytes 3145728 | tf_op jit(solution)/shard_map/all_to_all | solution.py:313
  19.4 9.3 %collective-permute-start.30 = (bf16[704,128]{1,0:T(8,128)(2,1)}, bf16[704,128]{1,0:T(8,128)(2,1)}, u32[]{:S(2)}, u32[]{:S(2)}) collective-permute-start(bf16[704,128]{1,0:T(8,128)(2,1)} %pack.1), channel_id=1, source_target_pairs={{0,128},{32,160},{64,192},{96,224},{128,0},{160,32},{192,64},{224,... | collective-permute-start | bytes 540680 | tf_op jit(solution)/shard_map/ppermute | solution.py:39
  22.1 15.1 %collective-permute-start.27 = (bf16[704,128]{1,0:T(8,128)(2,1)}, bf16[704,128]{1,0:T(8,128)(2,1)}, u32[]{:S(2)}, u32[]{:S(2)}) collective-permute-start(bf16[704,128]{1,0:T(8,128)(2,1)} %pack.1), channel_id=1, source_target_pairs={{0,32},{32,0},{64,96},{96,64},{128,160},{160,128},{192,224},{224,1... | collective-permute-start | bytes 540680 | tf_op jit(solution)/shard_map/ppermute | solution.py:45
  26.6 10.5 %collective-permute-start.33 = (bf16[704,128]{1,0:T(8,128)(2,1)}, bf16[704,128]{1,0:T(8,128)(2,1)}, u32[]{:S(2)}, u32[]{:S(2)}) collective-permute-start(bf16[704,128]{1,0:T(8,128)(2,1)} %collective-permute-done.32), channel_id=1, source_target_pairs={{0,32},{32,0},{64,96},{96,64},{128,160},{160,128},{192,224},{224,1... | collective-permute-start | bytes 540680 | tf_op jit(solution)/shard_map/ppermute | solution.py:45
  50.1 10.6 %collective-permute-start.2 = (bf16[704,128]{1,0:T(8,128)(2,1)}, bf16[704,128]{1,0:T(8,128)(2,1)S(1)}, u32[]{:S(2)}, u32[]{:S(2)}) collective-permute-start(bf16[704,128]{1,0:T(8,128)(2,1)} %get-tuple-element.87), channel_id=1, source_target_pairs={{0,128},{32,160},{64,192},{96,224},{128,0},{160,32},{192,64},{224,... | collective-permute-start | bytes 540680 | tf_op jit(solution)/shard_map/cond/branch_1_fun/ppermute | solution.py:39
  51.5 10.0 %collective-permute-start.3 = (bf16[704,128]{1,0:T(8,128)(2,1)}, bf16[704,128]{1,0:T(8,128)(2,1)S(1)}, u32[]{:S(2)}, u32[]{:S(2)}) collective-permute-start(bf16[704,128]{1,0:T(8,128)(2,1)} %get-tuple-element.88), channel_id=1, source_target_pairs={{0,192},{32,224},{64,0},{96,32},{128,64},{160,96},{192,128},{224,1... | collective-permute-start | bytes 540680 | tf_op jit(solution)/shard_map/cond/branch_1_fun/ppermute | solution.py:39
  64.9 11.7 %collective-permute-start.4 = (bf16[256,128]{1,0:T(8,128)(2,1)}, bf16[256,128]{1,0:T(8,128)(2,1)}, u32[]{:S(2)}, u32[]{:S(2)}) collective-permute-start(bf16[256,128]{1,0:T(8,128)(2,1)} %get-tuple-element.96), channel_id=1, source_target_pairs={{0,4},{1,5},{2,6},{3,7},{4,8},{5,9},{6,10},{7,11},{8,12},{9,13},{1... | collective-permute-start | bytes 196616 | tf_op jit(solution)/shard_map/cond/branch_1_fun/ppermute | solution.py:55
  66.5 13.7 %collective-permute-start.5 = (bf16[256,128]{1,0:T(8,128)(2,1)}, bf16[256,128]{1,0:T(8,128)(2,1)}, u32[]{:S(2)}, u32[]{:S(2)}) collective-permute-start(bf16[256,128]{1,0:T(8,128)(2,1)} %get-tuple-element.97), channel_id=1, source_target_pairs={{0,8},{1,9},{2,10},{3,11},{4,12},{5,13},{6,14},{7,15},{8,16},{9,17... | collective-permute-start | bytes 196616 | tf_op jit(solution)/shard_map/cond/branch_1_fun/ppermute | solution.py:55
  68.8 11.3 %collective-permute-start.6 = (bf16[256,128]{1,0:T(8,128)(2,1)}, bf16[256,128]{1,0:T(8,128)(2,1)}, u32[]{:S(2)}, u32[]{:S(2)}) collective-permute-start(bf16[256,128]{1,0:T(8,128)(2,1)} %get-tuple-element.98), channel_id=1, source_target_pairs={{0,12},{1,13},{2,14},{3,15},{4,16},{5,17},{6,18},{7,19},{8,20},{9,... | collective-permute-start | bytes 196616 | tf_op jit(solution)/shard_map/cond/branch_1_fun/ppermute | solution.py:55
  73.9 12.1 %collective-permute-start.8 = (bf16[256,128]{1,0:T(8,128)(2,1)}, bf16[256,128]{1,0:T(8,128)(2,1)}, u32[]{:S(2)}, u32[]{:S(2)}) collective-permute-start(bf16[256,128]{1,0:T(8,128)(2,1)} %get-tuple-element.100), channel_id=1, source_target_pairs={{0,20},{1,21},{2,22},{3,23},{4,24},{5,25},{6,26},{7,27},{8,28},{9,... | collective-permute-start | bytes 196616 | tf_op jit(solution)/shard_map/cond/branch_1_fun/ppermute | solution.py:55
  76.6 9.9 %collective-permute-start.9 = (bf16[256,128]{1,0:T(8,128)(2,1)}, bf16[256,128]{1,0:T(8,128)(2,1)}, u32[]{:S(2)}, u32[]{:S(2)}) collective-permute-start(bf16[256,128]{1,0:T(8,128)(2,1)} %get-tuple-element.101), channel_id=1, source_target_pairs={{0,24},{1,25},{2,26},{3,27},{4,28},{5,29},{6,30},{7,31},{8,0},{9,1... | collective-permute-start | bytes 196616 | tf_op jit(solution)/shard_map/cond/branch_1_fun/ppermute | solution.py:55
  88.0 96.1 %all-to-all-start.1 = ((bf16[32,16,1536]{2,1,0:T(8,128)(2,1)}), bf16[32,16,1536]{2,1,0:T(8,128)(2,1)S(1)}, u32[]{:S(2)}, u32[]{:S(2)}) async-start(bf16[32,16,1536]{2,1,0:T(8,128)(2,1)} %tiles.2), calls=%async_computation.1 | async-start | bytes 3145728 | tf_op jit(solution)/shard_map/all_to_all | solution.py:368
  96.8 45.3 %collective-permute-start.13 = (bf16[8,192,128]{2,1,0:T(8,128)(2,1)}, bf16[8,192,128]{2,1,0:T(8,128)(2,1)S(1)}, u32[]{:S(2)}, u32[]{:S(2)}) collective-permute-start(bf16[8,192,128]{2,1,0:T(8,128)(2,1)} %get-tuple-element.119.refs_0_), channel_id=1, source_target_pairs={{0,3},{1,0},{2,1},{3,2},{4,7},{5,4},{6,5},{7,6},{8,11},{9,8},{10,9... | collective-permute-start | bytes 1179656 | tf_op jit(solution)/shard_map/cond/branch_1_fun/ppermute | solution.py:49
  99.8 42.3 %collective-permute-start.12 = (bf16[8,192,128]{2,1,0:T(8,128)(2,1)}, bf16[8,192,128]{2,1,0:T(8,128)(2,1)S(1)}, u32[]{:S(2)}, u32[]{:S(2)}) collective-permute-start(bf16[8,192,128]{2,1,0:T(8,128)(2,1)} %get-tuple-element.119.refs_0_), channel_id=1, source_target_pairs={{0,2},{1,3},{2,0},{3,1},{4,6},{5,7},{6,4},{7,5},{8,10},{9,11},{10,... | collective-permute-start | bytes 1179656 | tf_op jit(solution)/shard_map/cond/branch_1_fun/ppermute | solution.py:49
  100.6 41.9 %collective-permute-start.11 = (bf16[8,192,128]{2,1,0:T(8,128)(2,1)}, bf16[8,192,128]{2,1,0:T(8,128)(2,1)S(1)}, u32[]{:S(2)}, u32[]{:S(2)}) collective-permute-start(bf16[8,192,128]{2,1,0:T(8,128)(2,1)} %get-tuple-element.119.refs_0_), channel_id=1, source_target_pairs={{0,1},{1,2},{2,3},{3,0},{4,5},{5,6},{6,7},{7,4},{8,9},{9,10},{10,1... | collective-permute-start | bytes 1179656 | tf_op jit(solution)/shard_map/cond/branch_1_fun/ppermute | solution.py:49
  101.5 33.0 %collective-permute-start.18 = (bf16[8,16,128]{2,1,0:T(8,128)(2,1)}, bf16[8,16,128]{2,1,0:T(8,128)(2,1)S(1)}, u32[]{:S(2)}, u32[]{:S(2)}) collective-permute-start(bf16[8,16,128]{2,1,0:T(8,128)(2,1)} %get-tuple-element.121), channel_id=1, source_target_pairs={{0,1},{1,2},{2,3},{3,0},{4,5},{5,6},{6,7},{7,4},{8,9},{9,10},{10,1... | collective-permute-start | bytes 98312 | tf_op jit(solution)/shard_map/cond/branch_1_fun/ppermute | solution.py:49
  103.3 32.3 %collective-permute-start.19 = (bf16[8,16,128]{2,1,0:T(8,128)(2,1)}, bf16[8,16,128]{2,1,0:T(8,128)(2,1)S(1)}, u32[]{:S(2)}, u32[]{:S(2)}) collective-permute-start(bf16[8,16,128]{2,1,0:T(8,128)(2,1)} %get-tuple-element.122), channel_id=1, source_target_pairs={{0,2},{1,3},{2,0},{3,1},{4,6},{5,7},{6,4},{7,5},{8,10},{9,11},{10,... | collective-permute-start | bytes 98312 | tf_op jit(solution)/shard_map/cond/branch_1_fun/ppermute | solution.py:49
  135.6 22.6 %collective-permute-start.14 = (bf16[8,192,128]{2,1,0:T(8,128)(2,1)}, bf16[8,192,128]{2,1,0:T(8,128)(2,1)S(1)}, u32[]{:S(2)}, u32[]{:S(2)}) collective-permute-start(bf16[8,192,128]{2,1,0:T(8,128)(2,1)} %get-tuple-element.119.refs_0_), channel_id=1, source_target_pairs={{0,32},{32,0},{64,96},{96,64},{128,160},{160,128},{192,224},{224,1... | collective-permute-start | bytes 1179656 | tf_op jit(solution)/shard_map/cond/branch_1_fun/ppermute | solution.py:45
  142.0 16.2 %collective-permute-start.17 = (bf16[8,192,128]{2,1,0:T(8,128)(2,1)S(1)}, bf16[8,192,128]{2,1,0:T(8,128)(2,1)S(1)}, u32[]{:S(2)}, u32[]{:S(2)}) collective-permute-start(bf16[8,192,128]{2,1,0:T(8,128)(2,1)S(1)} %collective-permute-done.13.refs_3_), channel_id=1, source_target_pairs={{0,32},{32,0},{64,96},{96,64},{128,160},{160,128},{192,224},{224,1... | collective-permute-start | bytes 1179656 | tf_op jit(solution)/shard_map/cond/branch_1_fun/ppermute | solution.py:45
  142.1 16.2 %collective-permute-start.16 = (bf16[8,192,128]{2,1,0:T(8,128)(2,1)S(1)}, bf16[8,192,128]{2,1,0:T(8,128)(2,1)S(1)}, u32[]{:S(2)}, u32[]{:S(2)}) collective-permute-start(bf16[8,192,128]{2,1,0:T(8,128)(2,1)S(1)} %collective-permute-done.12.refs_2_), channel_id=1, source_target_pairs={{0,32},{32,0},{64,96},{96,64},{128,160},{160,128},{192,224},{224,1... | collective-permute-start | bytes 1179656 | tf_op jit(solution)/shard_map/cond/branch_1_fun/ppermute | solution.py:45
  142.6 15.7 %collective-permute-start.15 = (bf16[8,192,128]{2,1,0:T(8,128)(2,1)S(1)}, bf16[8,192,128]{2,1,0:T(8,128)(2,1)S(1)}, u32[]{:S(2)}, u32[]{:S(2)}) collective-permute-start(bf16[8,192,128]{2,1,0:T(8,128)(2,1)S(1)} %collective-permute-done.11.refs_1_), channel_id=1, source_target_pairs={{0,32},{32,0},{64,96},{96,64},{128,160},{160,128},{192,224},{224,1... | collective-permute-start | bytes 1179656 | tf_op jit(solution)/shard_map/cond/branch_1_fun/ppermute | solution.py:45
  166.4 11.8 %collective-permute-start.24 = (bf16[16,16,768]{2,1,0:T(8,128)(2,1)}, bf16[16,16,768]{2,1,0:T(8,128)(2,1)}, u32[]{:S(2)}, u32[]{:S(2)}) collective-permute-start(bf16[16,16,768]{2,1,0:T(8,128)(2,1)} %get-tuple-element.125), channel_id=1, source_target_pairs={{0,192},{32,224},{64,0},{96,32},{128,64},{160,96},{192,128},{224,1... | collective-permute-start | bytes 1179656 | tf_op jit(solution)/shard_map/cond/branch_1_fun/ppermute | solution.py:39
  166.8 13.2 %collective-permute-start.25 = (bf16[16,16,768]{2,1,0:T(8,128)(2,1)}, bf16[16,16,768]{2,1,0:T(8,128)(2,1)}, u32[]{:S(2)}, u32[]{:S(2)}) collective-permute-start(bf16[16,16,768]{2,1,0:T(8,128)(2,1)} %get-tuple-element.126), channel_id=1, source_target_pairs={{0,128},{32,160},{64,192},{96,224},{128,0},{160,32},{192,64},{224,... | collective-permute-start | bytes 1179656 | tf_op jit(solution)/shard_map/cond/branch_1_fun/ppermute | solution.py:39
  170.9 13.2 %collective-permute-start.26 = (bf16[16,16,768]{2,1,0:T(8,128)(2,1)}, bf16[16,16,768]{2,1,0:T(8,128)(2,1)}, u32[]{:S(2)}, u32[]{:S(2)}) collective-permute-start(bf16[16,16,768]{2,1,0:T(8,128)(2,1)} %get-tuple-element.127), channel_id=1, source_target_pairs={{0,64},{32,96},{64,128},{96,160},{128,192},{160,224},{192,0},{224,... | collective-permute-start | bytes 1179656 | tf_op jit(solution)/shard_map/cond/branch_1_fun/ppermute | solution.py:39
  (37 other events, 289.2 us)

commit v2 on v1

--- a/solution.py
+++ b/solution.py
@@ -1,5 +1,3 @@
-import functools
-
 import jax
 import jax.numpy as jnp
 from jax import lax
@@ -11,6 +9,7 @@
 TILE_ROWS = 16
 TILES = 32
 SLOTS = 16
+EARLY = 1
 Z, Y, DP = 8, 4, 8
 X = 4
 
@@ -51,12 +50,6 @@
     )
 
 
-def shift_z(array, k):
-    return lax.ppermute(
-        array, "expert", [(i, (i // Y + k) % Z * Y + i % Y) for i in range(Z * Y)]
-    )
-
-
 def vmem():
     return pl.BlockSpec(memory_space=pltpu.VMEM)
 
@@ -75,7 +68,7 @@
 def gradient_kernel(ids, counts, x, g, *refs):
     blocks, keep, give = refs[:DP], refs[DP], refs[DP + 1]
     chip, core = ids[0] // 2, lax.rem(ids[0], 2)
-    live = counts[ids[0], 0]
+    live = counts[ids[0]]
     rows = x.shape[0]
     a_rows = x.shape[1] // DP
     cols = g.shape[1] // DP
@@ -140,13 +133,12 @@
     blocks = refs[:X]
     a, a1, a2, b, b1, b2 = refs[X : X + 6]
     na, na1, na2, nb, nb1, nb2 = refs[X + 6 : X + 12]
-    outs, ah = refs[X + 12 : -1], refs[-1]
-    tokens = counts[0, 0]
+    send, rest, rows, ah = refs[X + 12 :]
+    tokens = counts[0]
     for p in range(1, DP):
-        tokens += counts[p, 0]
+        tokens += counts[p]
     factor = adapter_scale / jnp.full((1, 128), tokens, jnp.int32).astype(F32)
     a_rows = a.shape[0]
-    b_rows = b.shape[1] // 128 * LOW_RANK
 
     def total(lo, hi):
         s = blocks[0][lo:hi, :].astype(F32)
@@ -159,61 +151,80 @@
         grad = total(a_rows + t * LOW_RANK, a_rows + (t + 1) * LOW_RANK)
         new, one, two = adam_step(b[:, c], b1[:, c], b2[:, c], grad)
         nb[:, c], nb1[:, c], nb2[:, c] = new, one, two
-        for dz in range(Z):
-            outs[dz][t * LOW_RANK : (t + 1) * LOW_RANK, :] = new.astype(BF16)
+        if t < EARLY:
+            for dz in range(Z):
+                send[dz, t * LOW_RANK : (t + 1) * LOW_RANK, :] = new.astype(BF16)
+        else:
+            rest[(t - EARLY) * LOW_RANK : (t - EARLY + 1) * LOW_RANK, :] = new.astype(BF16)
     for t in range(a_rows // 128):
         r = slice(t * 128, (t + 1) * 128)
         grad = jnp.transpose(total(t * 128, (t + 1) * 128))
         new, one, two = adam_step(a[r, :], a1[r, :], a2[r, :], grad)
         na[r, :], na1[r, :], na2[r, :] = new, one, two
         ah[r, :] = new.astype(BF16)
-    z, y = ids[1] // Y, lax.rem(ids[1], Y)
+    for owner in range(Z * Y):
+        start = pl.multiple_of(pick[owner] * TILE_ROWS, TILE_ROWS)
+        rows[owner * TILE_ROWS : (owner + 1) * TILE_ROWS, :] = ah[pl.ds(start, TILE_ROWS), :]
+    y = lax.rem(ids[1], Y)
     for dz in range(Z):
         for dy in range(Y):
-            owner = lax.rem(z + dz, Z) * Y + lax.rem(y + dy, Y)
-            start = pl.multiple_of(pick[owner] * TILE_ROWS, TILE_ROWS)
-            r = slice(b_rows + dy * TILE_ROWS, b_rows + (dy + 1) * TILE_ROWS)
-            outs[dz][r, :] = ah[pl.ds(start, TILE_ROWS), :]
-
-
-def tiles_kernel(half, pick, frozen, out, sem):
-    cols = out.shape[2]
+            owner = dz * Y + lax.rem(y + dy, Y)
+            start = pl.multiple_of(owner * TILE_ROWS, TILE_ROWS)
+            first = EARLY * LOW_RANK + dy * TILE_ROWS
+            send[dz, first : first + TILE_ROWS, :] = rows[pl.ds(start, TILE_ROWS), :]
+
+
+def tiles_kernel(pick, frozen, early, late, whole, sem):
     copies = []
-    for owner in range(out.shape[0]):
-        start = pl.multiple_of(pick[owner] * TILE_ROWS, TILE_ROWS)
-        src = frozen.at[pl.ds(start, TILE_ROWS), pl.ds(half * cols, cols)]
-        copies.append(pltpu.make_async_copy(src, out.at[owner], sem.at[owner]))
-    for copy in copies:
-        copy.start()
-    for copy in copies:
-        copy.wait()
-
-
-def send_tiles(half, pick, frozen):
-    shape = (Z * Y, TILE_ROWS, frozen.shape[1] // 2)
-    return pl.pallas_call(
-        functools.partial(tiles_kernel, half),
-        out_shape=jax.ShapeDtypeStruct(shape, BF16),
-        in_specs=[smem(), anywhere()],
-        out_specs=vmem(),
-        scratch_shapes=[pltpu.SemaphoreType.DMA((Z * Y,))],
-        compiler_params=PARAMS,
-        name="tiles",
-    )(pick, frozen)
-
-
-def stack_kernel(*refs):
-    ins, up, downs = refs[:Z], refs[Z], refs[Z + 1 :]
-    b_rows = up.shape[1]
-    for i, ref in enumerate(ins):
-        up[i] = ref[:b_rows, :]
-        for dy, down in enumerate(downs):
-            down[i] = ref[b_rows + dy * TILE_ROWS : b_rows + (dy + 1) * TILE_ROWS, :]
+    for owner in range(Z * Y):
+        rows = pl.ds(pl.multiple_of(pick[owner] * TILE_ROWS, TILE_ROWS), TILE_ROWS)
+        copies.append(
+            pltpu.make_async_copy(frozen.at[rows, :], whole.at[owner], sem.at[owner])
+        )
+        copies[owner].start()
+    cols, one, two = whole.shape[2] // DP, early.shape[2] // DP, late.shape[2] // DP
+    for owner in range(Z * Y):
+        copies[owner].wait()
+        for j in range(DP):
+            tile = whole[owner, :, j * cols : (j + 1) * cols]
+            early[owner, :, j * one : (j + 1) * one] = tile[:, :one]
+            late[owner, :, j * two : (j + 1) * two] = tile[:, one:]
+
+
+def mix_kernel(ids, late, rows, *refs):
+    blocks, out = refs[:DP], refs[DP]
+    chip, core = ids[0] // 2, lax.rem(ids[0], 2)
+    cols = out.shape[2] // DP
+    for i in range(DP):
+        k, c = i // 2, i % 2
+        j = 2 * lax.rem(chip + X - k, X) + (1 - core if c else core)
+        left = jnp.where(j < DP // 2, rows[:, :LOW_RANK], rows[:, LOW_RANK:])
+        for t in range(cols // 128):
+            right = blocks[i][t * LOW_RANK : (t + 1) * LOW_RANK, :]
+            delta = adapter_scale * jnp.dot(left, right, preferred_element_type=F32)
+            span = pl.ds(pl.multiple_of(j * cols + t * 128, 128), 128)
+            base = late[:, :, span].astype(F32)
+            out[:, :, span] = (base + delta.reshape(base.shape)).astype(BF16)
+
+
+def stack_kernel(arrived, *outs):
+    b_rows = arrived.shape[1] - Y * TILE_ROWS
+    for dy, out in enumerate(outs):
+        first = b_rows + dy * TILE_ROWS
+        out[:, :b_rows, :] = arrived[:, :b_rows, :]
+        out[:, b_rows:, :] = arrived[:, first : first + TILE_ROWS, :]
+
+
+def rows_kernel(*refs):
+    parts, out = refs[:Y], refs[Y]
+    b_rows = parts[0].shape[1] - TILE_ROWS
+    for dy, part in enumerate(parts):
+        out[dy] = part[:, b_rows:, :]
 
 
 def slot_of(ids, table, s):
     source = table[ids[1] * SLOTS + s] // TILES
-    dz = lax.rem(ids[1] // Y + Z - source // Y, Z)
+    dz = source // Y
     dy = lax.rem(lax.rem(ids[1], Y) + Y - lax.rem(source, Y), Y)
     return source, dz, dy
 
@@ -224,6 +235,7 @@
     n_tiles = own.shape[1] // LOW_RANK
     cols = n_tiles * 128
     chip, core = ids[0] // 2, lax.rem(ids[0], 2)
+    up = pl.ds(0, own.shape[1])
     places = []
     for s in range(SLOTS):
         _, dz, dy = slot_of(ids, table, s)
@@ -232,43 +244,44 @@
 
             @pl.when(dy == i)
             def _(s=s, i=i, dz=dz):
-                pltpu.make_async_copy(ups[i].at[dz], own.at[s], sem.at[0, s]).start()
-                pltpu.make_async_copy(others[i].at[dz], other.at[s], sem.at[1, s]).start()
-
+                pltpu.make_async_copy(ups[i].at[dz, up], own.at[s], sem.at[0, s]).start()
+                pltpu.make_async_copy(others[i].at[dz, up], other.at[s], sem.at[1, s]).start()
+
+    for s in range(SLOTS):
+        pltpu.make_async_copy(ups[0].at[0, up], own.at[s], sem.at[0, s]).wait()
+        pltpu.make_async_copy(others[0].at[0, up], other.at[s], sem.at[1, s]).wait()
     is_gate = chip < X // 2
-    first = jnp.int32(0) == core
+    spans = [pl.ds(pl.multiple_of(c * cols, 128), cols) for c in (core, 1 - core)]
     for s in range(SLOTS):
-        pltpu.make_async_copy(ups[0].at[0], own.at[s], sem.at[0, s]).wait()
-        pltpu.make_async_copy(others[0].at[0], other.at[s], sem.at[1, s]).wait()
         left = jnp.concatenate([downs[k][places[s]] for k in range(X)], axis=0)
         left = jnp.where(is_gate, left[:, :LOW_RANK], left[:, LOW_RANK:])
-        halves = []
-        for ref in (own, other):
+        for ref, span in zip((own, other), spans):
             right = jnp.concatenate(
                 [ref[s, t * LOW_RANK : (t + 1) * LOW_RANK, :] for t in range(n_tiles)], axis=1
             )
             delta = adapter_scale * jnp.dot(left, right, preferred_element_type=F32)
-            halves.append(delta.astype(BF16))
-        mine, theirs = halves
-        for k in range(X):
-            r = slice(k * TILE_ROWS, (k + 1) * TILE_ROWS)
-            outs[k][s, :, :cols] = jnp.where(first, mine[r], theirs[r])
-            outs[k][s, :, cols:] = jnp.where(first, theirs[r], mine[r])
-
-
-def merge_kernel(ids, table, low, high, *refs):
+            delta = delta.astype(BF16)
+            for k in range(X):
+                outs[k][s, :, span] = delta[k * TILE_ROWS : (k + 1) * TILE_ROWS]
+
+
+def merge_kernel(ids, table, early, late, *refs):
     deltas, out = refs[:X], refs[X]
     chip = ids[0] // 2
-    cols = deltas[0].shape[2]
-    width = low.shape[2]
+    one, two = early.shape[2] // DP, late.shape[2] // DP
     for s in range(SLOTS):
         source = table[ids[1] * SLOTS + s] // TILES
-        out[s, :, :width] = low[source]
-        out[s, :, width:] = high[source]
         for k in range(X):
-            j = lax.rem(chip + k, X)
-            c = pl.ds(pl.multiple_of(j * cols, 128), cols)
-            out[s, :, c] = (out[s, :, c].astype(F32) + deltas[k][s].astype(F32)).astype(BF16)
+            for c in range(2):
+                j = 2 * lax.rem(chip + k, X) + c
+                span = pl.ds(pl.multiple_of(j * one, 128), one)
+                new = early[source, :, span].astype(F32)
+                new += deltas[k][s, :, c * one : (c + 1) * one].astype(F32)
+                start = pl.multiple_of(j * (one + two), 128)
+                out[s, :, pl.ds(start, one)] = new.astype(BF16)
+        for j in range(DP):
+            start = j * (one + two) + one
+            out[s, :, start : start + two] = late[source, :, j * two : (j + 1) * two]
 
 
 def per_device(
@@ -290,31 +303,59 @@
     a, a1, a2 = a_param[0], a_first[0], a_second[0]
     b, b1, b2 = b_param[0], b_first[0], b_second[0]
     frozen = frozen_tiles[0]
+    counts = token_counts.reshape(DP)
     a_rows, width = a.shape[0], frozen.shape[1]
     cols = b.shape[1]
     shape_a, shape_b = jax.ShapeDtypeStruct(a.shape, F32), jax.ShapeDtypeStruct(b.shape, F32)
     shape_block = jax.ShapeDtypeStruct((a_rows + cols // 128 * LOW_RANK, 128), BF16)
 
-    block = pl.pallas_call(
-        pack_kernel,
-        out_shape=shape_block,
-        in_specs=[vmem()] * 2,
-        out_specs=vmem(),
-        compiler_params=PARAMS,
-        name="pack",
-    )(a, b)
-    blocks = []
-    for k in range(X):
-        mine = block if k == 0 else shift_x(block, k)
-        blocks += [mine, swap_core(mine)]
-
     table = placement_map.reshape(Z * Y, SLOTS)
     pick = jnp.sum(jnp.where(table // TILES == expert, table % TILES, 0), axis=1)
-    low = lax.all_to_all(
-        send_tiles(0, pick, frozen), "expert", split_axis=0, concat_axis=0, tiled=True
-    )
-
-    def update(x, g, a, a1, a2, b, b1, b2, ids, pick, *blocks):
+    n_tiles = cols // 128
+    sizes = [DP * EARLY * 128, DP * (n_tiles - EARLY) * 128]
+    halves = [jax.ShapeDtypeStruct((Z * Y, TILE_ROWS, n), BF16) for n in sizes]
+    some = dp < DP
+
+    def zeros(shapes):
+        return lambda *_: tuple(jnp.zeros(s.shape, s.dtype) for s in shapes)
+
+    def begin(a, b, pick, frozen):
+        block = pl.pallas_call(
+            pack_kernel,
+            out_shape=shape_block,
+            in_specs=[vmem()] * 2,
+            out_specs=vmem(),
+            compiler_params=PARAMS,
+            name="pack",
+        )(a, b)
+        chips = [block] + [shift_x(block, k) for k in range(1, X)]
+        tiles = pl.pallas_call(
+            tiles_kernel,
+            out_shape=halves,
+            in_specs=[smem(), anywhere()],
+            out_specs=[vmem()] * 2,
+            scratch_shapes=[
+                pltpu.VMEM((Z * Y, TILE_ROWS, width), BF16),
+                pltpu.SemaphoreType.DMA((Z * Y,)),
+            ],
+            compiler_params=PARAMS,
+            cost_estimate=pl.CostEstimate(
+                flops=0, bytes_accessed=16 * Z * Y * TILE_ROWS * width, transcendentals=0
+            ),
+            name="tiles",
+        )(pick, frozen)
+        tiles, chips[-1] = lax.optimization_barrier((tiles, chips[-1]))
+        blocks = [b for mine in chips for b in (mine, swap_core(mine))]
+        return (*tiles, *blocks)
+
+    early_out, late_base, *blocks = lax.cond(
+        some, begin, zeros(halves + [shape_block] * DP), a, b, pick, frozen
+    )
+    early = lax.all_to_all(early_out, "expert", split_axis=0, concat_axis=0, tiled=True)
+    rest = jax.ShapeDtypeStruct(((n_tiles - EARLY) * LOW_RANK, 128), BF16)
+    rows = jax.ShapeDtypeStruct((Z * Y * TILE_ROWS, 128), BF16)
+
+    def update(x, g, a, a1, a2, b, b1, b2, ids, pick, counts, *blocks):
         kept, given = pl.pallas_call(
             gradient_kernel,
             out_shape=[jax.ShapeDtypeStruct((X,) + shape_block.shape, BF16)] * 2,
@@ -322,7 +363,7 @@
             out_specs=[vmem()] * 2,
             compiler_params=PARAMS,
             name="gradients",
-        )(ids, token_counts, x, g, *blocks)
+        )(ids, counts, x, g, *blocks)
         taken = swap_core(given)
         pairs = pl.pallas_call(
             pair_kernel,
@@ -334,53 +375,72 @@
         )(kept, taken)
         sums = [pairs[0]] + [shift_x(pairs[k], k) for k in range(1, X)]
 
-        new_a, new_a1, new_a2, new_b, new_b1, new_b2, *messages = pl.pallas_call(
+        new_a, new_a1, new_a2, new_b, new_b1, new_b2, messages, b_rest, a_rows = pl.pallas_call(
             adam_kernel,
-            out_shape=[shape_a] * 3 + [shape_b] * 3 + [message] * Z,
+            out_shape=[shape_a] * 3 + [shape_b] * 3 + [message, rest, rows],
             in_specs=[smem()] * 3 + [vmem()] * (X + 6),
-            out_specs=[vmem()] * (6 + Z),
+            out_specs=[vmem()] * 9,
             scratch_shapes=[pltpu.VMEM(a.shape, BF16)],
             compiler_params=PARAMS,
             name="adam",
-        )(ids, pick, token_counts, *sums, a, a1, a2, b, b1, b2)
-        arrived = [messages[dz] if dz == 0 else shift_z(messages[dz], dz) for dz in range(Z)]
-        return (new_a, new_a1, new_a2, new_b, new_b1, new_b2, *arrived)
-
-    some = jnp.min(token_counts) > 0
-    b_rows = cols // 128 * LOW_RANK
-    message = jax.ShapeDtypeStruct((b_rows + Y * TILE_ROWS, 128), BF16)
-    part = jax.ShapeDtypeStruct((SLOTS, TILE_ROWS, 2 * cols), BF16)
-
-    def zeros(shapes):
-        return lambda *_: tuple(jnp.zeros(s.shape, s.dtype) for s in shapes)
+        )(ids, pick, counts, *sums, a, a1, a2, b, b1, b2)
+        return (new_a, new_a1, new_a2, new_b, new_b1, new_b2, messages, b_rest, a_rows)
+
+    b_rows = EARLY * LOW_RANK
+    message = jax.ShapeDtypeStruct((Z, b_rows + Y * TILE_ROWS, 128), BF16)
+    part = jax.ShapeDtypeStruct((SLOTS, TILE_ROWS, 2 * EARLY * 128), BF16)
 
     outs = lax.cond(
         some,
         update,
-        zeros([shape_a] * 3 + [shape_b] * 3 + [message] * Z),
-        *(x, g, a, a1, a2, b, b1, b2, ids, pick, *blocks),
+        zeros([shape_a] * 3 + [shape_b] * 3 + [message, rest, rows]),
+        *(x, g, a, a1, a2, b, b1, b2, ids, pick, counts, *blocks),
     )
     new_a, new_a1, new_a2, new_b, new_b1, new_b2 = outs[:6]
 
-    high_out, low, arrived = lax.optimization_barrier(
-        (send_tiles(1, pick, frozen), low, outs[6:])
-    )
-    high = lax.all_to_all(high_out, "expert", split_axis=0, concat_axis=0, tiled=True)
-
-    def spread(ids, placement_map, *arrived):
-        up, *downs = pl.pallas_call(
+    messages, b_rest, a_rows = outs[6:]
+    chips = [b_rest] + [shift_x(b_rest, k) for k in range(1, X)]
+    messages, early = lax.optimization_barrier((messages, early))
+    arrived = lax.all_to_all(
+        messages,
+        "expert",
+        split_axis=0,
+        concat_axis=0,
+        tiled=True,
+        axis_index_groups=[[z * Y + y for z in range(Z)] for y in range(Y)],
+    )
+    others = [b for mine in chips for b in (mine, swap_core(mine))]
+    mixed = pl.pallas_call(
+        mix_kernel,
+        out_shape=jax.ShapeDtypeStruct(late_base.shape, BF16),
+        in_specs=[smem()] + [vmem()] * (2 + DP),
+        out_specs=vmem(),
+        compiler_params=PARAMS,
+        name="mix",
+    )(ids, late_base, a_rows, *others)
+    mixed, arrived = lax.optimization_barrier((mixed, arrived))
+    late = lax.all_to_all(mixed, "expert", split_axis=0, concat_axis=0, tiled=True)
+
+    def spread(ids, placement_map, arrived):
+        parts = pl.pallas_call(
             stack_kernel,
-            out_shape=[jax.ShapeDtypeStruct((Z, b_rows, 128), BF16)]
-            + [jax.ShapeDtypeStruct((Z, TILE_ROWS, 128), BF16)] * Y,
-            in_specs=[vmem()] * Z,
-            out_specs=[vmem()] * (1 + Y),
+            out_shape=[jax.ShapeDtypeStruct((Z, b_rows + TILE_ROWS, 128), BF16)] * Y,
+            in_specs=[vmem()],
+            out_specs=[vmem()] * Y,
             compiler_params=PARAMS,
             name="stack",
-        )(*arrived)
-        rows = jnp.stack([downs[0]] + [shift_y(downs[dy], dy) for dy in range(1, Y)])
-        ups = [up] + [shift_y(up, dy) for dy in range(1, Y)]
+        )(arrived)
+        ups = [parts[0]] + [shift_y(parts[dy], dy) for dy in range(1, Y)]
+        rows = pl.pallas_call(
+            rows_kernel,
+            out_shape=jax.ShapeDtypeStruct((Y, Z, TILE_ROWS, 128), BF16),
+            in_specs=[vmem()] * Y,
+            out_specs=vmem(),
+            compiler_params=PARAMS,
+            name="rows",
+        )(*ups)
+        chips = [rows] + [shift_x(rows, k) for k in range(1, X)]
         others = [swap_core(u) for u in ups]
-        chips = [rows] + [shift_x(rows, k) for k in range(1, X)]
         deltas = pl.pallas_call(
             delta_kernel,
             out_shape=[part] * X,
@@ -400,7 +460,7 @@
         some,
         spread,
         zeros([part] * X),
-        *(ids, placement_map, *arrived),
+        *(ids, placement_map, arrived),
     )
 
     served = pl.pallas_call(
@@ -410,7 +470,7 @@
         out_specs=vmem(),
         compiler_params=PARAMS,
         name="merge",
-    )(ids, placement_map, low, high, *shifted)
+    )(ids, placement_map, early, late, *shifted)
 
     return (
         new_a[None],

time: 192 us -> 145 us (0.76)
  the two profiles are of different devices: /device:TPU:4 before, /device:TPU:128 now
where the time goes in v2:
time: 145 us; the launch traced here: 144 us
  waiting for transfers between devices  57.5 us (40%)
  starting transfers between devices  49.3 us (34%)
  Pallas kernels  31.1 us (21%)
  local copies, waits for them, and re-layouts  5.47 us (4%)
    ppermute x15, waiting for transfers between devices, shift_x(): lax.ppermute(array, 'dp', [(i, (i // 2 + k) % X * 2 + i % 2) for i in ran...  34.6 us
    ppermute x3, waiting for transfers between devices, shift_y(): lax.ppermute(array, 'expert', [(i, i // Y * Y + (i % Y + k) % Y) for i in...  18 us
    ppermute x15, starting transfers between devices, shift_x(): lax.ppermute(array, 'dp', [(i, (i // 2 + k) % X * 2 + i % 2) for i in ran...  15 us
    all_to_all x1, starting transfers between devices, per_device(): lax.all_to_all(early_out, 'expert', split_axis=0, concat_axis=0, tiled=True)  10.1 us
    all_to_all x1, starting transfers between devices, per_device(): lax.all_to_all(mixed, 'expert', split_axis=0, concat_axis=0, tiled=True)  9.8 us
    all_to_all x1, starting transfers between devices, per_device(): lax.all_to_all(messages, 'expert', split_axis=0, concat_axis=0, tiled=Tru...  7.22 us
    pallas_call x1, Pallas kernels, begin(): pl.pallas_call(tiles_kernel, out_shape=halves, in_specs=[smem(), anywhere...  5.61 us
    ppermute x3, starting transfers between devices, shift_y(): lax.ppermute(array, 'expert', [(i, i // Y * Y + (i % Y + k) % Y) for i in...  5.6 us
  transfers between devices with their start and end apart: 34, of which 20 were waited for; matrix products, arithmetic and copies ran while one was open for 0% of the time, Pallas kernels for 18%

profile of v2, /device:TPU:128, one launch (start us, length us, event | category | flops | bytes accessed | tf_op | source)
XLA Modules:
  0.0 144.5 jit_solution(15248590033596877686)
XLA Ops:
  1.5 18.2 %conditional.3 = (bf16[32,16,1024]{2,1,0:T(8,128)(2,1)}, bf16[32,16,2048]{2,1,0:T(8,128)(2,1)S(1)}, bf16[704,128]{1,0:T(8,128)(2,1)}, bf16[704,128]{1,0:T(8,128)...) conditional(s32[]{:T(128)} %convert_element_type.2, () %tuple.48, ...), branch_computations={%region_1.2_spmd, %region_2.3_spmd} | conditional | bytes 30212456 | solution.py:351
  3.2 2.8 %collective-permute-start = (bf16[704,128]{1,0:T(8,128)(2,1)}, bf16[704,128]{1,0:T(8,128)(2,1)}, u32[]{:S(2)}, u32[]{:S(2)}) collective-permute-start(bf16[704,128]{1,0:T(8,128)(2,1)} %pack.1), channel_id=1, source_target_pairs={{0,192},{32,224},{64,0},{96,32},{128,64},{160,96},{192,128},{224,1... | collective-permute-start | bytes 540680 | tf_op jit(solution)/shard_map/cond/branch_1_fun/ppermute | solution.py:38
  7.7 5.6 %tiles.1 = (bf16[32,16,1024]{2,1,0:T(8,128)(2,1)}, bf16[32,16,2048]{2,1,0:T(8,128)(2,1)S(1)}) custom-call(s32[32]{0:T(128)S(1)} %get-tuple-element.75.pick, bf16[512,3072]{1,0:T(8,128)(2,1)} %bitcast.21), custom_call_target="tpu_custom_call" | custom-call | bytes 25165824 | tf_op jit(solution)/shard_map/cond/branch_1_fun/tiles/pallas_call | solution.py:332
  15.3 2.4 %collective-permute-done.2 = bf16[704,128]{1,0:T(8,128)(2,1)} collective-permute-done((bf16[704,128]{1,0:T(8,128)(2,1)}, bf16[704,128]{1,0:T(8,128)(2,1)}, u32[]{:S(2)}, u32[]{:S(2)}) %collective-permute-start.2) | collective-permute-done | bytes 180256 | tf_op jit(solution)/shard_map/cond/branch_1_fun/ppermute | solution.py:38
  19.7 10.1 %all-to-all-start = ((bf16[32,16,1024]{2,1,0:T(8,128)(2,1)}), bf16[32,16,1024]{2,1,0:T(8,128)(2,1)S(1)}, u32[]{:S(2)}, u32[]{:S(2)}) async-start(bf16[32,16,1024]{2,1,0:T(8,128)(2,1)} %get-tuple-element.178), calls=%async_computation | async-start | bytes 2097152 | tf_op jit(solution)/shard_map/all_to_all | solution.py:354
  29.9 26.2 %conditional.4 = (bf16[8,128,128]{2,1,0:T(8,128)(2,1)}, bf16[128,128]{1,0:T(8,128)(2,1)}, bf16[512,128]{1,0:T(8,128)(2,1)S(1)}, f32[1,512,128]{2,1,0:T(8,128)}, ...) conditional(s32[]{:T(128)} %convert_element_type.2, () %tuple.47, ...), branch_computations={%region_3.4_spmd, %region_4.5_spmd} | conditional | bytes 8651124 | solution.py:393
  29.9 5.6 %gradients.1 = (bf16[4,704,128]{2,1,0:T(8,128)(2,1)}, bf16[4,704,128]{2,1,0:T(8,128)(2,1)}) custom-call(s32[2]{0:T(128)S(1)} %get-tuple-element.84.ids, s32[8]{0:T(128)S(1)} %bitcast.33, bf16[256,4096]{1,0:T(8,128)(2,1)} %bitcast.22, bf16[256,3072]{1,0:T(8,128)(2,1)} %bitcast.23, bf16[704,128]{1,0:T(8,128)(2,1)} %get-tuple-element.89.refs_0_, ...), custom_call_target="tpu_custom_call" | custom-call | tf_op jit(solution)/shard_map/cond/branch_1_fun/gradients/pallas_call | solution.py:359
  35.5 2.5 %collective-permute-done.7.taken = bf16[4,704,128]{2,1,0:T(8,128)(2,1)} collective-permute-done((bf16[4,704,128]{2,1,0:T(8,128)(2,1)}, bf16[4,704,128]{2,1,0:T(8,128)(2,1)}, u32[]{:S(2)}, u32[]{:S(2)}) %collective-permute-start.7) | collective-permute-done | bytes 720928 | tf_op jit(solution)/shard_map/cond/branch_1_fun/ppermute | solution.py:44
  43.7 8.5 %collective-permute-done.8.refs_1_ = bf16[704,128]{1,0:T(8,128)(2,1)S(1)} collective-permute-done((bf16[704,128]{1,0:T(8,128)(2,1)}, bf16[704,128]{1,0:T(8,128)(2,1)S(1)}, u32[]{:S(2)}, u32[]{:S(2)}) %collective-permute-start.8) | collective-permute-done | bytes 180256 | tf_op jit(solution)/shard_map/cond/branch_1_fun/ppermute | solution.py:38
  53.4 2.7 %adam.1 = (f32[512,128]{1,0:T(8,128)}, f32[512,128]{1,0:T(8,128)}, f32[512,128]{1,0:T(8,128)}, f32[64,384]{1,0:T(8,128)}, f32[64,384]{1,0:T(8,128)}, /*index=5*/...) custom-call(s32[2]{0:T(128)S(1)} %get-tuple-element.84.ids, ...), custom_call_target="tpu_custom_call" | custom-call | tf_op jit(solution)/shard_map/cond/branch_1_fun/adam/pallas_call | solution.py:378
  56.1 7.2 %all-to-all-start.1 = ((bf16[8,128,128]{2,1,0:T(8,128)(2,1)}), bf16[8,128,128]{2,1,0:T(8,128)(2,1)S(1)}, u32[]{:S(2)}, u32[]{:S(2)}) async-start(bf16[8,128,128]{2,1,0:T(8,128)(2,1)} %get-tuple-element.183), calls=%async_computation.1 | async-start | bytes 524288 | tf_op jit(solution)/shard_map/all_to_all | solution.py:404
  67.6 3.8 %collective-permute-done.27.refs_4_ = bf16[128,128]{1,0:T(8,128)(2,1)S(1)} collective-permute-done((bf16[128,128]{1,0:T(8,128)(2,1)}, bf16[128,128]{1,0:T(8,128)(2,1)S(1)}, u32[]{:S(2)}, u32[]{:S(2)}) %collective-permute-start.27) | collective-permute-done | bytes 32800 | tf_op jit(solution)/shard_map/ppermute | solution.py:38
  73.3 3.6 %mix.1 = bf16[32,16,2048]{2,1,0:T(8,128)(2,1)} custom-call(s32[2]{0:T(128)S(1)} %pad_add_fusion.ids, bf16[32,16,2048]{2,1,0:T(8,128)(2,1)S(1)} %get-tuple-element.180.late, bf16[512,128]{1,0:T(8,128)(2,1)S(1)} %get-tuple-element.181.rows, bf16[128,128]{1,0:T(8,128)(2,1)} %get-tuple-element.182.refs_0_, bf16[128,128]{1,0:T(8,128)(2,1)} %copy-done.21, ...), custom_call_target="tpu_custom_call" | custom-call | tf_op jit(solution)/shard_map/mix/pallas_call | solution.py:413
  76.9 9.8 %all-to-all-start.2 = ((bf16[32,16,2048]{2,1,0:T(8,128)(2,1)}), bf16[32,16,2048]{2,1,0:T(8,128)(2,1)S(1)}, u32[]{:S(2)}, u32[]{:S(2)}) async-start(bf16[32,16,2048]{2,1,0:T(8,128)(2,1)} %mix.1), calls=%async_computation.2 | async-start | bytes 4194304 | tf_op jit(solution)/shard_map/all_to_all | solution.py:422
  86.7 53.0 %conditional.5 = (bf16[16,16,256]{2,1,0:T(8,128)(2,1)S(1)}, bf16[16,16,256]{2,1,0:T(8,128)(2,1)}, bf16[16,16,256]{2,1,0:T(8,128)(2,1)}, bf16[16,16,256]{2,1,0:T(8,128)(2,1)}) conditional(s32[]{:T(128)} %convert_element_type.2, () %tuple.53, (bf16[8,128,128]{2,1,0:T(8,128)(2,1)S(1)}, s32[2]{0:T(128)S(1)}, s32[512]{0:T(512)S(1)}) %tuple.68), branch_computations={%region_5.6_spmd, %region_6.7_spmd} | conditional | bytes 13894464 | solution.py:459
  89.1 2.7 %collective-permute-start.12 = (bf16[8,80,128]{2,1,0:T(8,128)(2,1)}, bf16[8,80,128]{2,1,0:T(8,128)(2,1)S(1)}, u32[]{:S(2)}, u32[]{:S(2)}) collective-permute-start(bf16[8,80,128]{2,1,0:T(8,128)(2,1)} %get-tuple-element.123), channel_id=1, source_target_pairs={{0,2},{1,3},{2,0},{3,1},{4,6},{5,7},{6,4},{7,5},{8,10},{9,11},{10,... | collective-permute-start | bytes 491528 | tf_op jit(solution)/shard_map/cond/branch_1_fun/ppermute | solution.py:48
  93.2 7.7 %collective-permute-done.11.refs_1_ = bf16[8,80,128]{2,1,0:T(8,128)(2,1)S(1)} collective-permute-done((bf16[8,80,128]{2,1,0:T(8,128)(2,1)}, bf16[8,80,128]{2,1,0:T(8,128)(2,1)S(1)}, u32[]{:S(2)}, u32[]{:S(2)}) %collective-permute-start.11) | collective-permute-done | bytes 163872 | tf_op jit(solution)/shard_map/cond/branch_1_fun/ppermute | solution.py:48
  100.9 10.3 %collective-permute-done.12.refs_2_ = bf16[8,80,128]{2,1,0:T(8,128)(2,1)S(1)} collective-permute-done((bf16[8,80,128]{2,1,0:T(8,128)(2,1)}, bf16[8,80,128]{2,1,0:T(8,128)(2,1)S(1)}, u32[]{:S(2)}, u32[]{:S(2)}) %collective-permute-start.12) | collective-permute-done | bytes 163872 | tf_op jit(solution)/shard_map/cond/branch_1_fun/ppermute | solution.py:48
  116.7 3.3 %collective-permute-done.20.refs_11_ = bf16[4,8,16,128]{3,2,1,0:T(8,128)(2,1)S(1)} collective-permute-done((bf16[4,8,16,128]{3,2,1,0:T(8,128)(2,1)}, bf16[4,8,16,128]{3,2,1,0:T(8,128)(2,1)S(1)}, u32[]{:S(2)}, u32[]{:S(2)}) %collective-permute-start.20) | collective-permute-done | bytes 131104 | tf_op jit(solution)/shard_map/cond/branch_1_fun/ppermute | solution.py:38
  120.0 3.5 %collective-permute-done.19.refs_10_ = bf16[4,8,16,128]{3,2,1,0:T(8,128)(2,1)S(1)} collective-permute-done((bf16[4,8,16,128]{3,2,1,0:T(8,128)(2,1)}, bf16[4,8,16,128]{3,2,1,0:T(8,128)(2,1)S(1)}, u32[]{:S(2)}, u32[]{:S(2)}) %collective-permute-start.19) | collective-permute-done | bytes 131104 | tf_op jit(solution)/shard_map/cond/branch_1_fun/ppermute | solution.py:38
  123.4 2.9 %collective-permute-done.18.refs_9_ = bf16[4,8,16,128]{3,2,1,0:T(8,128)(2,1)S(1)} collective-permute-done((bf16[4,8,16,128]{3,2,1,0:T(8,128)(2,1)}, bf16[4,8,16,128]{3,2,1,0:T(8,128)(2,1)S(1)}, u32[]{:S(2)}, u32[]{:S(2)}) %collective-permute-start.18) | collective-permute-done | bytes 131104 | tf_op jit(solution)/shard_map/cond/branch_1_fun/ppermute | solution.py:38
  127.2 3.7 %deltas.1 = (bf16[16,16,256]{2,1,0:T(8,128)(2,1)S(1)}, bf16[16,16,256]{2,1,0:T(8,128)(2,1)}, bf16[16,16,256]{2,1,0:T(8,128)(2,1)}, bf16[16,16,256]{2,1,0:T(8,128)(2,1)}) custom-call(s32[2]{0:T(128)S(1)} %get-tuple-element.118.ids, s32[512]{0:T(512)S(1)} %get-tuple-element.119.table, bf16[8,80,128]{2,1,0:T(8,128)(2,1)} %get-tuple-element.121.refs_0_, ...), custom_call_target="tpu_custom_call" | custom-call | tf_op jit(solution)/shard_map/cond/branch_1_fun/deltas/pallas_call | solution.py:444
  133.0 3.2 %collective-permute-done.21 = bf16[16,16,256]{2,1,0:T(8,128)(2,1)} collective-permute-done((bf16[16,16,256]{2,1,0:T(8,128)(2,1)}, bf16[16,16,256]{2,1,0:T(8,128)(2,1)}, u32[]{:S(2)}, u32[]{:S(2)}) %collective-permute-start.21) | collective-permute-done | bytes 131104 | tf_op jit(solution)/shard_map/cond/branch_1_fun/ppermute | solution.py:38
  141.1 3.4 %merge.1 = bf16[16,16,3072]{2,1,0:T(8,128)(2,1)} custom-call(s32[2]{0:T(128)S(1)} %pad_add_fusion.ids, s32[512]{0:T(512)S(1)} %copy-done.25, bf16[32,16,1024]{2,1,0:T(8,128)(2,1)} %copy-done.1, bf16[32,16,2048]{2,1,0:T(8,128)(2,1)} %copy-done, bf16[16,16,256]{2,1,0:T(8,128)(2,1)S(1)} %get-tuple-element.186.refs_0_, ...), custom_call_target="tpu_custom_call" | custom-call | tf_op jit(solution)/shard_map/merge/pallas_call | solution.py:466
  (114 shorter events, 38.6 us)
Async XLA Ops:
  3.2 10.8 %collective-permute-start = (bf16[704,128]{1,0:T(8,128)(2,1)}, bf16[704,128]{1,0:T(8,128)(2,1)}, u32[]{:S(2)}, u32[]{:S(2)}) collective-permute-start(bf16[704,128]{1,0:T(8,128)(2,1)} %pack.1), channel_id=1, source_target_pairs={{0,192},{32,224},{64,0},{96,32},{128,64},{160,96},{192,128},{224,1... | collective-permute-start | bytes 540680 | tf_op jit(solution)/shard_map/cond/branch_1_fun/ppermute | solution.py:38
  6.0 9.3 %collective-permute-start.4 = (bf16[704,128]{1,0:T(8,128)(2,1)}, bf16[704,128]{1,0:T(8,128)(2,1)}, u32[]{:S(2)}, u32[]{:S(2)}) collective-permute-start(bf16[704,128]{1,0:T(8,128)(2,1)} %pack.1), channel_id=1, source_target_pairs={{0,128},{32,160},{64,192},{96,224},{128,0},{160,32},{192,64},{224,... | collective-permute-start | bytes 540680 | tf_op jit(solution)/shard_map/cond/branch_1_fun/ppermute | solution.py:38
  6.8 10.9 %collective-permute-start.2 = (bf16[704,128]{1,0:T(8,128)(2,1)}, bf16[704,128]{1,0:T(8,128)(2,1)}, u32[]{:S(2)}, u32[]{:S(2)}) collective-permute-start(bf16[704,128]{1,0:T(8,128)(2,1)} %pack.1), channel_id=1, source_target_pairs={{0,64},{32,96},{64,128},{96,160},{128,192},{160,224},{192,0},{224,... | collective-permute-start | bytes 540680 | tf_op jit(solution)/shard_map/cond/branch_1_fun/ppermute | solution.py:38
  7.7 10.5 %collective-permute-start.1 = (bf16[704,128]{1,0:T(8,128)(2,1)}, bf16[704,128]{1,0:T(8,128)(2,1)}, u32[]{:S(2)}, u32[]{:S(2)}) collective-permute-start(bf16[704,128]{1,0:T(8,128)(2,1)} %pack.1), channel_id=1, source_target_pairs={{0,32},{32,0},{64,96},{96,64},{128,160},{160,128},{192,224},{224,1... | collective-permute-start | bytes 540680 | tf_op jit(solution)/shard_map/cond/branch_1_fun/ppermute | solution.py:44
  19.7 36.4 %all-to-all-start = ((bf16[32,16,1024]{2,1,0:T(8,128)(2,1)}), bf16[32,16,1024]{2,1,0:T(8,128)(2,1)S(1)}, u32[]{:S(2)}, u32[]{:S(2)}) async-start(bf16[32,16,1024]{2,1,0:T(8,128)(2,1)} %get-tuple-element.178), calls=%async_computation | async-start | bytes 2097152 | tf_op jit(solution)/shard_map/all_to_all | solution.py:354
  40.2 11.9 %collective-permute-start.8 = (bf16[704,128]{1,0:T(8,128)(2,1)}, bf16[704,128]{1,0:T(8,128)(2,1)S(1)}, u32[]{:S(2)}, u32[]{:S(2)}) collective-permute-start(bf16[704,128]{1,0:T(8,128)(2,1)} %get-tuple-element.100), channel_id=1, source_target_pairs={{0,64},{32,96},{64,128},{96,160},{128,192},{160,224},{192,0},{224,... | collective-permute-start | bytes 540680 | tf_op jit(solution)/shard_map/cond/branch_1_fun/ppermute | solution.py:38
  40.2 11.9 %collective-permute-start.9 = (bf16[704,128]{1,0:T(8,128)(2,1)}, bf16[704,128]{1,0:T(8,128)(2,1)S(1)}, u32[]{:S(2)}, u32[]{:S(2)}) collective-permute-start(bf16[704,128]{1,0:T(8,128)(2,1)} %get-tuple-element.101), channel_id=1, source_target_pairs={{0,128},{32,160},{64,192},{96,224},{128,0},{160,32},{192,64},{224,... | collective-permute-start | bytes 540680 | tf_op jit(solution)/shard_map/cond/branch_1_fun/ppermute | solution.py:38
  42.3 10.4 %collective-permute-start.10 = (bf16[704,128]{1,0:T(8,128)(2,1)}, bf16[704,128]{1,0:T(8,128)(2,1)S(1)}, u32[]{:S(2)}, u32[]{:S(2)}) collective-permute-start(bf16[704,128]{1,0:T(8,128)(2,1)} %get-tuple-element.102), channel_id=1, source_target_pairs={{0,192},{32,224},{64,0},{96,32},{128,64},{160,96},{192,128},{224,1... | collective-permute-start | bytes 540680 | tf_op jit(solution)/shard_map/cond/branch_1_fun/ppermute | solution.py:38
  56.1 20.8 %all-to-all-start.1 = ((bf16[8,128,128]{2,1,0:T(8,128)(2,1)}), bf16[8,128,128]{2,1,0:T(8,128)(2,1)S(1)}, u32[]{:S(2)}, u32[]{:S(2)}) async-start(bf16[8,128,128]{2,1,0:T(8,128)(2,1)} %get-tuple-element.183), calls=%async_computation.1 | async-start | bytes 524288 | tf_op jit(solution)/shard_map/all_to_all | solution.py:404
  65.7 5.7 %collective-permute-start.27 = (bf16[128,128]{1,0:T(8,128)(2,1)}, bf16[128,128]{1,0:T(8,128)(2,1)S(1)}, u32[]{:S(2)}, u32[]{:S(2)}) collective-permute-start(bf16[128,128]{1,0:T(8,128)(2,1)} %get-tuple-element.182.refs_0_), channel_id=1, source_target_pairs={{0,128},{32,160},{64,192},{96,224},{128,0},{160,32},{192,64},{224,... | collective-permute-start | bytes 98312 | tf_op jit(solution)/shard_map/ppermute | solution.py:38
  65.7 5.7 %collective-permute-start.25 = (bf16[128,128]{1,0:T(8,128)(2,1)}, bf16[128,128]{1,0:T(8,128)(2,1)S(1)}, u32[]{:S(2)}, u32[]{:S(2)}) collective-permute-start(bf16[128,128]{1,0:T(8,128)(2,1)} %get-tuple-element.182.refs_0_), channel_id=1, source_target_pairs={{0,64},{32,96},{64,128},{96,160},{128,192},{160,224},{192,0},{224,... | collective-permute-start | bytes 98312 | tf_op jit(solution)/shard_map/ppermute | solution.py:38
  76.9 62.8 %all-to-all-start.2 = ((bf16[32,16,2048]{2,1,0:T(8,128)(2,1)}), bf16[32,16,2048]{2,1,0:T(8,128)(2,1)S(1)}, u32[]{:S(2)}, u32[]{:S(2)}) async-start(bf16[32,16,2048]{2,1,0:T(8,128)(2,1)} %mix.1), calls=%async_computation.2 | async-start | bytes 4194304 | tf_op jit(solution)/shard_map/all_to_all | solution.py:422
  87.6 13.3 %collective-permute-start.11 = (bf16[8,80,128]{2,1,0:T(8,128)(2,1)}, bf16[8,80,128]{2,1,0:T(8,128)(2,1)S(1)}, u32[]{:S(2)}, u32[]{:S(2)}) collective-permute-start(bf16[8,80,128]{2,1,0:T(8,128)(2,1)} %get-tuple-element.122), channel_id=1, source_target_pairs={{0,1},{1,2},{2,3},{3,0},{4,5},{5,6},{6,7},{7,4},{8,9},{9,10},{10,1... | collective-permute-start | bytes 491528 | tf_op jit(solution)/shard_map/cond/branch_1_fun/ppermute | solution.py:48
  89.1 22.1 %collective-permute-start.12 = (bf16[8,80,128]{2,1,0:T(8,128)(2,1)}, bf16[8,80,128]{2,1,0:T(8,128)(2,1)S(1)}, u32[]{:S(2)}, u32[]{:S(2)}) collective-permute-start(bf16[8,80,128]{2,1,0:T(8,128)(2,1)} %get-tuple-element.123), channel_id=1, source_target_pairs={{0,2},{1,3},{2,0},{3,1},{4,6},{5,7},{6,4},{7,5},{8,10},{9,11},{10,... | collective-permute-start | bytes 491528 | tf_op jit(solution)/shard_map/cond/branch_1_fun/ppermute | solution.py:48
  91.8 19.5 %collective-permute-start.13 = (bf16[8,80,128]{2,1,0:T(8,128)(2,1)}, bf16[8,80,128]{2,1,0:T(8,128)(2,1)S(1)}, u32[]{:S(2)}, u32[]{:S(2)}) collective-permute-start(bf16[8,80,128]{2,1,0:T(8,128)(2,1)} %get-tuple-element.124), channel_id=1, source_target_pairs={{0,3},{1,0},{2,1},{3,2},{4,7},{5,4},{6,5},{7,6},{8,11},{9,8},{10,9... | collective-permute-start | bytes 491528 | tf_op jit(solution)/shard_map/cond/branch_1_fun/ppermute | solution.py:48
  93.2 22.1 %collective-permute-start.14 = (bf16[8,80,128]{2,1,0:T(8,128)(2,1)}, bf16[8,80,128]{2,1,0:T(8,128)(2,1)S(1)}, u32[]{:S(2)}, u32[]{:S(2)}) collective-permute-start(bf16[8,80,128]{2,1,0:T(8,128)(2,1)} %get-tuple-element.121.refs_0_), channel_id=1, source_target_pairs={{0,32},{32,0},{64,96},{96,64},{128,160},{160,128},{192,224},{224,1... | collective-permute-start | bytes 491528 | tf_op jit(solution)/shard_map/cond/branch_1_fun/ppermute | solution.py:44
  114.4 5.6 %collective-permute-start.20 = (bf16[4,8,16,128]{3,2,1,0:T(8,128)(2,1)}, bf16[4,8,16,128]{3,2,1,0:T(8,128)(2,1)S(1)}, u32[]{:S(2)}, u32[]{:S(2)}) collective-permute-start(bf16[4,8,16,128]{3,2,1,0:T(8,128)(2,1)} %rows.1.refs_8_), channel_id=1, source_target_pairs={{0,192},{32,224},{64,0},{96,32},{128,64},{160,96},{192,128},{224,1... | collective-permute-start | bytes 393224 | tf_op jit(solution)/shard_map/cond/branch_1_fun/ppermute | solution.py:38
  114.8 11.5 %collective-permute-start.15 = (bf16[8,80,128]{2,1,0:T(8,128)(2,1)}, bf16[8,80,128]{2,1,0:T(8,128)(2,1)S(1)}, u32[]{:S(2)}, u32[]{:S(2)}) collective-permute-start(bf16[8,80,128]{2,1,0:T(8,128)(2,1)} %copy-done.3), channel_id=1, source_target_pairs={{0,32},{32,0},{64,96},{96,64},{128,160},{160,128},{192,224},{224,1... | collective-permute-start | bytes 491528 | tf_op jit(solution)/shard_map/cond/branch_1_fun/ppermute | solution.py:44
  114.8 11.5 %collective-permute-start.16 = (bf16[8,80,128]{2,1,0:T(8,128)(2,1)}, bf16[8,80,128]{2,1,0:T(8,128)(2,1)S(1)}, u32[]{:S(2)}, u32[]{:S(2)}) collective-permute-start(bf16[8,80,128]{2,1,0:T(8,128)(2,1)} %copy-done.4), channel_id=1, source_target_pairs={{0,32},{32,0},{64,96},{96,64},{128,160},{160,128},{192,224},{224,1... | collective-permute-start | bytes 491528 | tf_op jit(solution)/shard_map/cond/branch_1_fun/ppermute | solution.py:44
  115.3 11.1 %collective-permute-start.17 = (bf16[8,80,128]{2,1,0:T(8,128)(2,1)}, bf16[8,80,128]{2,1,0:T(8,128)(2,1)S(1)}, u32[]{:S(2)}, u32[]{:S(2)}) collective-permute-start(bf16[8,80,128]{2,1,0:T(8,128)(2,1)} %copy-done.5), channel_id=1, source_target_pairs={{0,32},{32,0},{64,96},{96,64},{128,160},{160,128},{192,224},{224,1... | collective-permute-start | bytes 491528 | tf_op jit(solution)/shard_map/cond/branch_1_fun/ppermute | solution.py:44
  115.3 8.1 %collective-permute-start.19 = (bf16[4,8,16,128]{3,2,1,0:T(8,128)(2,1)}, bf16[4,8,16,128]{3,2,1,0:T(8,128)(2,1)S(1)}, u32[]{:S(2)}, u32[]{:S(2)}) collective-permute-start(bf16[4,8,16,128]{3,2,1,0:T(8,128)(2,1)} %rows.1.refs_8_), channel_id=1, source_target_pairs={{0,128},{32,160},{64,192},{96,224},{128,0},{160,32},{192,64},{224,... | collective-permute-start | bytes 393224 | tf_op jit(solution)/shard_map/cond/branch_1_fun/ppermute | solution.py:38
  120.0 6.4 %collective-permute-start.18 = (bf16[4,8,16,128]{3,2,1,0:T(8,128)(2,1)}, bf16[4,8,16,128]{3,2,1,0:T(8,128)(2,1)S(1)}, u32[]{:S(2)}, u32[]{:S(2)}) collective-permute-start(bf16[4,8,16,128]{3,2,1,0:T(8,128)(2,1)} %rows.1.refs_8_), channel_id=1, source_target_pairs={{0,64},{32,96},{64,128},{96,160},{128,192},{160,224},{192,0},{224,... | collective-permute-start | bytes 393224 | tf_op jit(solution)/shard_map/cond/branch_1_fun/ppermute | solution.py:38
  130.9 7.5 %collective-permute-start.22 = (bf16[16,16,256]{2,1,0:T(8,128)(2,1)}, bf16[16,16,256]{2,1,0:T(8,128)(2,1)}, u32[]{:S(2)}, u32[]{:S(2)}) collective-permute-start(bf16[16,16,256]{2,1,0:T(8,128)(2,1)} %get-tuple-element.127), channel_id=1, source_target_pairs={{0,128},{32,160},{64,192},{96,224},{128,0},{160,32},{192,64},{224,... | collective-permute-start | bytes 393224 | tf_op jit(solution)/shard_map/cond/branch_1_fun/ppermute | solution.py:38
  132.2 7.5 %collective-permute-start.23 = (bf16[16,16,256]{2,1,0:T(8,128)(2,1)}, bf16[16,16,256]{2,1,0:T(8,128)(2,1)}, u32[]{:S(2)}, u32[]{:S(2)}) collective-permute-start(bf16[16,16,256]{2,1,0:T(8,128)(2,1)} %get-tuple-element.128), channel_id=1, source_target_pairs={{0,64},{32,96},{64,128},{96,160},{128,192},{160,224},{192,0},{224,... | collective-permute-start | bytes 393224 | tf_op jit(solution)/shard_map/cond/branch_1_fun/ppermute | solution.py:38
  (37 other events, 179.1 us)

commit v3 on v2

--- a/solution.py
+++ b/solution.py
@@ -1,3 +1,5 @@
+import functools
+
 import jax
 import jax.numpy as jnp
 from jax import lax
@@ -10,6 +12,7 @@
 TILES = 32
 SLOTS = 16
 EARLY = 1
+LONG = 10**12
 Z, Y, DP = 8, 4, 8
 X = 4
 
@@ -63,6 +66,7 @@
 
 
 PARAMS = pltpu.CompilerParams(vmem_limit_bytes=60 * 1024 * 1024)
+HEAVY = pl.CostEstimate(flops=LONG, bytes_accessed=LONG // 100, transcendentals=0)
 
 
 def gradient_kernel(ids, counts, x, g, *refs):
@@ -174,7 +178,7 @@
             send[dz, first : first + TILE_ROWS, :] = rows[pl.ds(start, TILE_ROWS), :]
 
 
-def tiles_kernel(pick, frozen, early, late, whole, sem):
+def tiles_kernel(first, pick, frozen, out, whole, sem):
     copies = []
     for owner in range(Z * Y):
         rows = pl.ds(pl.multiple_of(pick[owner] * TILE_ROWS, TILE_ROWS), TILE_ROWS)
@@ -182,13 +186,28 @@
             pltpu.make_async_copy(frozen.at[rows, :], whole.at[owner], sem.at[owner])
         )
         copies[owner].start()
-    cols, one, two = whole.shape[2] // DP, early.shape[2] // DP, late.shape[2] // DP
+    cols, part = whole.shape[2] // DP, out.shape[2] // DP
     for owner in range(Z * Y):
         copies[owner].wait()
         for j in range(DP):
-            tile = whole[owner, :, j * cols : (j + 1) * cols]
-            early[owner, :, j * one : (j + 1) * one] = tile[:, :one]
-            late[owner, :, j * two : (j + 1) * two] = tile[:, one:]
+            start = j * cols + first
+            out[owner, :, j * part : (j + 1) * part] = whole[owner, :, start : start + part]
+
+
+def choose_tiles(first, cols, pick, frozen):
+    shape = (Z * Y, TILE_ROWS, DP * cols)
+    return pl.pallas_call(
+        functools.partial(tiles_kernel, first),
+        out_shape=jax.ShapeDtypeStruct(shape, BF16),
+        in_specs=[smem(), anywhere()],
+        out_specs=vmem(),
+        scratch_shapes=[
+            pltpu.VMEM((Z * Y, TILE_ROWS, frozen.shape[1]), BF16),
+            pltpu.SemaphoreType.DMA((Z * Y,)),
+        ],
+        compiler_params=PARAMS,
+        name="tiles",
+    )(pick, frozen)
 
 
 def mix_kernel(ids, late, rows, *refs):
@@ -215,13 +234,6 @@
         out[:, b_rows:, :] = arrived[:, first : first + TILE_ROWS, :]
 
 
-def rows_kernel(*refs):
-    parts, out = refs[:Y], refs[Y]
-    b_rows = parts[0].shape[1] - TILE_ROWS
-    for dy, part in enumerate(parts):
-        out[dy] = part[:, b_rows:, :]
-
-
 def slot_of(ids, table, s):
     source = table[ids[1] * SLOTS + s] // TILES
     dz = source // Y
@@ -229,58 +241,45 @@
     return source, dz, dy
 
 
-def delta_kernel(ids, table, *refs):
-    ups, others, downs = refs[:Y], refs[Y : 2 * Y], refs[2 * Y : 2 * Y + X]
-    outs, (own, other, sem) = refs[2 * Y + X : 2 * Y + 2 * X], refs[2 * Y + 2 * X :]
-    n_tiles = own.shape[1] // LOW_RANK
-    cols = n_tiles * 128
+def select_kernel(ids, table, *refs):
+    parts, ups, downs = refs[:Y], refs[Y], refs[Y + 1]
+    b_rows = ups.shape[1]
+    for s in range(SLOTS):
+        _, z, dy = slot_of(ids, table, s)
+        for i in range(Y):
+
+            @pl.when(dy == i)
+            def _(s=s, i=i, z=z):
+                ups[s] = parts[i][z, :b_rows, :]
+                downs[s] = parts[i][z, b_rows:, :]
+
+
+def early_kernel(ids, table, early, downs, *refs):
+    ups, out = refs[:DP], refs[DP]
     chip, core = ids[0] // 2, lax.rem(ids[0], 2)
-    up = pl.ds(0, own.shape[1])
-    places = []
-    for s in range(SLOTS):
-        _, dz, dy = slot_of(ids, table, s)
-        places.append((dy, dz))
-        for i in range(Y):
-
-            @pl.when(dy == i)
-            def _(s=s, i=i, dz=dz):
-                pltpu.make_async_copy(ups[i].at[dz, up], own.at[s], sem.at[0, s]).start()
-                pltpu.make_async_copy(others[i].at[dz, up], other.at[s], sem.at[1, s]).start()
-
-    for s in range(SLOTS):
-        pltpu.make_async_copy(ups[0].at[0, up], own.at[s], sem.at[0, s]).wait()
-        pltpu.make_async_copy(others[0].at[0, up], other.at[s], sem.at[1, s]).wait()
-    is_gate = chip < X // 2
-    spans = [pl.ds(pl.multiple_of(c * cols, 128), cols) for c in (core, 1 - core)]
-    for s in range(SLOTS):
-        left = jnp.concatenate([downs[k][places[s]] for k in range(X)], axis=0)
-        left = jnp.where(is_gate, left[:, :LOW_RANK], left[:, LOW_RANK:])
-        for ref, span in zip((own, other), spans):
-            right = jnp.concatenate(
-                [ref[s, t * LOW_RANK : (t + 1) * LOW_RANK, :] for t in range(n_tiles)], axis=1
-            )
-            delta = adapter_scale * jnp.dot(left, right, preferred_element_type=F32)
-            delta = delta.astype(BF16)
-            for k in range(X):
-                outs[k][s, :, span] = delta[k * TILE_ROWS : (k + 1) * TILE_ROWS]
-
-
-def merge_kernel(ids, table, early, late, *refs):
-    deltas, out = refs[:X], refs[X]
-    chip = ids[0] // 2
+    sources = [slot_of(ids, table, s)[0] for s in range(SLOTS)]
+    for i in range(DP):
+        k, c = i // 2, i % 2
+        j = 2 * lax.rem(chip + X - k, X) + (1 - core if c else core)
+        is_gate = j < DP // 2
+        for s in range(SLOTS):
+            left = jnp.where(is_gate, downs[s, :, :LOW_RANK], downs[s, :, LOW_RANK:])
+            for t in range(EARLY):
+                right = ups[i][s, t * LOW_RANK : (t + 1) * LOW_RANK, :]
+                delta = adapter_scale * jnp.dot(left, right, preferred_element_type=F32)
+                span = pl.ds(pl.multiple_of((j * EARLY + t) * 128, 128), 128)
+                base = early[sources[s], :, span].astype(F32)
+                out[s, :, span] = (base + delta).astype(BF16)
+
+
+def merge_kernel(ids, table, early, late, out):
     one, two = early.shape[2] // DP, late.shape[2] // DP
     for s in range(SLOTS):
-        source = table[ids[1] * SLOTS + s] // TILES
-        for k in range(X):
-            for c in range(2):
-                j = 2 * lax.rem(chip + k, X) + c
-                span = pl.ds(pl.multiple_of(j * one, 128), one)
-                new = early[source, :, span].astype(F32)
-                new += deltas[k][s, :, c * one : (c + 1) * one].astype(F32)
-                start = pl.multiple_of(j * (one + two), 128)
-                out[s, :, pl.ds(start, one)] = new.astype(BF16)
+        source = slot_of(ids, table, s)[0]
         for j in range(DP):
-            start = j * (one + two) + one
+            start = j * (one + two)
+            out[s, :, start : start + one] = early[s, :, j * one : (j + 1) * one]
+            start += one
             out[s, :, start : start + two] = late[source, :, j * two : (j + 1) * two]
 
 
@@ -309,8 +308,6 @@
     shape_a, shape_b = jax.ShapeDtypeStruct(a.shape, F32), jax.ShapeDtypeStruct(b.shape, F32)
     shape_block = jax.ShapeDtypeStruct((a_rows + cols // 128 * LOW_RANK, 128), BF16)
 
-    table = placement_map.reshape(Z * Y, SLOTS)
-    pick = jnp.sum(jnp.where(table // TILES == expert, table % TILES, 0), axis=1)
     n_tiles = cols // 128
     sizes = [DP * EARLY * 128, DP * (n_tiles - EARLY) * 128]
     halves = [jax.ShapeDtypeStruct((Z * Y, TILE_ROWS, n), BF16) for n in sizes]
@@ -319,86 +316,62 @@
     def zeros(shapes):
         return lambda *_: tuple(jnp.zeros(s.shape, s.dtype) for s in shapes)
 
-    def begin(a, b, pick, frozen):
-        block = pl.pallas_call(
-            pack_kernel,
-            out_shape=shape_block,
-            in_specs=[vmem()] * 2,
-            out_specs=vmem(),
-            compiler_params=PARAMS,
-            name="pack",
-        )(a, b)
-        chips = [block] + [shift_x(block, k) for k in range(1, X)]
-        tiles = pl.pallas_call(
-            tiles_kernel,
-            out_shape=halves,
-            in_specs=[smem(), anywhere()],
-            out_specs=[vmem()] * 2,
-            scratch_shapes=[
-                pltpu.VMEM((Z * Y, TILE_ROWS, width), BF16),
-                pltpu.SemaphoreType.DMA((Z * Y,)),
-            ],
-            compiler_params=PARAMS,
-            cost_estimate=pl.CostEstimate(
-                flops=0, bytes_accessed=16 * Z * Y * TILE_ROWS * width, transcendentals=0
-            ),
-            name="tiles",
-        )(pick, frozen)
-        tiles, chips[-1] = lax.optimization_barrier((tiles, chips[-1]))
-        blocks = [b for mine in chips for b in (mine, swap_core(mine))]
-        return (*tiles, *blocks)
-
-    early_out, late_base, *blocks = lax.cond(
-        some, begin, zeros(halves + [shape_block] * DP), a, b, pick, frozen
-    )
+    block = pl.pallas_call(
+        pack_kernel,
+        out_shape=shape_block,
+        in_specs=[vmem()] * 2,
+        out_specs=vmem(),
+        compiler_params=PARAMS,
+        name="pack",
+    )(a, b)
+    chips = [block] + [shift_x(block, k) for k in range(1, X)]
+
+    table = placement_map.reshape(Z * Y, SLOTS)
+    pick = jnp.sum(jnp.where(table // TILES == expert, table % TILES, 0), axis=1)
+    early_out = choose_tiles(0, EARLY * 128, pick, frozen)
     early = lax.all_to_all(early_out, "expert", split_axis=0, concat_axis=0, tiled=True)
     rest = jax.ShapeDtypeStruct(((n_tiles - EARLY) * LOW_RANK, 128), BF16)
     rows = jax.ShapeDtypeStruct((Z * Y * TILE_ROWS, 128), BF16)
 
-    def update(x, g, a, a1, a2, b, b1, b2, ids, pick, counts, *blocks):
+    def gradients(x, g, ids, counts, *chips):
+        blocks = [b for mine in chips for b in (mine, swap_core(mine))]
         kept, given = pl.pallas_call(
             gradient_kernel,
-            out_shape=[jax.ShapeDtypeStruct((X,) + shape_block.shape, BF16)] * 2,
+            out_shape=[shape_blocks] * 2,
             in_specs=[smem()] * 2 + [vmem()] * (2 + DP),
             out_specs=[vmem()] * 2,
             compiler_params=PARAMS,
             name="gradients",
         )(ids, counts, x, g, *blocks)
-        taken = swap_core(given)
-        pairs = pl.pallas_call(
-            pair_kernel,
-            out_shape=[shape_block] * X,
-            in_specs=[vmem()] * 2,
-            out_specs=[vmem()] * X,
-            compiler_params=PARAMS,
-            name="pairs",
-        )(kept, taken)
-        sums = [pairs[0]] + [shift_x(pairs[k], k) for k in range(1, X)]
-
-        new_a, new_a1, new_a2, new_b, new_b1, new_b2, messages, b_rest, a_rows = pl.pallas_call(
-            adam_kernel,
-            out_shape=[shape_a] * 3 + [shape_b] * 3 + [message, rest, rows],
-            in_specs=[smem()] * 3 + [vmem()] * (X + 6),
-            out_specs=[vmem()] * 9,
-            scratch_shapes=[pltpu.VMEM(a.shape, BF16)],
-            compiler_params=PARAMS,
-            name="adam",
-        )(ids, pick, counts, *sums, a, a1, a2, b, b1, b2)
-        return (new_a, new_a1, new_a2, new_b, new_b1, new_b2, messages, b_rest, a_rows)
-
+        return kept, swap_core(given)
+
+    shape_blocks = jax.ShapeDtypeStruct((X,) + shape_block.shape, BF16)
+    kept, taken = lax.cond(
+        some, gradients, zeros([shape_blocks] * 2), x, g, ids, counts, *chips
+    )
+    pairs = pl.pallas_call(
+        pair_kernel,
+        out_shape=[shape_block] * X,
+        in_specs=[vmem()] * 2,
+        out_specs=[vmem()] * X,
+        compiler_params=PARAMS,
+        cost_estimate=HEAVY,
+        name="pairs",
+    )(kept, taken)
+    sums = [pairs[0]] + [shift_x(pairs[k], k) for k in range(1, X)]
+    late_base = choose_tiles(EARLY * 128, (n_tiles - EARLY) * 128, pick, frozen)
+    sums[-1], late_base = lax.optimization_barrier((sums[-1], late_base))
     b_rows = EARLY * LOW_RANK
     message = jax.ShapeDtypeStruct((Z, b_rows + Y * TILE_ROWS, 128), BF16)
-    part = jax.ShapeDtypeStruct((SLOTS, TILE_ROWS, 2 * EARLY * 128), BF16)
-
-    outs = lax.cond(
-        some,
-        update,
-        zeros([shape_a] * 3 + [shape_b] * 3 + [message, rest, rows]),
-        *(x, g, a, a1, a2, b, b1, b2, ids, pick, counts, *blocks),
-    )
-    new_a, new_a1, new_a2, new_b, new_b1, new_b2 = outs[:6]
-
-    messages, b_rest, a_rows = outs[6:]
+    new_a, new_a1, new_a2, new_b, new_b1, new_b2, messages, b_rest, a_rows = pl.pallas_call(
+        adam_kernel,
+        out_shape=[shape_a] * 3 + [shape_b] * 3 + [message, rest, rows],
+        in_specs=[smem()] * 3 + [vmem()] * (X + 6),
+        out_specs=[vmem()] * 9,
+        scratch_shapes=[pltpu.VMEM(a.shape, BF16)],
+        compiler_params=pltpu.CompilerParams(vmem_limit_bytes=12 * 1024 * 1024),
+        name="adam",
+    )(ids, pick, counts, *sums, a, a1, a2, b, b1, b2)
     chips = [b_rest] + [shift_x(b_rest, k) for k in range(1, X)]
     messages, early = lax.optimization_barrier((messages, early))
     arrived = lax.all_to_all(
@@ -409,19 +382,26 @@
         tiled=True,
         axis_index_groups=[[z * Y + y for z in range(Z)] for y in range(Y)],
     )
-    others = [b for mine in chips for b in (mine, swap_core(mine))]
+
+    def swap_all(*chips):
+        return tuple(b for mine in chips for b in (mine, swap_core(mine)))
+
+    others = lax.cond(some, swap_all, zeros([rest] * DP), *chips)
     mixed = pl.pallas_call(
         mix_kernel,
         out_shape=jax.ShapeDtypeStruct(late_base.shape, BF16),
         in_specs=[smem()] + [vmem()] * (2 + DP),
         out_specs=vmem(),
-        compiler_params=PARAMS,
+        compiler_params=pltpu.CompilerParams(vmem_limit_bytes=12 * 1024 * 1024),
+        cost_estimate=pl.CostEstimate(flops=4680000000, bytes_accessed=15600000, transcendentals=0),
         name="mix",
     )(ids, late_base, a_rows, *others)
     mixed, arrived = lax.optimization_barrier((mixed, arrived))
     late = lax.all_to_all(mixed, "expert", split_axis=0, concat_axis=0, tiled=True)
 
-    def spread(ids, placement_map, arrived):
+    served_early = jax.ShapeDtypeStruct((SLOTS, TILE_ROWS, sizes[0]), BF16)
+
+    def spread(ids, placement_map, early, arrived):
         parts = pl.pallas_call(
             stack_kernel,
             out_shape=[jax.ShapeDtypeStruct((Z, b_rows + TILE_ROWS, 128), BF16)] * Y,
@@ -430,47 +410,42 @@
             compiler_params=PARAMS,
             name="stack",
         )(arrived)
-        ups = [parts[0]] + [shift_y(parts[dy], dy) for dy in range(1, Y)]
-        rows = pl.pallas_call(
-            rows_kernel,
-            out_shape=jax.ShapeDtypeStruct((Y, Z, TILE_ROWS, 128), BF16),
-            in_specs=[vmem()] * Y,
+        parts = [parts[0]] + [shift_y(parts[dy], dy) for dy in range(1, Y)]
+        ups, downs = pl.pallas_call(
+            select_kernel,
+            out_shape=[
+                jax.ShapeDtypeStruct((SLOTS, b_rows, 128), BF16),
+                jax.ShapeDtypeStruct((SLOTS, TILE_ROWS, 128), BF16),
+            ],
+            in_specs=[smem()] * 2 + [vmem()] * Y,
+            out_specs=[vmem()] * 2,
+            compiler_params=PARAMS,
+            name="select",
+        )(ids, placement_map, *parts)
+        chips = [ups] + [shift_x(ups, k) for k in range(1, X)]
+        every = [b for mine in chips for b in (mine, swap_core(mine))]
+        return pl.pallas_call(
+            early_kernel,
+            out_shape=served_early,
+            in_specs=[smem()] * 2 + [vmem()] * (2 + DP),
             out_specs=vmem(),
             compiler_params=PARAMS,
-            name="rows",
-        )(*ups)
-        chips = [rows] + [shift_x(rows, k) for k in range(1, X)]
-        others = [swap_core(u) for u in ups]
-        deltas = pl.pallas_call(
-            delta_kernel,
-            out_shape=[part] * X,
-            in_specs=[smem()] * 2 + [anywhere()] * (2 * Y) + [vmem()] * X,
-            out_specs=[vmem()] * X,
-            scratch_shapes=[
-                pltpu.VMEM((SLOTS, b_rows, 128), BF16),
-                pltpu.VMEM((SLOTS, b_rows, 128), BF16),
-                pltpu.SemaphoreType.DMA((2, SLOTS)),
-            ],
-            compiler_params=PARAMS,
-            name="deltas",
-        )(ids, placement_map, *ups, *others, *chips)
-        return tuple([deltas[0]] + [shift_x(deltas[k], -k) for k in range(1, X)])
-
-    shifted = lax.cond(
-        some,
-        spread,
-        zeros([part] * X),
-        *(ids, placement_map, arrived),
-    )
+            name="early",
+        )(ids, placement_map, early, downs, *every)
+
+    def no_spread(*_):
+        return jnp.zeros(served_early.shape, BF16)
+
+    first = lax.cond(some, spread, no_spread, ids, placement_map, early, arrived)
 
     served = pl.pallas_call(
         merge_kernel,
         out_shape=jax.ShapeDtypeStruct((SLOTS, TILE_ROWS, width), BF16),
-        in_specs=[smem()] * 2 + [vmem()] * (2 + X),
+        in_specs=[smem()] * 2 + [vmem()] * 2,
         out_specs=vmem(),
-        compiler_params=PARAMS,
+        compiler_params=pltpu.CompilerParams(vmem_limit_bytes=12 * 1024 * 1024),
         name="merge",
-    )(ids, placement_map, early, late, *shifted)
+    )(ids, placement_map, first, late)
 
     return (
         new_a[None],

time: 145 us -> 133 us (0.917)
  the two profiles are of different devices: /device:TPU:128 before, /device:TPU:4 now
where the time goes in v3:
time: 133 us; the launch traced here: 132 us
  starting transfers between devices  46.7 us (35%)
  waiting for transfers between devices  46.3 us (35%)
  Pallas kernels  32.3 us (24%)
  local copies, waits for them, and re-layouts  4.33 us (3%)
    ppermute x12, starting transfers between devices, shift_x(): lax.ppermute(array, 'dp', [(i, (i // 2 + k) % X * 2 + i % 2) for i in ran...  16.8 us
    ppermute x3, waiting for transfers between devices, shift_y(): lax.ppermute(array, 'expert', [(i, i // Y * Y + (i % Y + k) % Y) for i in...  14.7 us
    ppermute x12, waiting for transfers between devices, shift_x(): lax.ppermute(array, 'dp', [(i, (i // 2 + k) % X * 2 + i % 2) for i in ran...  14.5 us
    pallas_call x2, Pallas kernels, choose_tiles(): pl.pallas_call(functools.partial(tiles_kernel, first), out_shape=jax.Shap...  12.5 us
    all_to_all x1, starting transfers between devices, per_device(): lax.all_to_all(early_out, 'expert', split_axis=0, concat_axis=0, tiled=True)  9.27 us
    all_to_all x1, starting transfers between devices, per_device(): lax.all_to_all(messages, 'expert', split_axis=0, concat_axis=0, tiled=Tru...  6.91 us
    all_to_all x1, waiting for transfers between devices, per_device(): lax.all_to_all(mixed, 'expert', split_axis=0, concat_axis=0, tiled=True)  6.44 us
    ppermute x3, starting transfers between devices, shift_y(): lax.ppermute(array, 'expert', [(i, i // Y * Y + (i % Y + k) % Y) for i in...  5.93 us
  transfers between devices with their start and end apart: 31, of which 18 were waited for; matrix products, arithmetic and copies ran while one was open for 2% of the time, Pallas kernels for 22%

profile of v3, /device:TPU:4, one launch (start us, length us, event | category | flops | bytes accessed | tf_op | source)
XLA Modules:
  0.0 131.9 jit_solution(8078111150863539972)
XLA Ops:
  2.2 2.7 %collective-permute-start.20 = (bf16[704,128]{1,0:T(8,128)(2,1)S(1)}, bf16[704,128]{1,0:T(8,128)(2,1)S(1)}, u32[]{:S(2)}, u32[]{:S(2)}) collective-permute-start(bf16[704,128]{1,0:T(8,128)(2,1)S(1)} %pack.1), channel_id=1, source_target_pairs={{0,128},{32,160},{64,192},{96,224},{128,0},{160,32},{192,64},{224,... | collective-permute-start | bytes 540680 | tf_op jit(solution)/shard_map/ppermute | solution.py:41
  8.0 6.1 %tiles.3 = bf16[32,16,1024]{2,1,0:T(8,128)(2,1)} custom-call(s32[32]{0:T(128)} %fusion.2.pick, bf16[512,3072]{1,0:T(8,128)(2,1)} %bitcast.29), custom_call_target="tpu_custom_call" | custom-call | tf_op jit(solution)/shard_map/tiles/pallas_call | solution.py:199
  14.1 9.3 %all-to-all-start = ((bf16[32,16,1024]{2,1,0:T(8,128)(2,1)}), bf16[32,16,1024]{2,1,0:T(8,128)(2,1)}, u32[]{:S(2)}, u32[]{:S(2)}) async-start(bf16[32,16,1024]{2,1,0:T(8,128)(2,1)} %tiles.3), calls=%async_computation | async-start | bytes 2097152 | tf_op jit(solution)/shard_map/all_to_all | solution.py:332
  24.0 10.1 %conditional.3 = (bf16[4,704,128]{2,1,0:T(8,128)(2,1)S(1)}, bf16[4,704,128]{2,1,0:T(8,128)(2,1)}) conditional(s32[]{:T(128)} %convert_element_type.2, () %tuple.33, (bf16[1,1,256,4096]{3,2,1,0:T(8,128)(2,1)S(1)}, bf16[1,1,256,3072]{3,2,1,0:T(8,128)(2,1)}, bf16[704,128]{1,0:T(8,128)(2,1)S(1)}, bf16[704,128]{1,0:T(8,128)(2,1)S(1)}, ...), branch_computations={%region_1.2_spmd, %region_2.3_spmd} | conditional | bytes 8651080 | solution.py:349
  27.0 4.6 %gradients.1 = (bf16[4,704,128]{2,1,0:T(8,128)(2,1)S(1)}, bf16[4,704,128]{2,1,0:T(8,128)(2,1)}) custom-call(s32[2]{0:T(128)} %get-tuple-element.37.ids, s32[8]{0:T(128)S(1)} %get-tuple-element.38.counts, bf16[256,4096]{1,0:T(8,128)(2,1)S(1)} %bitcast.31, bf16[256,3072]{1,0:T(8,128)(2,1)} %bitcast.32, bf16[704,128]{1,0:T(8,128)(2,1)S(1)} %get-tuple-element.41.refs_0_, ...), custom_call_target="tpu_custom_call" | custom-call | tf_op jit(solution)/shard_map/cond/branch_1_fun/gradients/pallas_call | solution.py:338
  31.9 2.3 %collective-permute-done.4 = bf16[4,704,128]{2,1,0:T(8,128)(2,1)} collective-permute-done((bf16[4,704,128]{2,1,0:T(8,128)(2,1)}, bf16[4,704,128]{2,1,0:T(8,128)(2,1)}, u32[]{:S(2)}, u32[]{:S(2)}) %collective-permute-start.4) | collective-permute-done | bytes 720928 | tf_op jit(solution)/shard_map/cond/branch_1_fun/ppermute | solution.py:47
  40.4 6.4 %tiles.2.late = bf16[32,16,2048]{2,1,0:T(8,128)(2,1)} custom-call(s32[32]{0:T(128)} %fusion.2.pick, bf16[512,3072]{1,0:T(8,128)(2,1)} %bitcast.30), custom_call_target="tpu_custom_call" | custom-call | tf_op jit(solution)/shard_map/tiles/pallas_call | solution.py:199
  46.8 2.1 %collective-permute-done.23.refs_2_ = bf16[704,128]{1,0:T(8,128)(2,1)S(1)} collective-permute-done((bf16[704,128]{1,0:T(8,128)(2,1)}, bf16[704,128]{1,0:T(8,128)(2,1)S(1)}, u32[]{:S(2)}, u32[]{:S(2)}) %collective-permute-start.23) | collective-permute-done | bytes 180256 | tf_op jit(solution)/shard_map/ppermute | solution.py:41
  51.7 2.6 %collective-permute-start.26 = (bf16[128,128]{1,0:T(8,128)(2,1)S(1)}, bf16[128,128]{1,0:T(8,128)(2,1)S(1)}, u32[]{:S(2)}, u32[]{:S(2)}) collective-permute-start(bf16[128,128]{1,0:T(8,128)(2,1)S(1)} %get-tuple-element.112), channel_id=1, source_target_pairs={{0,128},{32,160},{64,192},{96,224},{128,0},{160,32},{192,64},{224,... | collective-permute-start | bytes 98312 | tf_op jit(solution)/shard_map/ppermute | solution.py:41
  54.3 2.3 %collective-permute-start.25 = (bf16[128,128]{1,0:T(8,128)(2,1)S(1)}, bf16[128,128]{1,0:T(8,128)(2,1)S(1)}, u32[]{:S(2)}, u32[]{:S(2)}) collective-permute-start(bf16[128,128]{1,0:T(8,128)(2,1)S(1)} %get-tuple-element.112), channel_id=1, source_target_pairs={{0,64},{32,96},{64,128},{96,160},{128,192},{160,224},{192,0},{224,... | collective-permute-start | bytes 98312 | tf_op jit(solution)/shard_map/ppermute | solution.py:41
  56.6 6.9 %all-to-all-start.1 = ((bf16[8,128,128]{2,1,0:T(8,128)(2,1)}), bf16[8,128,128]{2,1,0:T(8,128)(2,1)S(1)}, u32[]{:S(2)}, u32[]{:S(2)}) async-start(bf16[8,128,128]{2,1,0:T(8,128)(2,1)} %get-tuple-element.122), calls=%async_computation.1 | async-start | bytes 524288 | tf_op jit(solution)/shard_map/all_to_all | solution.py:377
  63.5 2.1 %conditional.4 = (bf16[128,128]{1,0:T(8,128)(2,1)S(1)}, bf16[128,128]{1,0:T(8,128)(2,1)}, bf16[128,128]{1,0:T(8,128)(2,1)S(1)}, bf16[128,128]{1,0:T(8,128)(2,1)}...) conditional(s32[]{:T(128)} %convert_element_type.2, () %tuple.37, ...), branch_computations={%region_3.4_spmd, %region_4.5_spmd} | conditional | bytes 786656 | solution.py:389
  65.7 2.2 %mix.1 = bf16[32,16,2048]{2,1,0:T(8,128)(2,1)S(1)} custom-call(s32[2]{0:T(128)} %pad_add_fusion.ids, bf16[32,16,2048]{2,1,0:T(8,128)(2,1)S(1)} %copy-done, bf16[512,128]{1,0:T(8,128)(2,1)S(1)} %get-tuple-element.111.rows, bf16[128,128]{1,0:T(8,128)(2,1)S(1)} %get-tuple-element.113.refs_0_, bf16[128,128]{1,0:T(8,128)(2,1)} %get-tuple-element.114.refs_1_, ...), custom_call_target="tpu_custom_call" | custom-call | flops 4680000000 | bytes 15600000 | tf_op jit(solution)/shard_map/mix/pallas_call | solution.py:390
  69.2 4.8 %all-to-all-done.1 = bf16[8,128,128]{2,1,0:T(8,128)(2,1)S(1)} async-done(((bf16[8,128,128]{2,1,0:T(8,128)(2,1)}), bf16[8,128,128]{2,1,0:T(8,128)(2,1)S(1)}, u32[]{:S(2)}, u32[]{:S(2)}) %all-to-all-start.1) | async-done | bytes 262176 | tf_op jit(solution)/shard_map/all_to_all | solution.py:377
  74.0 5.3 %all-to-all-start.2 = ((bf16[32,16,2048]{2,1,0:T(8,128)(2,1)}), bf16[32,16,2048]{2,1,0:T(8,128)(2,1)S(1)}, u32[]{:S(2)}, u32[]{:S(2)}) async-start(bf16[32,16,2048]{2,1,0:T(8,128)(2,1)} %copy-done.1), calls=%async_computation.2 | async-start | bytes 4194304 | tf_op jit(solution)/shard_map/all_to_all | solution.py:400
  79.3 44.2 %conditional.5 = (bf16[16,16,1024]{2,1,0:T(8,128)(2,1)S(1)}) conditional(s32[]{:T(128)} %convert_element_type.2, () %tuple.36, (bf16[8,128,128]{2,1,0:T(8,128)(2,1)S(1)}, s32[2]{0:T(128)}, s32[512]{0:T(512)S(1)}, bf16[32,16,1024]{2,1,0:T(8,128)(2,1)}) %tuple.52), branch_computations={%region_5.6_spmd, %region_6.7_spmd} | conditional | bytes 18612912 | solution.py:439
  82.0 2.7 %collective-permute-start.10 = (bf16[8,80,128]{2,1,0:T(8,128)(2,1)}, bf16[8,80,128]{2,1,0:T(8,128)(2,1)S(1)}, u32[]{:S(2)}, u32[]{:S(2)}) collective-permute-start(bf16[8,80,128]{2,1,0:T(8,128)(2,1)} %get-tuple-element.57), channel_id=1, source_target_pairs={{0,2},{1,3},{2,0},{3,1},{4,6},{5,7},{6,4},{7,5},{8,10},{9,11},{10,... | collective-permute-start | bytes 491528 | tf_op jit(solution)/shard_map/cond/branch_1_fun/ppermute | solution.py:51
  86.2 4.1 %collective-permute-done.9.refs_1_ = bf16[8,80,128]{2,1,0:T(8,128)(2,1)S(1)} collective-permute-done((bf16[8,80,128]{2,1,0:T(8,128)(2,1)}, bf16[8,80,128]{2,1,0:T(8,128)(2,1)S(1)}, u32[]{:S(2)}, u32[]{:S(2)}) %collective-permute-start.9) | collective-permute-done | bytes 163872 | tf_op jit(solution)/shard_map/cond/branch_1_fun/ppermute | solution.py:51
  90.2 10.6 %collective-permute-done.10.refs_2_ = bf16[8,80,128]{2,1,0:T(8,128)(2,1)S(1)} collective-permute-done((bf16[8,80,128]{2,1,0:T(8,128)(2,1)}, bf16[8,80,128]{2,1,0:T(8,128)(2,1)S(1)}, u32[]{:S(2)}, u32[]{:S(2)}) %collective-permute-start.10) | collective-permute-done | bytes 163872 | tf_op jit(solution)/shard_map/cond/branch_1_fun/ppermute | solution.py:51
  101.6 2.5 %select.7 = (bf16[16,64,128]{2,1,0:T(8,128)(2,1)}, bf16[16,16,128]{2,1,0:T(8,128)(2,1)}) custom-call(s32[2]{0:T(128)} %get-tuple-element.51.ids, s32[512]{0:T(512)S(1)} %get-tuple-element.52.table, bf16[8,80,128]{2,1,0:T(8,128)(2,1)} %get-tuple-element.55.refs_0_, bf16[8,80,128]{2,1,0:T(8,128)(2,1)} %copy-done.22, bf16[8,80,128]{2,1,0:T(8,128)(2,1)} %copy-done.23, ...), custom_call_target="tpu_custom_call" | custom-call | tf_op jit(solution)/shard_map/cond/branch_1_fun/select/pallas_call | solution.py:414
  106.3 7.3 %collective-permute-done.17.refs_6_ = bf16[16,64,128]{2,1,0:T(8,128)(2,1)S(1)} collective-permute-done((bf16[16,64,128]{2,1,0:T(8,128)(2,1)}, bf16[16,64,128]{2,1,0:T(8,128)(2,1)S(1)}, u32[]{:S(2)}, u32[]{:S(2)}) %collective-permute-start.17) | collective-permute-done | bytes 262176 | tf_op jit(solution)/shard_map/cond/branch_1_fun/ppermute | solution.py:41
  115.1 3.5 %collective-permute-done.13.refs_2_ = bf16[16,64,128]{2,1,0:T(8,128)(2,1)S(1)} collective-permute-done((bf16[16,64,128]{2,1,0:T(8,128)(2,1)}, bf16[16,64,128]{2,1,0:T(8,128)(2,1)S(1)}, u32[]{:S(2)}, u32[]{:S(2)}) %collective-permute-start.13) | collective-permute-done | bytes 262176 | tf_op jit(solution)/shard_map/cond/branch_1_fun/ppermute | solution.py:41
  120.9 2.6 %early.1 = bf16[16,16,1024]{2,1,0:T(8,128)(2,1)S(1)} custom-call(s32[2]{0:T(128)} %get-tuple-element.51.ids, s32[512]{0:T(512)S(1)} %get-tuple-element.52.table, bf16[32,16,1024]{2,1,0:T(8,128)(2,1)} %get-tuple-element.53.early, bf16[16,16,128]{2,1,0:T(8,128)(2,1)} %get-tuple-element.59.downs, bf16[16,64,128]{2,1,0:T(8,128)(2,1)} %get-tuple-element.60.refs_0_, ...), custom_call_target="tpu_custom_call" | custom-call | tf_op jit(solution)/shard_map/cond/branch_1_fun/early/pallas_call | solution.py:427
  123.5 6.4 %all-to-all-done.2.late = bf16[32,16,2048]{2,1,0:T(8,128)(2,1)S(1)} async-done(((bf16[32,16,2048]{2,1,0:T(8,128)(2,1)}), bf16[32,16,2048]{2,1,0:T(8,128)(2,1)S(1)}, u32[]{:S(2)}, u32[]{:S(2)}) %all-to-all-start.2) | async-done | bytes 2097184 | tf_op jit(solution)/shard_map/all_to_all | solution.py:400
  (115 shorter events, 33.5 us)
Async XLA Ops:
  1.6 22.4 %collective-permute-start.21 = (bf16[704,128]{1,0:T(8,128)(2,1)S(1)}, bf16[704,128]{1,0:T(8,128)(2,1)S(1)}, u32[]{:S(2)}, u32[]{:S(2)}) collective-permute-start(bf16[704,128]{1,0:T(8,128)(2,1)S(1)} %pack.1), channel_id=1, source_target_pairs={{0,192},{32,224},{64,0},{96,32},{128,64},{160,96},{192,128},{224,1... | collective-permute-start | bytes 540680 | tf_op jit(solution)/shard_map/ppermute | solution.py:41
  2.2 21.8 %collective-permute-start.20 = (bf16[704,128]{1,0:T(8,128)(2,1)S(1)}, bf16[704,128]{1,0:T(8,128)(2,1)S(1)}, u32[]{:S(2)}, u32[]{:S(2)}) collective-permute-start(bf16[704,128]{1,0:T(8,128)(2,1)S(1)} %pack.1), channel_id=1, source_target_pairs={{0,128},{32,160},{64,192},{96,224},{128,0},{160,32},{192,64},{224,... | collective-permute-start | bytes 540680 | tf_op jit(solution)/shard_map/ppermute | solution.py:41
  5.0 19.0 %collective-permute-start.19 = (bf16[704,128]{1,0:T(8,128)(2,1)S(1)}, bf16[704,128]{1,0:T(8,128)(2,1)S(1)}, u32[]{:S(2)}, u32[]{:S(2)}) collective-permute-start(bf16[704,128]{1,0:T(8,128)(2,1)S(1)} %pack.1), channel_id=1, source_target_pairs={{0,64},{32,96},{64,128},{96,160},{128,192},{160,224},{192,0},{224,... | collective-permute-start | bytes 540680 | tf_op jit(solution)/shard_map/ppermute | solution.py:41
  14.1 42.5 %all-to-all-start = ((bf16[32,16,1024]{2,1,0:T(8,128)(2,1)}), bf16[32,16,1024]{2,1,0:T(8,128)(2,1)}, u32[]{:S(2)}, u32[]{:S(2)}) async-start(bf16[32,16,1024]{2,1,0:T(8,128)(2,1)} %tiles.3), calls=%async_computation | async-start | bytes 2097152 | tf_op jit(solution)/shard_map/all_to_all | solution.py:332
  24.2 1.7 %collective-permute-start.1 = (bf16[704,128]{1,0:T(8,128)(2,1)S(1)}, bf16[704,128]{1,0:T(8,128)(2,1)S(1)}, u32[]{:S(2)}, u32[]{:S(2)}) collective-permute-start(bf16[704,128]{1,0:T(8,128)(2,1)S(1)} %get-tuple-element.42.refs_2_), channel_id=1, source_target_pairs={{0,32},{32,0},{64,96},{96,64},{128,160},{160,128},{192,224},{224,1... | collective-permute-start | bytes 540680 | tf_op jit(solution)/shard_map/cond/branch_1_fun/ppermute | solution.py:47
  24.7 1.6 %collective-permute-start.3 = (bf16[704,128]{1,0:T(8,128)(2,1)S(1)}, bf16[704,128]{1,0:T(8,128)(2,1)S(1)}, u32[]{:S(2)}, u32[]{:S(2)}) collective-permute-start(bf16[704,128]{1,0:T(8,128)(2,1)S(1)} %get-tuple-element.44.refs_6_), channel_id=1, source_target_pairs={{0,32},{32,0},{64,96},{96,64},{128,160},{160,128},{192,224},{224,1... | collective-permute-start | bytes 540680 | tf_op jit(solution)/shard_map/cond/branch_1_fun/ppermute | solution.py:47
  31.6 2.5 %collective-permute-start.4 = (bf16[4,704,128]{2,1,0:T(8,128)(2,1)}, bf16[4,704,128]{2,1,0:T(8,128)(2,1)}, u32[]{:S(2)}, u32[]{:S(2)}) collective-permute-start(bf16[4,704,128]{2,1,0:T(8,128)(2,1)} %get-tuple-element.46), channel_id=1, source_target_pairs={{0,32},{32,0},{64,96},{96,64},{128,160},{160,128},{192,224},{224,1... | collective-permute-start | bytes 2162696 | tf_op jit(solution)/shard_map/cond/branch_1_fun/ppermute | solution.py:47
  36.1 10.7 %collective-permute-start.24 = (bf16[704,128]{1,0:T(8,128)(2,1)}, bf16[704,128]{1,0:T(8,128)(2,1)S(1)}, u32[]{:S(2)}, u32[]{:S(2)}) collective-permute-start(bf16[704,128]{1,0:T(8,128)(2,1)} %get-tuple-element.102), channel_id=1, source_target_pairs={{0,192},{32,224},{64,0},{96,32},{128,64},{160,96},{192,128},{224,1... | collective-permute-start | bytes 540680 | tf_op jit(solution)/shard_map/ppermute | solution.py:41
  38.2 8.7 %collective-permute-start.22 = (bf16[704,128]{1,0:T(8,128)(2,1)}, bf16[704,128]{1,0:T(8,128)(2,1)S(1)}, u32[]{:S(2)}, u32[]{:S(2)}) collective-permute-start(bf16[704,128]{1,0:T(8,128)(2,1)} %get-tuple-element.100), channel_id=1, source_target_pairs={{0,64},{32,96},{64,128},{96,160},{128,192},{160,224},{192,0},{224,... | collective-permute-start | bytes 540680 | tf_op jit(solution)/shard_map/ppermute | solution.py:41
  38.3 10.7 %collective-permute-start.23 = (bf16[704,128]{1,0:T(8,128)(2,1)}, bf16[704,128]{1,0:T(8,128)(2,1)S(1)}, u32[]{:S(2)}, u32[]{:S(2)}) collective-permute-start(bf16[704,128]{1,0:T(8,128)(2,1)} %get-tuple-element.101), channel_id=1, source_target_pairs={{0,128},{32,160},{64,192},{96,224},{128,0},{160,32},{192,64},{224,... | collective-permute-start | bytes 540680 | tf_op jit(solution)/shard_map/ppermute | solution.py:41
  51.0 12.5 %collective-permute-start.27 = (bf16[128,128]{1,0:T(8,128)(2,1)S(1)}, bf16[128,128]{1,0:T(8,128)(2,1)S(1)}, u32[]{:S(2)}, u32[]{:S(2)}) collective-permute-start(bf16[128,128]{1,0:T(8,128)(2,1)S(1)} %get-tuple-element.112), channel_id=1, source_target_pairs={{0,192},{32,224},{64,0},{96,32},{128,64},{160,96},{192,128},{224,1... | collective-permute-start | bytes 98312 | tf_op jit(solution)/shard_map/ppermute | solution.py:41
  51.7 11.8 %collective-permute-start.26 = (bf16[128,128]{1,0:T(8,128)(2,1)S(1)}, bf16[128,128]{1,0:T(8,128)(2,1)S(1)}, u32[]{:S(2)}, u32[]{:S(2)}) collective-permute-start(bf16[128,128]{1,0:T(8,128)(2,1)S(1)} %get-tuple-element.112), channel_id=1, source_target_pairs={{0,128},{32,160},{64,192},{96,224},{128,0},{160,32},{192,64},{224,... | collective-permute-start | bytes 98312 | tf_op jit(solution)/shard_map/ppermute | solution.py:41
  54.3 9.3 %collective-permute-start.25 = (bf16[128,128]{1,0:T(8,128)(2,1)S(1)}, bf16[128,128]{1,0:T(8,128)(2,1)S(1)}, u32[]{:S(2)}, u32[]{:S(2)}) collective-permute-start(bf16[128,128]{1,0:T(8,128)(2,1)S(1)} %get-tuple-element.112), channel_id=1, source_target_pairs={{0,64},{32,96},{64,128},{96,160},{128,192},{160,224},{192,0},{224,... | collective-permute-start | bytes 98312 | tf_op jit(solution)/shard_map/ppermute | solution.py:41
  56.6 17.4 %all-to-all-start.1 = ((bf16[8,128,128]{2,1,0:T(8,128)(2,1)}), bf16[8,128,128]{2,1,0:T(8,128)(2,1)S(1)}, u32[]{:S(2)}, u32[]{:S(2)}) async-start(bf16[8,128,128]{2,1,0:T(8,128)(2,1)} %get-tuple-element.122), calls=%async_computation.1 | async-start | bytes 524288 | tf_op jit(solution)/shard_map/all_to_all | solution.py:377
  74.0 56.0 %all-to-all-start.2 = ((bf16[32,16,2048]{2,1,0:T(8,128)(2,1)}), bf16[32,16,2048]{2,1,0:T(8,128)(2,1)S(1)}, u32[]{:S(2)}, u32[]{:S(2)}) async-start(bf16[32,16,2048]{2,1,0:T(8,128)(2,1)} %copy-done.1), calls=%async_computation.2 | async-start | bytes 4194304 | tf_op jit(solution)/shard_map/all_to_all | solution.py:400
  80.2 10.0 %collective-permute-start.9 = (bf16[8,80,128]{2,1,0:T(8,128)(2,1)}, bf16[8,80,128]{2,1,0:T(8,128)(2,1)S(1)}, u32[]{:S(2)}, u32[]{:S(2)}) collective-permute-start(bf16[8,80,128]{2,1,0:T(8,128)(2,1)} %get-tuple-element.56), channel_id=1, source_target_pairs={{0,1},{1,2},{2,3},{3,0},{4,5},{5,6},{6,7},{7,4},{8,9},{9,10},{10,1... | collective-permute-start | bytes 491528 | tf_op jit(solution)/shard_map/cond/branch_1_fun/ppermute | solution.py:51
  82.0 18.9 %collective-permute-start.10 = (bf16[8,80,128]{2,1,0:T(8,128)(2,1)}, bf16[8,80,128]{2,1,0:T(8,128)(2,1)S(1)}, u32[]{:S(2)}, u32[]{:S(2)}) collective-permute-start(bf16[8,80,128]{2,1,0:T(8,128)(2,1)} %get-tuple-element.57), channel_id=1, source_target_pairs={{0,2},{1,3},{2,0},{3,1},{4,6},{5,7},{6,4},{7,5},{8,10},{9,11},{10,... | collective-permute-start | bytes 491528 | tf_op jit(solution)/shard_map/cond/branch_1_fun/ppermute | solution.py:51
  84.7 16.2 %collective-permute-start.11 = (bf16[8,80,128]{2,1,0:T(8,128)(2,1)}, bf16[8,80,128]{2,1,0:T(8,128)(2,1)S(1)}, u32[]{:S(2)}, u32[]{:S(2)}) collective-permute-start(bf16[8,80,128]{2,1,0:T(8,128)(2,1)} %get-tuple-element.58), channel_id=1, source_target_pairs={{0,3},{1,0},{2,1},{3,2},{4,7},{5,4},{6,5},{7,6},{8,11},{9,8},{10,9... | collective-permute-start | bytes 491528 | tf_op jit(solution)/shard_map/cond/branch_1_fun/ppermute | solution.py:51
  104.1 9.5 %collective-permute-start.17 = (bf16[16,64,128]{2,1,0:T(8,128)(2,1)}, bf16[16,64,128]{2,1,0:T(8,128)(2,1)S(1)}, u32[]{:S(2)}, u32[]{:S(2)}) collective-permute-start(bf16[16,64,128]{2,1,0:T(8,128)(2,1)} %get-tuple-element.60.refs_0_), channel_id=1, source_target_pairs={{0,192},{32,224},{64,0},{96,32},{128,64},{160,96},{192,128},{224,1... | collective-permute-start | bytes 786440 | tf_op jit(solution)/shard_map/cond/branch_1_fun/ppermute | solution.py:41
  104.1 11.0 %collective-permute-start.15 = (bf16[16,64,128]{2,1,0:T(8,128)(2,1)}, bf16[16,64,128]{2,1,0:T(8,128)(2,1)S(1)}, u32[]{:S(2)}, u32[]{:S(2)}) collective-permute-start(bf16[16,64,128]{2,1,0:T(8,128)(2,1)} %get-tuple-element.60.refs_0_), channel_id=1, source_target_pairs={{0,128},{32,160},{64,192},{96,224},{128,0},{160,32},{192,64},{224,... | collective-permute-start | bytes 786440 | tf_op jit(solution)/shard_map/cond/branch_1_fun/ppermute | solution.py:41
  106.2 12.4 %collective-permute-start.13 = (bf16[16,64,128]{2,1,0:T(8,128)(2,1)}, bf16[16,64,128]{2,1,0:T(8,128)(2,1)S(1)}, u32[]{:S(2)}, u32[]{:S(2)}) collective-permute-start(bf16[16,64,128]{2,1,0:T(8,128)(2,1)} %get-tuple-element.60.refs_0_), channel_id=1, source_target_pairs={{0,64},{32,96},{64,128},{96,160},{128,192},{160,224},{192,0},{224,... | collective-permute-start | bytes 786440 | tf_op jit(solution)/shard_map/cond/branch_1_fun/ppermute | solution.py:41
  106.3 12.4 %collective-permute-start.12 = (bf16[16,64,128]{2,1,0:T(8,128)(2,1)}, bf16[16,64,128]{2,1,0:T(8,128)(2,1)S(1)}, u32[]{:S(2)}, u32[]{:S(2)}) collective-permute-start(bf16[16,64,128]{2,1,0:T(8,128)(2,1)} %get-tuple-element.60.refs_0_), channel_id=1, source_target_pairs={{0,32},{32,0},{64,96},{96,64},{128,160},{160,128},{192,224},{224,1... | collective-permute-start | bytes 786440 | tf_op jit(solution)/shard_map/cond/branch_1_fun/ppermute | solution.py:47
  113.6 5.0 %collective-permute-start.18 = (bf16[16,64,128]{2,1,0:T(8,128)(2,1)S(1)}, bf16[16,64,128]{2,1,0:T(8,128)(2,1)S(1)}, u32[]{:S(2)}, u32[]{:S(2)}) collective-permute-start(bf16[16,64,128]{2,1,0:T(8,128)(2,1)S(1)} %collective-permute-done.17.refs_6_), channel_id=1, source_target_pairs={{0,32},{32,0},{64,96},{96,64},{128,160},{160,128},{192,224},{224,1... | collective-permute-start | bytes 786440 | tf_op jit(solution)/shard_map/cond/branch_1_fun/ppermute | solution.py:47
  115.1 3.6 %collective-permute-start.16 = (bf16[16,64,128]{2,1,0:T(8,128)(2,1)S(1)}, bf16[16,64,128]{2,1,0:T(8,128)(2,1)S(1)}, u32[]{:S(2)}, u32[]{:S(2)}) collective-permute-start(bf16[16,64,128]{2,1,0:T(8,128)(2,1)S(1)} %collective-permute-done.15.refs_4_), channel_id=1, source_target_pairs={{0,32},{32,0},{64,96},{96,64},{128,160},{160,128},{192,224},{224,1... | collective-permute-start | bytes 786440 | tf_op jit(solution)/shard_map/cond/branch_1_fun/ppermute | solution.py:47
  (35 other events, 195.7 us)

commit v4 on v3

--- a/solution.py
+++ b/solution.py
@@ -178,20 +178,13 @@
             send[dz, first : first + TILE_ROWS, :] = rows[pl.ds(start, TILE_ROWS), :]
 
 
-def tiles_kernel(first, pick, frozen, out, whole, sem):
-    copies = []
+def tiles_kernel(first, pick, frozen, out):
+    cols, part = frozen.shape[1] // DP, out.shape[2] // DP
     for owner in range(Z * Y):
         rows = pl.ds(pl.multiple_of(pick[owner] * TILE_ROWS, TILE_ROWS), TILE_ROWS)
-        copies.append(
-            pltpu.make_async_copy(frozen.at[rows, :], whole.at[owner], sem.at[owner])
-        )
-        copies[owner].start()
-    cols, part = whole.shape[2] // DP, out.shape[2] // DP
-    for owner in range(Z * Y):
-        copies[owner].wait()
         for j in range(DP):
             start = j * cols + first
-            out[owner, :, j * part : (j + 1) * part] = whole[owner, :, start : start + part]
+            out[owner, :, j * part : (j + 1) * part] = frozen[rows, start : start + part]
 
 
 def choose_tiles(first, cols, pick, frozen):
@@ -199,12 +192,8 @@
     return pl.pallas_call(
         functools.partial(tiles_kernel, first),
         out_shape=jax.ShapeDtypeStruct(shape, BF16),
-        in_specs=[smem(), anywhere()],
+        in_specs=[smem(), vmem()],
         out_specs=vmem(),
-        scratch_shapes=[
-            pltpu.VMEM((Z * Y, TILE_ROWS, frozen.shape[1]), BF16),
-            pltpu.SemaphoreType.DMA((Z * Y,)),
-        ],
         compiler_params=PARAMS,
         name="tiles",
     )(pick, frozen)

time: 133 us -> 130 us (0.977)
  Pallas kernels: 32.3 us -> 26.2 us
  waiting for transfers between devices: 46.3 us -> 49.4 us
    pallas_call x2, Pallas kernels: 12.5 us -> 6.46 us  [choose_tiles(): pl.pallas_call(functools.partial(tiles_kernel, first), out_shape=jax.Shap...]
    ppermute x12, waiting for transfers between devices: 14.5 us -> 17.6 us  [shift_x(): lax.ppermute(array, 'dp', [(i, (i // 2 + k) % X * 2 + i % 2) for i in ran...]
  transfers between devices with their start and end apart: 31 -> 31, of which waited for: 18 -> 19; matrix products, arithmetic and copies ran while one was open for 2% -> 2% of each run, Pallas kernels for 22% -> 18%
where the time goes in v4:
time: 130 us
  waiting for transfers between devices  49.4 us (38%)
  starting transfers between devices  47.5 us (37%)
  Pallas kernels  26.2 us (20%)
  local copies, waits for them, and re-layouts  4.33 us (3%)
    ppermute x12, waiting for transfers between devices, shift_x(): lax.ppermute(array, 'dp', [(i, (i // 2 + k) % X * 2 + i % 2) for i in ran...  17.6 us
    ppermute x12, starting transfers between devices, shift_x(): lax.ppermute(array, 'dp', [(i, (i // 2 + k) % X * 2 + i % 2) for i in ran...  16.8 us
    ppermute x3, waiting for transfers between devices, shift_y(): lax.ppermute(array, 'expert', [(i, i // Y * Y + (i % Y + k) % Y) for i in...  14.7 us
    all_to_all x1, starting transfers between devices, per_device(): lax.all_to_all(early_out, 'expert', split_axis=0, concat_axis=0, tiled=True)  10.1 us
    all_to_all x1, starting transfers between devices, per_device(): lax.all_to_all(messages, 'expert', split_axis=0, concat_axis=0, tiled=Tru...  6.91 us
    pallas_call x2, Pallas kernels, choose_tiles(): pl.pallas_call(functools.partial(tiles_kernel, first), out_shape=jax.Shap...  6.46 us
    all_to_all x1, waiting for transfers between devices, per_device(): lax.all_to_all(mixed, 'expert', split_axis=0, concat_axis=0, tiled=True)  6.44 us
    ppermute x3, starting transfers between devices, shift_y(): lax.ppermute(array, 'expert', [(i, i // Y * Y + (i % Y + k) % Y) for i in...  5.93 us
  transfers between devices with their start and end apart: 31, of which 19 were waited for; matrix products, arithmetic and copies ran while one was open for 2% of the time, Pallas kernels for 18%

profile of v4, /device:TPU:4, one launch (start us, length us, event | category | flops | bytes accessed | tf_op | source)
XLA Modules:
  0.0 129.8 jit_solution(9655911781333125581)
XLA Ops:
  2.2 2.7 %collective-permute-start.20 = (bf16[704,128]{1,0:T(8,128)(2,1)S(1)}, bf16[704,128]{1,0:T(8,128)(2,1)S(1)}, u32[]{:S(2)}, u32[]{:S(2)}) collective-permute-start(bf16[704,128]{1,0:T(8,128)(2,1)S(1)} %pack.1), channel_id=1, source_target_pairs={{0,128},{32,160},{64,192},{96,224},{128,0},{160,32},{192,64},{224,... | collective-permute-start | bytes 540680 | tf_op jit(solution)/shard_map/ppermute | solution.py:41
  8.0 3.1 %tiles.3 = bf16[32,16,1024]{2,1,0:T(8,128)(2,1)} custom-call(s32[32]{0:T(128)} %fusion.2.pick, bf16[512,3072]{1,0:T(8,128)(2,1)} %bitcast.29), custom_call_target="tpu_custom_call" | custom-call | tf_op jit(solution)/shard_map/tiles/pallas_call | solution.py:192
  11.1 10.1 %all-to-all-start = ((bf16[32,16,1024]{2,1,0:T(8,128)(2,1)}), bf16[32,16,1024]{2,1,0:T(8,128)(2,1)}, u32[]{:S(2)}, u32[]{:S(2)}) async-start(bf16[32,16,1024]{2,1,0:T(8,128)(2,1)} %tiles.3), calls=%async_computation | async-start | bytes 2097152 | tf_op jit(solution)/shard_map/all_to_all | solution.py:321
  21.9 10.1 %conditional.3 = (bf16[4,704,128]{2,1,0:T(8,128)(2,1)S(1)}, bf16[4,704,128]{2,1,0:T(8,128)(2,1)}) conditional(s32[]{:T(128)} %convert_element_type.2, () %tuple.33, (bf16[1,1,256,4096]{3,2,1,0:T(8,128)(2,1)S(1)}, bf16[1,1,256,3072]{3,2,1,0:T(8,128)(2,1)}, bf16[704,128]{1,0:T(8,128)(2,1)S(1)}, bf16[704,128]{1,0:T(8,128)(2,1)S(1)}, ...), branch_computations={%region_1.2_spmd, %region_2.3_spmd} | conditional | bytes 8651080 | solution.py:338
  24.9 4.6 %gradients.1 = (bf16[4,704,128]{2,1,0:T(8,128)(2,1)S(1)}, bf16[4,704,128]{2,1,0:T(8,128)(2,1)}) custom-call(s32[2]{0:T(128)} %get-tuple-element.37.ids, s32[8]{0:T(128)S(1)} %get-tuple-element.38.counts, bf16[256,4096]{1,0:T(8,128)(2,1)S(1)} %bitcast.31, bf16[256,3072]{1,0:T(8,128)(2,1)} %bitcast.32, bf16[704,128]{1,0:T(8,128)(2,1)S(1)} %get-tuple-element.41.refs_0_, ...), custom_call_target="tpu_custom_call" | custom-call | tf_op jit(solution)/shard_map/cond/branch_1_fun/gradients/pallas_call | solution.py:327
  29.7 2.3 %collective-permute-done.4 = bf16[4,704,128]{2,1,0:T(8,128)(2,1)} collective-permute-done((bf16[4,704,128]{2,1,0:T(8,128)(2,1)}, bf16[4,704,128]{2,1,0:T(8,128)(2,1)}, u32[]{:S(2)}, u32[]{:S(2)}) %collective-permute-start.4) | collective-permute-done | bytes 720928 | tf_op jit(solution)/shard_map/cond/branch_1_fun/ppermute | solution.py:47
  38.2 3.4 %tiles.2.late = bf16[32,16,2048]{2,1,0:T(8,128)(2,1)} custom-call(s32[32]{0:T(128)} %fusion.2.pick, bf16[512,3072]{1,0:T(8,128)(2,1)} %bitcast.30), custom_call_target="tpu_custom_call" | custom-call | tf_op jit(solution)/shard_map/tiles/pallas_call | solution.py:192
  41.6 2.9 %collective-permute-done.24.refs_3_ = bf16[704,128]{1,0:T(8,128)(2,1)S(1)} collective-permute-done((bf16[704,128]{1,0:T(8,128)(2,1)}, bf16[704,128]{1,0:T(8,128)(2,1)S(1)}, u32[]{:S(2)}, u32[]{:S(2)}) %collective-permute-start.24) | collective-permute-done | bytes 180256 | tf_op jit(solution)/shard_map/ppermute | solution.py:41
  44.5 2.3 %collective-permute-done.23.refs_2_ = bf16[704,128]{1,0:T(8,128)(2,1)S(1)} collective-permute-done((bf16[704,128]{1,0:T(8,128)(2,1)}, bf16[704,128]{1,0:T(8,128)(2,1)S(1)}, u32[]{:S(2)}, u32[]{:S(2)}) %collective-permute-start.23) | collective-permute-done | bytes 180256 | tf_op jit(solution)/shard_map/ppermute | solution.py:41
  48.9 3.2 %collective-permute-start.26 = (bf16[128,128]{1,0:T(8,128)(2,1)S(1)}, bf16[128,128]{1,0:T(8,128)(2,1)S(1)}, u32[]{:S(2)}, u32[]{:S(2)}) collective-permute-start(bf16[128,128]{1,0:T(8,128)(2,1)S(1)} %get-tuple-element.112), channel_id=1, source_target_pairs={{0,128},{32,160},{64,192},{96,224},{128,0},{160,32},{192,64},{224,... | collective-permute-start | bytes 98312 | tf_op jit(solution)/shard_map/ppermute | solution.py:41
  52.1 2.3 %collective-permute-start.25 = (bf16[128,128]{1,0:T(8,128)(2,1)S(1)}, bf16[128,128]{1,0:T(8,128)(2,1)S(1)}, u32[]{:S(2)}, u32[]{:S(2)}) collective-permute-start(bf16[128,128]{1,0:T(8,128)(2,1)S(1)} %get-tuple-element.112), channel_id=1, source_target_pairs={{0,64},{32,96},{64,128},{96,160},{128,192},{160,224},{192,0},{224,... | collective-permute-start | bytes 98312 | tf_op jit(solution)/shard_map/ppermute | solution.py:41
  54.5 6.9 %all-to-all-start.1 = ((bf16[8,128,128]{2,1,0:T(8,128)(2,1)}), bf16[8,128,128]{2,1,0:T(8,128)(2,1)S(1)}, u32[]{:S(2)}, u32[]{:S(2)}) async-start(bf16[8,128,128]{2,1,0:T(8,128)(2,1)} %get-tuple-element.122), calls=%async_computation.1 | async-start | bytes 524288 | tf_op jit(solution)/shard_map/all_to_all | solution.py:366
  63.5 2.2 %mix.1 = bf16[32,16,2048]{2,1,0:T(8,128)(2,1)S(1)} custom-call(s32[2]{0:T(128)} %pad_add_fusion.ids, bf16[32,16,2048]{2,1,0:T(8,128)(2,1)S(1)} %copy-done, bf16[512,128]{1,0:T(8,128)(2,1)S(1)} %get-tuple-element.111.rows, bf16[128,128]{1,0:T(8,128)(2,1)S(1)} %get-tuple-element.113.refs_0_, bf16[128,128]{1,0:T(8,128)(2,1)} %get-tuple-element.114.refs_1_, ...), custom_call_target="tpu_custom_call" | custom-call | flops 4680000000 | bytes 15600000 | tf_op jit(solution)/shard_map/mix/pallas_call | solution.py:379
  67.0 4.8 %all-to-all-done.1 = bf16[8,128,128]{2,1,0:T(8,128)(2,1)S(1)} async-done(((bf16[8,128,128]{2,1,0:T(8,128)(2,1)}), bf16[8,128,128]{2,1,0:T(8,128)(2,1)S(1)}, u32[]{:S(2)}, u32[]{:S(2)}) %all-to-all-start.1) | async-done | bytes 262176 | tf_op jit(solution)/shard_map/all_to_all | solution.py:366
  71.9 5.3 %all-to-all-start.2 = ((bf16[32,16,2048]{2,1,0:T(8,128)(2,1)}), bf16[32,16,2048]{2,1,0:T(8,128)(2,1)S(1)}, u32[]{:S(2)}, u32[]{:S(2)}) async-start(bf16[32,16,2048]{2,1,0:T(8,128)(2,1)} %copy-done.1), calls=%async_computation.2 | async-start | bytes 4194304 | tf_op jit(solution)/shard_map/all_to_all | solution.py:389
  77.2 44.2 %conditional.5 = (bf16[16,16,1024]{2,1,0:T(8,128)(2,1)S(1)}) conditional(s32[]{:T(128)} %convert_element_type.2, () %tuple.36, (bf16[8,128,128]{2,1,0:T(8,128)(2,1)S(1)}, s32[2]{0:T(128)}, s32[512]{0:T(512)S(1)}, bf16[32,16,1024]{2,1,0:T(8,128)(2,1)}) %tuple.52), branch_computations={%region_5.6_spmd, %region_6.7_spmd} | conditional | bytes 18612912 | solution.py:428
  79.9 2.7 %collective-permute-start.10 = (bf16[8,80,128]{2,1,0:T(8,128)(2,1)}, bf16[8,80,128]{2,1,0:T(8,128)(2,1)S(1)}, u32[]{:S(2)}, u32[]{:S(2)}) collective-permute-start(bf16[8,80,128]{2,1,0:T(8,128)(2,1)} %get-tuple-element.57), channel_id=1, source_target_pairs={{0,2},{1,3},{2,0},{3,1},{4,6},{5,7},{6,4},{7,5},{8,10},{9,11},{10,... | collective-permute-start | bytes 491528 | tf_op jit(solution)/shard_map/cond/branch_1_fun/ppermute | solution.py:51
  84.0 4.1 %collective-permute-done.9.refs_1_ = bf16[8,80,128]{2,1,0:T(8,128)(2,1)S(1)} collective-permute-done((bf16[8,80,128]{2,1,0:T(8,128)(2,1)}, bf16[8,80,128]{2,1,0:T(8,128)(2,1)S(1)}, u32[]{:S(2)}, u32[]{:S(2)}) %collective-permute-start.9) | collective-permute-done | bytes 163872 | tf_op jit(solution)/shard_map/cond/branch_1_fun/ppermute | solution.py:51
  88.1 10.6 %collective-permute-done.10.refs_2_ = bf16[8,80,128]{2,1,0:T(8,128)(2,1)S(1)} collective-permute-done((bf16[8,80,128]{2,1,0:T(8,128)(2,1)}, bf16[8,80,128]{2,1,0:T(8,128)(2,1)S(1)}, u32[]{:S(2)}, u32[]{:S(2)}) %collective-permute-start.10) | collective-permute-done | bytes 163872 | tf_op jit(solution)/shard_map/cond/branch_1_fun/ppermute | solution.py:51
  99.5 2.5 %select.7 = (bf16[16,64,128]{2,1,0:T(8,128)(2,1)}, bf16[16,16,128]{2,1,0:T(8,128)(2,1)}) custom-call(s32[2]{0:T(128)} %get-tuple-element.51.ids, s32[512]{0:T(512)S(1)} %get-tuple-element.52.table, bf16[8,80,128]{2,1,0:T(8,128)(2,1)} %get-tuple-element.55.refs_0_, bf16[8,80,128]{2,1,0:T(8,128)(2,1)} %copy-done.22, bf16[8,80,128]{2,1,0:T(8,128)(2,1)} %copy-done.23, ...), custom_call_target="tpu_custom_call" | custom-call | tf_op jit(solution)/shard_map/cond/branch_1_fun/select/pallas_call | solution.py:403
  104.1 7.3 %collective-permute-done.17.refs_6_ = bf16[16,64,128]{2,1,0:T(8,128)(2,1)S(1)} collective-permute-done((bf16[16,64,128]{2,1,0:T(8,128)(2,1)}, bf16[16,64,128]{2,1,0:T(8,128)(2,1)S(1)}, u32[]{:S(2)}, u32[]{:S(2)}) %collective-permute-start.17) | collective-permute-done | bytes 262176 | tf_op jit(solution)/shard_map/cond/branch_1_fun/ppermute | solution.py:41
  113.0 3.5 %collective-permute-done.13.refs_2_ = bf16[16,64,128]{2,1,0:T(8,128)(2,1)S(1)} collective-permute-done((bf16[16,64,128]{2,1,0:T(8,128)(2,1)}, bf16[16,64,128]{2,1,0:T(8,128)(2,1)S(1)}, u32[]{:S(2)}, u32[]{:S(2)}) %collective-permute-start.13) | collective-permute-done | bytes 262176 | tf_op jit(solution)/shard_map/cond/branch_1_fun/ppermute | solution.py:41
  118.8 2.6 %early.1 = bf16[16,16,1024]{2,1,0:T(8,128)(2,1)S(1)} custom-call(s32[2]{0:T(128)} %get-tuple-element.51.ids, s32[512]{0:T(512)S(1)} %get-tuple-element.52.table, bf16[32,16,1024]{2,1,0:T(8,128)(2,1)} %get-tuple-element.53.early, bf16[16,16,128]{2,1,0:T(8,128)(2,1)} %get-tuple-element.59.downs, bf16[16,64,128]{2,1,0:T(8,128)(2,1)} %get-tuple-element.60.refs_0_, ...), custom_call_target="tpu_custom_call" | custom-call | tf_op jit(solution)/shard_map/cond/branch_1_fun/early/pallas_call | solution.py:416
  121.4 6.4 %all-to-all-done.2.late = bf16[32,16,2048]{2,1,0:T(8,128)(2,1)S(1)} async-done(((bf16[32,16,2048]{2,1,0:T(8,128)(2,1)}), bf16[32,16,2048]{2,1,0:T(8,128)(2,1)S(1)}, u32[]{:S(2)}, u32[]{:S(2)}) %all-to-all-start.2) | async-done | bytes 2097184 | tf_op jit(solution)/shard_map/all_to_all | solution.py:389
  (115 shorter events, 35.0 us)
Async XLA Ops:
  1.6 20.2 %collective-permute-start.21 = (bf16[704,128]{1,0:T(8,128)(2,1)S(1)}, bf16[704,128]{1,0:T(8,128)(2,1)S(1)}, u32[]{:S(2)}, u32[]{:S(2)}) collective-permute-start(bf16[704,128]{1,0:T(8,128)(2,1)S(1)} %pack.1), channel_id=1, source_target_pairs={{0,192},{32,224},{64,0},{96,32},{128,64},{160,96},{192,128},{224,1... | collective-permute-start | bytes 540680 | tf_op jit(solution)/shard_map/ppermute | solution.py:41
  2.2 19.6 %collective-permute-start.20 = (bf16[704,128]{1,0:T(8,128)(2,1)S(1)}, bf16[704,128]{1,0:T(8,128)(2,1)S(1)}, u32[]{:S(2)}, u32[]{:S(2)}) collective-permute-start(bf16[704,128]{1,0:T(8,128)(2,1)S(1)} %pack.1), channel_id=1, source_target_pairs={{0,128},{32,160},{64,192},{96,224},{128,0},{160,32},{192,64},{224,... | collective-permute-start | bytes 540680 | tf_op jit(solution)/shard_map/ppermute | solution.py:41
  5.0 16.9 %collective-permute-start.19 = (bf16[704,128]{1,0:T(8,128)(2,1)S(1)}, bf16[704,128]{1,0:T(8,128)(2,1)S(1)}, u32[]{:S(2)}, u32[]{:S(2)}) collective-permute-start(bf16[704,128]{1,0:T(8,128)(2,1)S(1)} %pack.1), channel_id=1, source_target_pairs={{0,64},{32,96},{64,128},{96,160},{128,192},{160,224},{192,0},{224,... | collective-permute-start | bytes 540680 | tf_op jit(solution)/shard_map/ppermute | solution.py:41
  11.1 43.4 %all-to-all-start = ((bf16[32,16,1024]{2,1,0:T(8,128)(2,1)}), bf16[32,16,1024]{2,1,0:T(8,128)(2,1)}, u32[]{:S(2)}, u32[]{:S(2)}) async-start(bf16[32,16,1024]{2,1,0:T(8,128)(2,1)} %tiles.3), calls=%async_computation | async-start | bytes 2097152 | tf_op jit(solution)/shard_map/all_to_all | solution.py:321
  22.0 1.7 %collective-permute-start.1 = (bf16[704,128]{1,0:T(8,128)(2,1)S(1)}, bf16[704,128]{1,0:T(8,128)(2,1)S(1)}, u32[]{:S(2)}, u32[]{:S(2)}) collective-permute-start(bf16[704,128]{1,0:T(8,128)(2,1)S(1)} %get-tuple-element.42.refs_2_), channel_id=1, source_target_pairs={{0,32},{32,0},{64,96},{96,64},{128,160},{160,128},{192,224},{224,1... | collective-permute-start | bytes 540680 | tf_op jit(solution)/shard_map/cond/branch_1_fun/ppermute | solution.py:47
  22.6 1.6 %collective-permute-start.3 = (bf16[704,128]{1,0:T(8,128)(2,1)S(1)}, bf16[704,128]{1,0:T(8,128)(2,1)S(1)}, u32[]{:S(2)}, u32[]{:S(2)}) collective-permute-start(bf16[704,128]{1,0:T(8,128)(2,1)S(1)} %get-tuple-element.44.refs_6_), channel_id=1, source_target_pairs={{0,32},{32,0},{64,96},{96,64},{128,160},{160,128},{192,224},{224,1... | collective-permute-start | bytes 540680 | tf_op jit(solution)/shard_map/cond/branch_1_fun/ppermute | solution.py:47
  29.5 2.5 %collective-permute-start.4 = (bf16[4,704,128]{2,1,0:T(8,128)(2,1)}, bf16[4,704,128]{2,1,0:T(8,128)(2,1)}, u32[]{:S(2)}, u32[]{:S(2)}) collective-permute-start(bf16[4,704,128]{2,1,0:T(8,128)(2,1)} %get-tuple-element.46), channel_id=1, source_target_pairs={{0,32},{32,0},{64,96},{96,64},{128,160},{160,128},{192,224},{224,1... | collective-permute-start | bytes 2162696 | tf_op jit(solution)/shard_map/cond/branch_1_fun/ppermute | solution.py:47
  34.0 10.5 %collective-permute-start.24 = (bf16[704,128]{1,0:T(8,128)(2,1)}, bf16[704,128]{1,0:T(8,128)(2,1)S(1)}, u32[]{:S(2)}, u32[]{:S(2)}) collective-permute-start(bf16[704,128]{1,0:T(8,128)(2,1)} %get-tuple-element.102), channel_id=1, source_target_pairs={{0,192},{32,224},{64,0},{96,32},{128,64},{160,96},{192,128},{224,1... | collective-permute-start | bytes 540680 | tf_op jit(solution)/shard_map/ppermute | solution.py:41
  36.0 8.4 %collective-permute-start.22 = (bf16[704,128]{1,0:T(8,128)(2,1)}, bf16[704,128]{1,0:T(8,128)(2,1)S(1)}, u32[]{:S(2)}, u32[]{:S(2)}) collective-permute-start(bf16[704,128]{1,0:T(8,128)(2,1)} %get-tuple-element.100), channel_id=1, source_target_pairs={{0,64},{32,96},{64,128},{96,160},{128,192},{160,224},{192,0},{224,... | collective-permute-start | bytes 540680 | tf_op jit(solution)/shard_map/ppermute | solution.py:41
  36.1 10.7 %collective-permute-start.23 = (bf16[704,128]{1,0:T(8,128)(2,1)}, bf16[704,128]{1,0:T(8,128)(2,1)S(1)}, u32[]{:S(2)}, u32[]{:S(2)}) collective-permute-start(bf16[704,128]{1,0:T(8,128)(2,1)} %get-tuple-element.101), channel_id=1, source_target_pairs={{0,128},{32,160},{64,192},{96,224},{128,0},{160,32},{192,64},{224,... | collective-permute-start | bytes 540680 | tf_op jit(solution)/shard_map/ppermute | solution.py:41
  48.9 12.5 %collective-permute-start.27 = (bf16[128,128]{1,0:T(8,128)(2,1)S(1)}, bf16[128,128]{1,0:T(8,128)(2,1)S(1)}, u32[]{:S(2)}, u32[]{:S(2)}) collective-permute-start(bf16[128,128]{1,0:T(8,128)(2,1)S(1)} %get-tuple-element.112), channel_id=1, source_target_pairs={{0,192},{32,224},{64,0},{96,32},{128,64},{160,96},{192,128},{224,1... | collective-permute-start | bytes 98312 | tf_op jit(solution)/shard_map/ppermute | solution.py:41
  48.9 12.5 %collective-permute-start.26 = (bf16[128,128]{1,0:T(8,128)(2,1)S(1)}, bf16[128,128]{1,0:T(8,128)(2,1)S(1)}, u32[]{:S(2)}, u32[]{:S(2)}) collective-permute-start(bf16[128,128]{1,0:T(8,128)(2,1)S(1)} %get-tuple-element.112), channel_id=1, source_target_pairs={{0,128},{32,160},{64,192},{96,224},{128,0},{160,32},{192,64},{224,... | collective-permute-start | bytes 98312 | tf_op jit(solution)/shard_map/ppermute | solution.py:41
  52.1 9.3 %collective-permute-start.25 = (bf16[128,128]{1,0:T(8,128)(2,1)S(1)}, bf16[128,128]{1,0:T(8,128)(2,1)S(1)}, u32[]{:S(2)}, u32[]{:S(2)}) collective-permute-start(bf16[128,128]{1,0:T(8,128)(2,1)S(1)} %get-tuple-element.112), channel_id=1, source_target_pairs={{0,64},{32,96},{64,128},{96,160},{128,192},{160,224},{192,0},{224,... | collective-permute-start | bytes 98312 | tf_op jit(solution)/shard_map/ppermute | solution.py:41
  54.5 17.4 %all-to-all-start.1 = ((bf16[8,128,128]{2,1,0:T(8,128)(2,1)}), bf16[8,128,128]{2,1,0:T(8,128)(2,1)S(1)}, u32[]{:S(2)}, u32[]{:S(2)}) async-start(bf16[8,128,128]{2,1,0:T(8,128)(2,1)} %get-tuple-element.122), calls=%async_computation.1 | async-start | bytes 524288 | tf_op jit(solution)/shard_map/all_to_all | solution.py:366
  71.9 56.0 %all-to-all-start.2 = ((bf16[32,16,2048]{2,1,0:T(8,128)(2,1)}), bf16[32,16,2048]{2,1,0:T(8,128)(2,1)S(1)}, u32[]{:S(2)}, u32[]{:S(2)}) async-start(bf16[32,16,2048]{2,1,0:T(8,128)(2,1)} %copy-done.1), calls=%async_computation.2 | async-start | bytes 4194304 | tf_op jit(solution)/shard_map/all_to_all | solution.py:389
  78.1 10.0 %collective-permute-start.9 = (bf16[8,80,128]{2,1,0:T(8,128)(2,1)}, bf16[8,80,128]{2,1,0:T(8,128)(2,1)S(1)}, u32[]{:S(2)}, u32[]{:S(2)}) collective-permute-start(bf16[8,80,128]{2,1,0:T(8,128)(2,1)} %get-tuple-element.56), channel_id=1, source_target_pairs={{0,1},{1,2},{2,3},{3,0},{4,5},{5,6},{6,7},{7,4},{8,9},{9,10},{10,1... | collective-permute-start | bytes 491528 | tf_op jit(solution)/shard_map/cond/branch_1_fun/ppermute | solution.py:51
  79.9 18.9 %collective-permute-start.10 = (bf16[8,80,128]{2,1,0:T(8,128)(2,1)}, bf16[8,80,128]{2,1,0:T(8,128)(2,1)S(1)}, u32[]{:S(2)}, u32[]{:S(2)}) collective-permute-start(bf16[8,80,128]{2,1,0:T(8,128)(2,1)} %get-tuple-element.57), channel_id=1, source_target_pairs={{0,2},{1,3},{2,0},{3,1},{4,6},{5,7},{6,4},{7,5},{8,10},{9,11},{10,... | collective-permute-start | bytes 491528 | tf_op jit(solution)/shard_map/cond/branch_1_fun/ppermute | solution.py:51
  82.6 16.2 %collective-permute-start.11 = (bf16[8,80,128]{2,1,0:T(8,128)(2,1)}, bf16[8,80,128]{2,1,0:T(8,128)(2,1)S(1)}, u32[]{:S(2)}, u32[]{:S(2)}) collective-permute-start(bf16[8,80,128]{2,1,0:T(8,128)(2,1)} %get-tuple-element.58), channel_id=1, source_target_pairs={{0,3},{1,0},{2,1},{3,2},{4,7},{5,4},{6,5},{7,6},{8,11},{9,8},{10,9... | collective-permute-start | bytes 491528 | tf_op jit(solution)/shard_map/cond/branch_1_fun/ppermute | solution.py:51
  102.0 9.5 %collective-permute-start.17 = (bf16[16,64,128]{2,1,0:T(8,128)(2,1)}, bf16[16,64,128]{2,1,0:T(8,128)(2,1)S(1)}, u32[]{:S(2)}, u32[]{:S(2)}) collective-permute-start(bf16[16,64,128]{2,1,0:T(8,128)(2,1)} %get-tuple-element.60.refs_0_), channel_id=1, source_target_pairs={{0,192},{32,224},{64,0},{96,32},{128,64},{160,96},{192,128},{224,1... | collective-permute-start | bytes 786440 | tf_op jit(solution)/shard_map/cond/branch_1_fun/ppermute | solution.py:41
  102.0 11.0 %collective-permute-start.15 = (bf16[16,64,128]{2,1,0:T(8,128)(2,1)}, bf16[16,64,128]{2,1,0:T(8,128)(2,1)S(1)}, u32[]{:S(2)}, u32[]{:S(2)}) collective-permute-start(bf16[16,64,128]{2,1,0:T(8,128)(2,1)} %get-tuple-element.60.refs_0_), channel_id=1, source_target_pairs={{0,128},{32,160},{64,192},{96,224},{128,0},{160,32},{192,64},{224,... | collective-permute-start | bytes 786440 | tf_op jit(solution)/shard_map/cond/branch_1_fun/ppermute | solution.py:41
  104.1 12.4 %collective-permute-start.13 = (bf16[16,64,128]{2,1,0:T(8,128)(2,1)}, bf16[16,64,128]{2,1,0:T(8,128)(2,1)S(1)}, u32[]{:S(2)}, u32[]{:S(2)}) collective-permute-start(bf16[16,64,128]{2,1,0:T(8,128)(2,1)} %get-tuple-element.60.refs_0_), channel_id=1, source_target_pairs={{0,64},{32,96},{64,128},{96,160},{128,192},{160,224},{192,0},{224,... | collective-permute-start | bytes 786440 | tf_op jit(solution)/shard_map/cond/branch_1_fun/ppermute | solution.py:41
  104.1 12.4 %collective-permute-start.12 = (bf16[16,64,128]{2,1,0:T(8,128)(2,1)}, bf16[16,64,128]{2,1,0:T(8,128)(2,1)S(1)}, u32[]{:S(2)}, u32[]{:S(2)}) collective-permute-start(bf16[16,64,128]{2,1,0:T(8,128)(2,1)} %get-tuple-element.60.refs_0_), channel_id=1, source_target_pairs={{0,32},{32,0},{64,96},{96,64},{128,160},{160,128},{192,224},{224,1... | collective-permute-start | bytes 786440 | tf_op jit(solution)/shard_map/cond/branch_1_fun/ppermute | solution.py:47
  111.5 5.0 %collective-permute-start.18 = (bf16[16,64,128]{2,1,0:T(8,128)(2,1)S(1)}, bf16[16,64,128]{2,1,0:T(8,128)(2,1)S(1)}, u32[]{:S(2)}, u32[]{:S(2)}) collective-permute-start(bf16[16,64,128]{2,1,0:T(8,128)(2,1)S(1)} %collective-permute-done.17.refs_6_), channel_id=1, source_target_pairs={{0,32},{32,0},{64,96},{96,64},{128,160},{160,128},{192,224},{224,1... | collective-permute-start | bytes 786440 | tf_op jit(solution)/shard_map/cond/branch_1_fun/ppermute | solution.py:47
  113.0 3.6 %collective-permute-start.16 = (bf16[16,64,128]{2,1,0:T(8,128)(2,1)S(1)}, bf16[16,64,128]{2,1,0:T(8,128)(2,1)S(1)}, u32[]{:S(2)}, u32[]{:S(2)}) collective-permute-start(bf16[16,64,128]{2,1,0:T(8,128)(2,1)S(1)} %collective-permute-done.15.refs_4_), channel_id=1, source_target_pairs={{0,32},{32,0},{64,96},{96,64},{128,160},{160,128},{192,224},{224,1... | collective-permute-start | bytes 786440 | tf_op jit(solution)/shard_map/cond/branch_1_fun/ppermute | solution.py:47
  (35 other events, 200.4 us)

commit v5 on v4

--- a/solution.py
+++ b/solution.py
@@ -343,7 +343,7 @@
         out_shape=[shape_block] * X,
         in_specs=[vmem()] * 2,
         out_specs=[vmem()] * X,
-        compiler_params=PARAMS,
+        compiler_params=pltpu.CompilerParams(vmem_limit_bytes=12 * 1024 * 1024),
         cost_estimate=HEAVY,
         name="pairs",
     )(kept, taken)
@@ -396,7 +396,7 @@
             out_shape=[jax.ShapeDtypeStruct((Z, b_rows + TILE_ROWS, 128), BF16)] * Y,
             in_specs=[vmem()],
             out_specs=[vmem()] * Y,
-            compiler_params=PARAMS,
+            compiler_params=pltpu.CompilerParams(vmem_limit_bytes=12 * 1024 * 1024),
             name="stack",
         )(arrived)
         parts = [parts[0]] + [shift_y(parts[dy], dy) for dy in range(1, Y)]
@@ -408,7 +408,7 @@
             ],
             in_specs=[smem()] * 2 + [vmem()] * Y,
             out_specs=[vmem()] * 2,
-            compiler_params=PARAMS,
+            compiler_params=pltpu.CompilerParams(vmem_limit_bytes=12 * 1024 * 1024),
             name="select",
         )(ids, placement_map, *parts)
         chips = [ups] + [shift_x(ups, k) for k in range(1, X)]

time: 130 us -> 130 us (level)
  waiting for transfers between devices: 49.4 us -> 51.5 us
  Pallas kernels: 26.2 us -> 24.1 us
  transfers between devices with their start and end apart: 31 -> 31, of which waited for: 19 -> 19; matrix products, arithmetic and copies ran while one was open for 2% -> 2% of each run, Pallas kernels for 18% -> 16%
where the time goes in v5:
time: 130 us
  waiting for transfers between devices  51.5 us (40%)
  starting transfers between devices  47.6 us (37%)
  Pallas kernels  24.1 us (19%)
  local copies, waits for them, and re-layouts  4.2 us (3%)
    ppermute x12, waiting for transfers between devices, shift_x(): lax.ppermute(array, 'dp', [(i, (i // 2 + k) % X * 2 + i % 2) for i in ran...  17.6 us
    ppermute x12, starting transfers between devices, shift_x(): lax.ppermute(array, 'dp', [(i, (i // 2 + k) % X * 2 + i % 2) for i in ran...  16.8 us
    ppermute x3, waiting for transfers between devices, shift_y(): lax.ppermute(array, 'expert', [(i, i // Y * Y + (i % Y + k) % Y) for i in...  15.5 us
    all_to_all x1, starting transfers between devices, per_device(): lax.all_to_all(early_out, 'expert', split_axis=0, concat_axis=0, tiled=True)  10.1 us
    all_to_all x1, waiting for transfers between devices, per_device(): lax.all_to_all(mixed, 'expert', split_axis=0, concat_axis=0, tiled=True)  7.71 us
    all_to_all x1, starting transfers between devices, per_device(): lax.all_to_all(messages, 'expert', split_axis=0, concat_axis=0, tiled=Tru...  6.91 us
    pallas_call x2, Pallas kernels, choose_tiles(): pl.pallas_call(functools.partial(tiles_kernel, first), out_shape=jax.Shap...  6.45 us
    ppermute x3, starting transfers between devices, shift_y(): lax.ppermute(array, 'expert', [(i, i // Y * Y + (i % Y + k) % Y) for i in...  6 us
  transfers between devices with their start and end apart: 31, of which 19 were waited for; matrix products, arithmetic and copies ran while one was open for 2% of the time, Pallas kernels for 16%

profile of v5, /device:TPU:4, one launch (start us, length us, event | category | flops | bytes accessed | tf_op | source)
XLA Modules:
  0.0 129.6 jit_solution(4075631480411544670)
XLA Ops:
  2.2 2.7 %collective-permute-start.20 = (bf16[704,128]{1,0:T(8,128)(2,1)S(1)}, bf16[704,128]{1,0:T(8,128)(2,1)S(1)}, u32[]{:S(2)}, u32[]{:S(2)}) collective-permute-start(bf16[704,128]{1,0:T(8,128)(2,1)S(1)} %pack.1), channel_id=1, source_target_pairs={{0,128},{32,160},{64,192},{96,224},{128,0},{160,32},{192,64},{224,... | collective-permute-start | bytes 540680 | tf_op jit(solution)/shard_map/ppermute | solution.py:41
  8.0 3.1 %tiles.3 = bf16[32,16,1024]{2,1,0:T(8,128)(2,1)} custom-call(s32[32]{0:T(128)} %fusion.2.pick, bf16[512,3072]{1,0:T(8,128)(2,1)} %bitcast.29), custom_call_target="tpu_custom_call" | custom-call | tf_op jit(solution)/shard_map/tiles/pallas_call | solution.py:192
  11.1 10.1 %all-to-all-start = ((bf16[32,16,1024]{2,1,0:T(8,128)(2,1)}), bf16[32,16,1024]{2,1,0:T(8,128)(2,1)}, u32[]{:S(2)}, u32[]{:S(2)}) async-start(bf16[32,16,1024]{2,1,0:T(8,128)(2,1)} %tiles.3), calls=%async_computation | async-start | bytes 2097152 | tf_op jit(solution)/shard_map/all_to_all | solution.py:321
  21.9 10.1 %conditional.3 = (bf16[4,704,128]{2,1,0:T(8,128)(2,1)S(1)}, bf16[4,704,128]{2,1,0:T(8,128)(2,1)}) conditional(s32[]{:T(128)} %convert_element_type.2, () %tuple.33, (bf16[1,1,256,4096]{3,2,1,0:T(8,128)(2,1)S(1)}, bf16[1,1,256,3072]{3,2,1,0:T(8,128)(2,1)}, bf16[704,128]{1,0:T(8,128)(2,1)S(1)}, bf16[704,128]{1,0:T(8,128)(2,1)S(1)}, ...), branch_computations={%region_1.2_spmd, %region_2.3_spmd} | conditional | bytes 8651080 | solution.py:338
  24.8 4.6 %gradients.1 = (bf16[4,704,128]{2,1,0:T(8,128)(2,1)S(1)}, bf16[4,704,128]{2,1,0:T(8,128)(2,1)}) custom-call(s32[2]{0:T(128)} %get-tuple-element.37.ids, s32[8]{0:T(128)S(1)} %get-tuple-element.38.counts, bf16[256,4096]{1,0:T(8,128)(2,1)S(1)} %bitcast.31, bf16[256,3072]{1,0:T(8,128)(2,1)} %bitcast.32, bf16[704,128]{1,0:T(8,128)(2,1)S(1)} %get-tuple-element.41.refs_0_, ...), custom_call_target="tpu_custom_call" | custom-call | tf_op jit(solution)/shard_map/cond/branch_1_fun/gradients/pallas_call | solution.py:327
  29.7 2.3 %collective-permute-done.4 = bf16[4,704,128]{2,1,0:T(8,128)(2,1)} collective-permute-done((bf16[4,704,128]{2,1,0:T(8,128)(2,1)}, bf16[4,704,128]{2,1,0:T(8,128)(2,1)}, u32[]{:S(2)}, u32[]{:S(2)}) %collective-permute-start.4) | collective-permute-done | bytes 720928 | tf_op jit(solution)/shard_map/cond/branch_1_fun/ppermute | solution.py:47
  38.0 3.4 %tiles.2.late = bf16[32,16,2048]{2,1,0:T(8,128)(2,1)} custom-call(s32[32]{0:T(128)} %fusion.2.pick, bf16[512,3072]{1,0:T(8,128)(2,1)} %bitcast.30), custom_call_target="tpu_custom_call" | custom-call | tf_op jit(solution)/shard_map/tiles/pallas_call | solution.py:192
  41.4 2.9 %collective-permute-done.24.refs_3_ = bf16[704,128]{1,0:T(8,128)(2,1)S(1)} collective-permute-done((bf16[704,128]{1,0:T(8,128)(2,1)}, bf16[704,128]{1,0:T(8,128)(2,1)S(1)}, u32[]{:S(2)}, u32[]{:S(2)}) %collective-permute-start.24) | collective-permute-done | bytes 180256 | tf_op jit(solution)/shard_map/ppermute | solution.py:41
  44.3 2.3 %collective-permute-done.23.refs_2_ = bf16[704,128]{1,0:T(8,128)(2,1)S(1)} collective-permute-done((bf16[704,128]{1,0:T(8,128)(2,1)S(1)}, bf16[704,128]{1,0:T(8,128)(2,1)S(1)}, u32[]{:S(2)}, u32[]{:S(2)}) %collective-permute-start.23) | collective-permute-done | bytes 180256 | tf_op jit(solution)/shard_map/ppermute | solution.py:41
  48.7 3.2 %collective-permute-start.26 = (bf16[128,128]{1,0:T(8,128)(2,1)S(1)}, bf16[128,128]{1,0:T(8,128)(2,1)S(1)}, u32[]{:S(2)}, u32[]{:S(2)}) collective-permute-start(bf16[128,128]{1,0:T(8,128)(2,1)S(1)} %get-tuple-element.112), channel_id=1, source_target_pairs={{0,128},{32,160},{64,192},{96,224},{128,0},{160,32},{192,64},{224,... | collective-permute-start | bytes 98312 | tf_op jit(solution)/shard_map/ppermute | solution.py:41
  52.0 2.3 %collective-permute-start.25 = (bf16[128,128]{1,0:T(8,128)(2,1)S(1)}, bf16[128,128]{1,0:T(8,128)(2,1)S(1)}, u32[]{:S(2)}, u32[]{:S(2)}) collective-permute-start(bf16[128,128]{1,0:T(8,128)(2,1)S(1)} %get-tuple-element.112), channel_id=1, source_target_pairs={{0,64},{32,96},{64,128},{96,160},{128,192},{160,224},{192,0},{224,... | collective-permute-start | bytes 98312 | tf_op jit(solution)/shard_map/ppermute | solution.py:41
  54.3 6.9 %all-to-all-start.1 = ((bf16[8,128,128]{2,1,0:T(8,128)(2,1)}), bf16[8,128,128]{2,1,0:T(8,128)(2,1)S(1)}, u32[]{:S(2)}, u32[]{:S(2)}) async-start(bf16[8,128,128]{2,1,0:T(8,128)(2,1)} %get-tuple-element.122), calls=%async_computation.1 | async-start | bytes 524288 | tf_op jit(solution)/shard_map/all_to_all | solution.py:366
  61.2 2.1 %conditional.4 = (bf16[128,128]{1,0:T(8,128)(2,1)S(1)}, bf16[128,128]{1,0:T(8,128)(2,1)}, bf16[128,128]{1,0:T(8,128)(2,1)S(1)}, bf16[128,128]{1,0:T(8,128)(2,1)}...) conditional(s32[]{:T(128)} %convert_element_type.2, () %tuple.37, ...), branch_computations={%region_3.4_spmd, %region_4.5_spmd} | conditional | bytes 786656 | solution.py:378
  63.3 2.2 %mix.1 = bf16[32,16,2048]{2,1,0:T(8,128)(2,1)S(1)} custom-call(s32[2]{0:T(128)} %pad_add_fusion.ids, bf16[32,16,2048]{2,1,0:T(8,128)(2,1)S(1)} %copy-done, bf16[512,128]{1,0:T(8,128)(2,1)S(1)} %get-tuple-element.111.rows, bf16[128,128]{1,0:T(8,128)(2,1)S(1)} %get-tuple-element.113.refs_0_, bf16[128,128]{1,0:T(8,128)(2,1)} %get-tuple-element.114.refs_1_, ...), custom_call_target="tpu_custom_call" | custom-call | flops 4680000000 | bytes 15600000 | tf_op jit(solution)/shard_map/mix/pallas_call | solution.py:379
  66.9 4.8 %all-to-all-done.1 = bf16[8,128,128]{2,1,0:T(8,128)(2,1)S(1)} async-done(((bf16[8,128,128]{2,1,0:T(8,128)(2,1)}), bf16[8,128,128]{2,1,0:T(8,128)(2,1)S(1)}, u32[]{:S(2)}, u32[]{:S(2)}) %all-to-all-start.1) | async-done | bytes 262176 | tf_op jit(solution)/shard_map/all_to_all | solution.py:366
  71.7 5.3 %all-to-all-start.2 = ((bf16[32,16,2048]{2,1,0:T(8,128)(2,1)}), bf16[32,16,2048]{2,1,0:T(8,128)(2,1)S(1)}, u32[]{:S(2)}, u32[]{:S(2)}) async-start(bf16[32,16,2048]{2,1,0:T(8,128)(2,1)} %copy-done.1), calls=%async_computation.2 | async-start | bytes 4194304 | tf_op jit(solution)/shard_map/all_to_all | solution.py:389
  77.0 42.9 %conditional.5 = (bf16[16,16,1024]{2,1,0:T(8,128)(2,1)S(1)}) conditional(s32[]{:T(128)} %convert_element_type.2, () %tuple.36, (bf16[8,128,128]{2,1,0:T(8,128)(2,1)S(1)}, s32[2]{0:T(128)}, s32[512]{0:T(512)S(1)}, bf16[32,16,1024]{2,1,0:T(8,128)(2,1)}) %tuple.52), branch_computations={%region_5.6_spmd, %region_6.7_spmd} | conditional | bytes 17957524 | solution.py:428
  79.0 2.7 %collective-permute-start.10 = (bf16[8,80,128]{2,1,0:T(8,128)(2,1)S(1)}, bf16[8,80,128]{2,1,0:T(8,128)(2,1)S(1)}, u32[]{:S(2)}, u32[]{:S(2)}) collective-permute-start(bf16[8,80,128]{2,1,0:T(8,128)(2,1)S(1)} %get-tuple-element.57), channel_id=1, source_target_pairs={{0,2},{1,3},{2,0},{3,1},{4,6},{5,7},{6,4},{7,5},{8,10},{9,11},{10,... | collective-permute-start | bytes 491528 | tf_op jit(solution)/shard_map/cond/branch_1_fun/ppermute | solution.py:51
  83.1 4.7 %collective-permute-done.9.refs_1_ = bf16[8,80,128]{2,1,0:T(8,128)(2,1)S(1)} collective-permute-done((bf16[8,80,128]{2,1,0:T(8,128)(2,1)S(1)}, bf16[8,80,128]{2,1,0:T(8,128)(2,1)S(1)}, u32[]{:S(2)}, u32[]{:S(2)}) %collective-permute-start.9) | collective-permute-done | bytes 163872 | tf_op jit(solution)/shard_map/cond/branch_1_fun/ppermute | solution.py:51
  87.8 10.8 %collective-permute-done.10.refs_2_ = bf16[8,80,128]{2,1,0:T(8,128)(2,1)S(1)} collective-permute-done((bf16[8,80,128]{2,1,0:T(8,128)(2,1)S(1)}, bf16[8,80,128]{2,1,0:T(8,128)(2,1)S(1)}, u32[]{:S(2)}, u32[]{:S(2)}) %collective-permute-start.10) | collective-permute-done | bytes 163872 | tf_op jit(solution)/shard_map/cond/branch_1_fun/ppermute | solution.py:51
  102.6 7.1 %collective-permute-done.17.refs_6_ = bf16[16,64,128]{2,1,0:T(8,128)(2,1)S(1)} collective-permute-done((bf16[16,64,128]{2,1,0:T(8,128)(2,1)S(1)}, bf16[16,64,128]{2,1,0:T(8,128)(2,1)S(1)}, u32[]{:S(2)}, u32[]{:S(2)}) %collective-permute-start.17) | collective-permute-done | bytes 262176 | tf_op jit(solution)/shard_map/cond/branch_1_fun/ppermute | solution.py:41
  111.3 3.7 %collective-permute-done.13.refs_2_ = bf16[16,64,128]{2,1,0:T(8,128)(2,1)S(1)} collective-permute-done((bf16[16,64,128]{2,1,0:T(8,128)(2,1)S(1)}, bf16[16,64,128]{2,1,0:T(8,128)(2,1)S(1)}, u32[]{:S(2)}, u32[]{:S(2)}) %collective-permute-start.13) | collective-permute-done | bytes 262176 | tf_op jit(solution)/shard_map/cond/branch_1_fun/ppermute | solution.py:41
  117.3 2.6 %early.1 = bf16[16,16,1024]{2,1,0:T(8,128)(2,1)S(1)} custom-call(s32[2]{0:T(128)} %get-tuple-element.51.ids, s32[512]{0:T(512)S(1)} %get-tuple-element.52.table, bf16[32,16,1024]{2,1,0:T(8,128)(2,1)} %get-tuple-element.53.early, bf16[16,16,128]{2,1,0:T(8,128)(2,1)} %copy-done.9, bf16[16,64,128]{2,1,0:T(8,128)(2,1)} %copy-done.4, ...), custom_call_target="tpu_custom_call" | custom-call | tf_op jit(solution)/shard_map/cond/branch_1_fun/early/pallas_call | solution.py:416
  119.9 7.7 %all-to-all-done.2.late = bf16[32,16,2048]{2,1,0:T(8,128)(2,1)S(1)} async-done(((bf16[32,16,2048]{2,1,0:T(8,128)(2,1)}), bf16[32,16,2048]{2,1,0:T(8,128)(2,1)S(1)}, u32[]{:S(2)}, u32[]{:S(2)}) %all-to-all-start.2) | async-done | bytes 2097184 | tf_op jit(solution)/shard_map/all_to_all | solution.py:389
  (111 shorter events, 33.1 us)
Async XLA Ops:
  1.6 20.2 %collective-permute-start.21 = (bf16[704,128]{1,0:T(8,128)(2,1)S(1)}, bf16[704,128]{1,0:T(8,128)(2,1)S(1)}, u32[]{:S(2)}, u32[]{:S(2)}) collective-permute-start(bf16[704,128]{1,0:T(8,128)(2,1)S(1)} %pack.1), channel_id=1, source_target_pairs={{0,192},{32,224},{64,0},{96,32},{128,64},{160,96},{192,128},{224,1... | collective-permute-start | bytes 540680 | tf_op jit(solution)/shard_map/ppermute | solution.py:41
  2.2 19.6 %collective-permute-start.20 = (bf16[704,128]{1,0:T(8,128)(2,1)S(1)}, bf16[704,128]{1,0:T(8,128)(2,1)S(1)}, u32[]{:S(2)}, u32[]{:S(2)}) collective-permute-start(bf16[704,128]{1,0:T(8,128)(2,1)S(1)} %pack.1), channel_id=1, source_target_pairs={{0,128},{32,160},{64,192},{96,224},{128,0},{160,32},{192,64},{224,... | collective-permute-start | bytes 540680 | tf_op jit(solution)/shard_map/ppermute | solution.py:41
  5.0 16.9 %collective-permute-start.19 = (bf16[704,128]{1,0:T(8,128)(2,1)S(1)}, bf16[704,128]{1,0:T(8,128)(2,1)S(1)}, u32[]{:S(2)}, u32[]{:S(2)}) collective-permute-start(bf16[704,128]{1,0:T(8,128)(2,1)S(1)} %pack.1), channel_id=1, source_target_pairs={{0,64},{32,96},{64,128},{96,160},{128,192},{160,224},{192,0},{224,... | collective-permute-start | bytes 540680 | tf_op jit(solution)/shard_map/ppermute | solution.py:41
  11.1 43.2 %all-to-all-start = ((bf16[32,16,1024]{2,1,0:T(8,128)(2,1)}), bf16[32,16,1024]{2,1,0:T(8,128)(2,1)}, u32[]{:S(2)}, u32[]{:S(2)}) async-start(bf16[32,16,1024]{2,1,0:T(8,128)(2,1)} %tiles.3), calls=%async_computation | async-start | bytes 2097152 | tf_op jit(solution)/shard_map/all_to_all | solution.py:321
  22.0 1.7 %collective-permute-start.1 = (bf16[704,128]{1,0:T(8,128)(2,1)S(1)}, bf16[704,128]{1,0:T(8,128)(2,1)S(1)}, u32[]{:S(2)}, u32[]{:S(2)}) collective-permute-start(bf16[704,128]{1,0:T(8,128)(2,1)S(1)} %get-tuple-element.42.refs_2_), channel_id=1, source_target_pairs={{0,32},{32,0},{64,96},{96,64},{128,160},{160,128},{192,224},{224,1... | collective-permute-start | bytes 540680 | tf_op jit(solution)/shard_map/cond/branch_1_fun/ppermute | solution.py:47
  22.6 1.6 %collective-permute-start.3 = (bf16[704,128]{1,0:T(8,128)(2,1)S(1)}, bf16[704,128]{1,0:T(8,128)(2,1)S(1)}, u32[]{:S(2)}, u32[]{:S(2)}) collective-permute-start(bf16[704,128]{1,0:T(8,128)(2,1)S(1)} %get-tuple-element.44.refs_6_), channel_id=1, source_target_pairs={{0,32},{32,0},{64,96},{96,64},{128,160},{160,128},{192,224},{224,1... | collective-permute-start | bytes 540680 | tf_op jit(solution)/shard_map/cond/branch_1_fun/ppermute | solution.py:47
  29.4 2.5 %collective-permute-start.4 = (bf16[4,704,128]{2,1,0:T(8,128)(2,1)}, bf16[4,704,128]{2,1,0:T(8,128)(2,1)}, u32[]{:S(2)}, u32[]{:S(2)}) collective-permute-start(bf16[4,704,128]{2,1,0:T(8,128)(2,1)} %get-tuple-element.46), channel_id=1, source_target_pairs={{0,32},{32,0},{64,96},{96,64},{128,160},{160,128},{192,224},{224,1... | collective-permute-start | bytes 2162696 | tf_op jit(solution)/shard_map/cond/branch_1_fun/ppermute | solution.py:47
  33.8 10.5 %collective-permute-start.24 = (bf16[704,128]{1,0:T(8,128)(2,1)}, bf16[704,128]{1,0:T(8,128)(2,1)S(1)}, u32[]{:S(2)}, u32[]{:S(2)}) collective-permute-start(bf16[704,128]{1,0:T(8,128)(2,1)} %get-tuple-element.102), channel_id=1, source_target_pairs={{0,192},{32,224},{64,0},{96,32},{128,64},{160,96},{192,128},{224,1... | collective-permute-start | bytes 540680 | tf_op jit(solution)/shard_map/ppermute | solution.py:41
  35.9 8.4 %collective-permute-start.22 = (bf16[704,128]{1,0:T(8,128)(2,1)}, bf16[704,128]{1,0:T(8,128)(2,1)S(1)}, u32[]{:S(2)}, u32[]{:S(2)}) collective-permute-start(bf16[704,128]{1,0:T(8,128)(2,1)} %get-tuple-element.100), channel_id=1, source_target_pairs={{0,64},{32,96},{64,128},{96,160},{128,192},{160,224},{192,0},{224,... | collective-permute-start | bytes 540680 | tf_op jit(solution)/shard_map/ppermute | solution.py:41
  35.9 10.7 %collective-permute-start.23 = (bf16[704,128]{1,0:T(8,128)(2,1)S(1)}, bf16[704,128]{1,0:T(8,128)(2,1)S(1)}, u32[]{:S(2)}, u32[]{:S(2)}) collective-permute-start(bf16[704,128]{1,0:T(8,128)(2,1)S(1)} %get-tuple-element.101), channel_id=1, source_target_pairs={{0,128},{32,160},{64,192},{96,224},{128,0},{160,32},{192,64},{224,... | collective-permute-start | bytes 540680 | tf_op jit(solution)/shard_map/ppermute | solution.py:41
  48.7 12.5 %collective-permute-start.27 = (bf16[128,128]{1,0:T(8,128)(2,1)S(1)}, bf16[128,128]{1,0:T(8,128)(2,1)S(1)}, u32[]{:S(2)}, u32[]{:S(2)}) collective-permute-start(bf16[128,128]{1,0:T(8,128)(2,1)S(1)} %get-tuple-element.112), channel_id=1, source_target_pairs={{0,192},{32,224},{64,0},{96,32},{128,64},{160,96},{192,128},{224,1... | collective-permute-start | bytes 98312 | tf_op jit(solution)/shard_map/ppermute | solution.py:41
  48.7 12.5 %collective-permute-start.26 = (bf16[128,128]{1,0:T(8,128)(2,1)S(1)}, bf16[128,128]{1,0:T(8,128)(2,1)S(1)}, u32[]{:S(2)}, u32[]{:S(2)}) collective-permute-start(bf16[128,128]{1,0:T(8,128)(2,1)S(1)} %get-tuple-element.112), channel_id=1, source_target_pairs={{0,128},{32,160},{64,192},{96,224},{128,0},{160,32},{192,64},{224,... | collective-permute-start | bytes 98312 | tf_op jit(solution)/shard_map/ppermute | solution.py:41
  52.0 9.3 %collective-permute-start.25 = (bf16[128,128]{1,0:T(8,128)(2,1)S(1)}, bf16[128,128]{1,0:T(8,128)(2,1)S(1)}, u32[]{:S(2)}, u32[]{:S(2)}) collective-permute-start(bf16[128,128]{1,0:T(8,128)(2,1)S(1)} %get-tuple-element.112), channel_id=1, source_target_pairs={{0,64},{32,96},{64,128},{96,160},{128,192},{160,224},{192,0},{224,... | collective-permute-start | bytes 98312 | tf_op jit(solution)/shard_map/ppermute | solution.py:41
  54.3 17.4 %all-to-all-start.1 = ((bf16[8,128,128]{2,1,0:T(8,128)(2,1)}), bf16[8,128,128]{2,1,0:T(8,128)(2,1)S(1)}, u32[]{:S(2)}, u32[]{:S(2)}) async-start(bf16[8,128,128]{2,1,0:T(8,128)(2,1)} %get-tuple-element.122), calls=%async_computation.1 | async-start | bytes 524288 | tf_op jit(solution)/shard_map/all_to_all | solution.py:366
  71.7 56.0 %all-to-all-start.2 = ((bf16[32,16,2048]{2,1,0:T(8,128)(2,1)}), bf16[32,16,2048]{2,1,0:T(8,128)(2,1)S(1)}, u32[]{:S(2)}, u32[]{:S(2)}) async-start(bf16[32,16,2048]{2,1,0:T(8,128)(2,1)} %copy-done.1), calls=%async_computation.2 | async-start | bytes 4194304 | tf_op jit(solution)/shard_map/all_to_all | solution.py:389
  77.1 10.7 %collective-permute-start.9 = (bf16[8,80,128]{2,1,0:T(8,128)(2,1)S(1)}, bf16[8,80,128]{2,1,0:T(8,128)(2,1)S(1)}, u32[]{:S(2)}, u32[]{:S(2)}) collective-permute-start(bf16[8,80,128]{2,1,0:T(8,128)(2,1)S(1)} %get-tuple-element.56), channel_id=1, source_target_pairs={{0,1},{1,2},{2,3},{3,0},{4,5},{5,6},{6,7},{7,4},{8,9},{9,10},{10,1... | collective-permute-start | bytes 491528 | tf_op jit(solution)/shard_map/cond/branch_1_fun/ppermute | solution.py:51
  79.0 19.6 %collective-permute-start.10 = (bf16[8,80,128]{2,1,0:T(8,128)(2,1)S(1)}, bf16[8,80,128]{2,1,0:T(8,128)(2,1)S(1)}, u32[]{:S(2)}, u32[]{:S(2)}) collective-permute-start(bf16[8,80,128]{2,1,0:T(8,128)(2,1)S(1)} %get-tuple-element.57), channel_id=1, source_target_pairs={{0,2},{1,3},{2,0},{3,1},{4,6},{5,7},{6,4},{7,5},{8,10},{9,11},{10,... | collective-permute-start | bytes 491528 | tf_op jit(solution)/shard_map/cond/branch_1_fun/ppermute | solution.py:51
  81.6 16.9 %collective-permute-start.11 = (bf16[8,80,128]{2,1,0:T(8,128)(2,1)S(1)}, bf16[8,80,128]{2,1,0:T(8,128)(2,1)S(1)}, u32[]{:S(2)}, u32[]{:S(2)}) collective-permute-start(bf16[8,80,128]{2,1,0:T(8,128)(2,1)S(1)} %get-tuple-element.58), channel_id=1, source_target_pairs={{0,3},{1,0},{2,1},{3,2},{4,7},{5,4},{6,5},{7,6},{8,11},{9,8},{10,9... | collective-permute-start | bytes 491528 | tf_op jit(solution)/shard_map/cond/branch_1_fun/ppermute | solution.py:51
  100.5 9.2 %collective-permute-start.17 = (bf16[16,64,128]{2,1,0:T(8,128)(2,1)S(1)}, bf16[16,64,128]{2,1,0:T(8,128)(2,1)S(1)}, u32[]{:S(2)}, u32[]{:S(2)}) collective-permute-start(bf16[16,64,128]{2,1,0:T(8,128)(2,1)S(1)} %get-tuple-element.60.refs_0_), channel_id=1, source_target_pairs={{0,192},{32,224},{64,0},{96,32},{128,64},{160,96},{192,128},{224,1... | collective-permute-start | bytes 786440 | tf_op jit(solution)/shard_map/cond/branch_1_fun/ppermute | solution.py:41
  100.5 10.8 %collective-permute-start.15 = (bf16[16,64,128]{2,1,0:T(8,128)(2,1)S(1)}, bf16[16,64,128]{2,1,0:T(8,128)(2,1)S(1)}, u32[]{:S(2)}, u32[]{:S(2)}) collective-permute-start(bf16[16,64,128]{2,1,0:T(8,128)(2,1)S(1)} %get-tuple-element.60.refs_0_), channel_id=1, source_target_pairs={{0,128},{32,160},{64,192},{96,224},{128,0},{160,32},{192,64},{224,... | collective-permute-start | bytes 786440 | tf_op jit(solution)/shard_map/cond/branch_1_fun/ppermute | solution.py:41
  102.6 12.4 %collective-permute-start.13 = (bf16[16,64,128]{2,1,0:T(8,128)(2,1)S(1)}, bf16[16,64,128]{2,1,0:T(8,128)(2,1)S(1)}, u32[]{:S(2)}, u32[]{:S(2)}) collective-permute-start(bf16[16,64,128]{2,1,0:T(8,128)(2,1)S(1)} %get-tuple-element.60.refs_0_), channel_id=1, source_target_pairs={{0,64},{32,96},{64,128},{96,160},{128,192},{160,224},{192,0},{224,... | collective-permute-start | bytes 786440 | tf_op jit(solution)/shard_map/cond/branch_1_fun/ppermute | solution.py:41
  102.6 12.4 %collective-permute-start.12 = (bf16[16,64,128]{2,1,0:T(8,128)(2,1)S(1)}, bf16[16,64,128]{2,1,0:T(8,128)(2,1)S(1)}, u32[]{:S(2)}, u32[]{:S(2)}) collective-permute-start(bf16[16,64,128]{2,1,0:T(8,128)(2,1)S(1)} %get-tuple-element.60.refs_0_), channel_id=1, source_target_pairs={{0,32},{32,0},{64,96},{96,64},{128,160},{160,128},{192,224},{224,1... | collective-permute-start | bytes 786440 | tf_op jit(solution)/shard_map/cond/branch_1_fun/ppermute | solution.py:47
  109.8 5.3 %collective-permute-start.18 = (bf16[16,64,128]{2,1,0:T(8,128)(2,1)S(1)}, bf16[16,64,128]{2,1,0:T(8,128)(2,1)S(1)}, u32[]{:S(2)}, u32[]{:S(2)}) collective-permute-start(bf16[16,64,128]{2,1,0:T(8,128)(2,1)S(1)} %collective-permute-done.17.refs_6_), channel_id=1, source_target_pairs={{0,32},{32,0},{64,96},{96,64},{128,160},{160,128},{192,224},{224,1... | collective-permute-start | bytes 786440 | tf_op jit(solution)/shard_map/cond/branch_1_fun/ppermute | solution.py:47
  111.3 3.8 %collective-permute-start.16 = (bf16[16,64,128]{2,1,0:T(8,128)(2,1)S(1)}, bf16[16,64,128]{2,1,0:T(8,128)(2,1)S(1)}, u32[]{:S(2)}, u32[]{:S(2)}) collective-permute-start(bf16[16,64,128]{2,1,0:T(8,128)(2,1)S(1)} %collective-permute-done.15.refs_4_), channel_id=1, source_target_pairs={{0,32},{32,0},{64,96},{96,64},{128,160},{160,128},{192,224},{224,1... | collective-permute-start | bytes 786440 | tf_op jit(solution)/shard_map/cond/branch_1_fun/ppermute | solution.py:47
  (33 other events, 194.6 us)
